TPU v7x, 32 devices: a whole 2x2x4 slice. The times are simulated.
32 devices in a mesh: section: 4 (over y, x), rows: 8 (over z, core).
Axes of the slice: x: 2, y: 2, z: 4, core: 2. Of those that a mesh axis runs over, the one named last changes fastest.
Arguments:
- node_features: bfloat16 [4, 128, 512], P(None, 'rows'), may hold values from -6 to 6
- edge_features: bfloat16 [4, 1024, 512], P(None, 'rows'), may hold values from -6 to 6
- sender_owner: int32 [4, 8, 128, 1], P(None, 'rows'), may hold values from 0 to 7; in each aligned block of 128 rows (0 to 127, 128 to 255, ..., all dimensions but the last counted through in order) at most 32 rows name the same one
- sender_local: int32 [4, 8, 128], P(None, 'rows'), may hold values from 0 to 15
- receivers: int32 [4, 8, 128], P(None, 'rows'), may hold values from 0 to 15, never falling along the last dimension, each value on 1 to 16 neighbouring positions
- cotangent: bfloat16 [4, 128, 512], P(None, 'rows'), may hold values from -6 to 6
- edge_w_one: bfloat16 [2, 1536, 512], replicated, may hold values from -0.15625 to 0.15625
- edge_b_one: bfloat16 [2, 512], replicated, may hold values from -3 to 3
- edge_w_two: bfloat16 [2, 512, 512], replicated, may hold values from -0.25 to 0.25
- edge_b_two: bfloat16 [2, 512], replicated, may hold values from -3 to 3
- edge_gain: bfloat16 [2, 512], replicated, may hold values from 0.5 to 1.5
- edge_shift: bfloat16 [2, 512], replicated, may hold values from -3 to 3
- node_w_one: bfloat16 [2, 1024, 512], replicated, may hold values from -0.1875 to 0.1875
- node_b_one: bfloat16 [2, 512], replicated, may hold values from -3 to 3
- node_w_two: bfloat16 [2, 512, 512], replicated, may hold values from -0.25 to 0.25
- node_b_two: bfloat16 [2, 512], replicated, may hold values from -3 to 3
- node_gain: bfloat16 [2, 512], replicated, may hold values from 0.5 to 1.5
- node_shift: bfloat16 [2, 512], replicated, may hold values from -3 to 3
Outputs:
- final_nodes: bfloat16 [4, 128, 512], P('section', 'rows')
- grad_nodes: float32 [4, 128, 512], P('section', 'rows')
- grad_edges: float32 [4, 1024, 512], P('section', 'rows')
- grad_edge_w_one: float32 [2, 1536, 512], P(None, 'rows')
- grad_edge_b_one: float32 [2, 512], P(None, 'rows')
- grad_edge_w_two: float32 [2, 512, 512], P(None, 'rows')
- grad_edge_b_two: float32 [2, 512], P(None, 'rows')
- grad_edge_gain: float32 [2, 512], P(None, 'rows')
- grad_edge_shift: float32 [2, 512], P(None, 'rows')
- grad_node_w_one: float32 [2, 1024, 512], P(None, 'rows')
- grad_node_b_one: float32 [2, 512], P(None, 'rows')
- grad_node_w_two: float32 [2, 512, 512], P(None, 'rows')
- grad_node_b_two: float32 [2, 512], P(None, 'rows')
- grad_node_gain: float32 [2, 512], P(None, 'rows')
- grad_node_shift: float32 [2, 512], P(None, 'rows')
Inputs may be any that keep to these rules, and one draw needn't show every extreme that they name: `sender_owner`: within one micro-batch, the 128 edges of one node block name any one node block as owner at most 32 times; in every draw some block is named exactly 32 times. `receivers`: within one node block of one micro-batch the values never fall; every node has 1 to 16 incoming edges, and in each node block of each micro-batch some node has exactly 16.
All inputs are finite; a program needn't handle non-finite values.
Results may differ from a plain program's by a relative error of at most 0.015.
Values may be sent and summed in bfloat16 or wider, within the bound.
A program may use at most 128 MiB of HBM per device.

v0:
```python
import jax
import jax.numpy as jnp
from jax import lax
from jax.sharding import PartitionSpec as P

norm_epsilon = 1e-05


def as_sent(x):

    def short(part):
        return part.astype(jnp.bfloat16) if part.dtype == jnp.float32 else part

    return jax.tree.map(short, x)


def passed_along(value, axis, steps):
    count = lax.axis_size(axis)
    first, last = (max(0, -steps), min(count, count - steps))
    return lax.ppermute(value, axis, [(source, source + steps) for source in range(first, last)])


def silu_slope(hidden_pre):
    sigmoid_value = jax.nn.sigmoid(hidden_pre)
    return sigmoid_value * (1.0 + hidden_pre * (1.0 - sigmoid_value))


def mlp_forward(inputs, weights):
    w_one, b_one, w_two, b_two, weight_gain, weight_shift = weights
    hidden_pre = jnp.dot(inputs, w_one, preferred_element_type=jnp.float32) + b_one.astype(
        jnp.float32
    )
    hidden = jax.nn.silu(hidden_pre).astype(jnp.bfloat16)
    lifted = jnp.dot(hidden, w_two, preferred_element_type=jnp.float32) + b_two.astype(jnp.float32)
    center = lifted - jnp.mean(lifted, axis=-1, keepdims=True)
    norm_scale = lax.rsqrt(jnp.mean(center * center, axis=-1, keepdims=True) + norm_epsilon)
    normed = center * norm_scale
    branch = normed * weight_gain.astype(jnp.float32) + weight_shift.astype(jnp.float32)
    return (branch, (hidden_pre, hidden, normed, norm_scale))


def contract_rows(left, right):
    return lax.dot_general(
        left, right, (((0,), (0,)), ((), ())), preferred_element_type=jnp.float32
    )


def contract_cols(left, right):
    return lax.dot_general(
        left, right, (((1,), (1,)), ((), ())), preferred_element_type=jnp.float32
    )


def mlp_backward(inputs, weights, saved, grad_branch):
    w_one, b_one, w_two, b_two, weight_gain, weight_shift = weights
    hidden_pre, hidden, normed, norm_scale = saved
    grad_normed = grad_branch * weight_gain.astype(jnp.float32)
    grad_lifted = norm_scale * (
        grad_normed
        - jnp.mean(grad_normed, axis=-1, keepdims=True)
        - normed * jnp.mean(grad_normed * normed, axis=-1, keepdims=True)
    )
    grad_lifted = grad_lifted.astype(jnp.bfloat16)
    grad_hidden = contract_cols(grad_lifted, w_two)
    grad_pre = (grad_hidden * silu_slope(hidden_pre)).astype(jnp.bfloat16)
    grad_inputs = contract_cols(grad_pre, w_one)
    gradients = (
        contract_rows(inputs, grad_pre),
        jnp.sum(grad_pre.astype(jnp.float32), axis=0),
        contract_rows(hidden, grad_lifted),
        jnp.sum(grad_lifted.astype(jnp.float32), axis=0),
        jnp.sum(grad_branch * normed, axis=0),
        jnp.sum(grad_branch, axis=0),
    )
    return (grad_inputs, gradients)


def pick_slot(store, micro_slot):
    return lax.dynamic_index_in_dim(store, micro_slot, 0, keepdims=False)


def keep_slot(store, value, micro_slot, flag):
    current = pick_slot(store, micro_slot)
    return lax.dynamic_update_index_in_dim(store, jnp.where(flag, value, current), micro_slot, 0)


def body(
    node_features,
    edge_features,
    sender_owner,
    sender_local,
    receivers,
    cotangent,
    edge_w_one,
    edge_b_one,
    edge_w_two,
    edge_b_two,
    edge_gain,
    edge_shift,
    node_w_one,
    node_b_one,
    node_w_two,
    node_b_two,
    node_gain,
    node_shift,
):
    sections = lax.axis_size("section")
    shards = lax.axis_size("rows")
    section_index = lax.axis_index("section")
    micro_count, node_dev, width = node_features.shape
    edge_dev = edge_features.shape[1]
    layer_count = edge_w_one.shape[0]
    layer_index = section_index // 2
    last_section = section_index == sections - 1
    from_inputs = section_index == 0
    branch_kind = jnp.where(section_index % 2 == 0, 1, 2)
    edge_set = tuple(
        (
            lax.dynamic_index_in_dim(weight_array, layer_index, 0, keepdims=False)
            for weight_array in (
                edge_w_one,
                edge_b_one,
                edge_w_two,
                edge_b_two,
                edge_gain,
                edge_shift,
            )
        )
    )
    node_set = tuple(
        (
            lax.dynamic_index_in_dim(weight_array, layer_index, 0, keepdims=False)
            for weight_array in (
                node_w_one,
                node_b_one,
                node_w_two,
                node_b_two,
                node_gain,
                node_shift,
            )
        )
    )
    owner_block = sender_owner[:, 0, :, 0]
    local_row = sender_local[:, 0, :]
    receiver_rows = receivers[:, 0, :]
    node_iota = jnp.arange(node_dev, dtype=jnp.int32)
    capacity = 2 * edge_dev // shards
    marks = (owner_block[:, :, None] == jnp.arange(shards, dtype=jnp.int32)[None, None, :]).astype(
        jnp.int32
    )
    position = jnp.sum((jnp.cumsum(marks, axis=1) - 1) * marks, axis=2)
    flat_slot = owner_block * capacity + position

    def fill_row(table_row, slot_row, value_row):
        return table_row.at[slot_row].set(value_row)

    request_table = jax.vmap(fill_row)(
        jnp.zeros((micro_count, shards * capacity), jnp.int32), flat_slot, local_row
    )
    wanted = lax.all_to_all(
        request_table.reshape(micro_count, shards, capacity),
        "rows",
        split_axis=1,
        concat_axis=1,
        tiled=True,
    )
    wanted = wanted.reshape(micro_count, shards * capacity)

    def fetch_senders(node_rows, micro_slot):
        outgoing = jnp.take(node_rows, pick_slot(wanted, micro_slot), axis=0)
        incoming = lax.all_to_all(
            as_sent(outgoing.reshape(shards, capacity, width)),
            "rows",
            split_axis=0,
            concat_axis=0,
            tiled=True,
        )
        return jnp.take(
            incoming.reshape(shards * capacity, width), pick_slot(flat_slot, micro_slot), axis=0
        )

    def edge_inputs(node_rows, edge_rows, sent_rows, targets):
        return jnp.concatenate([edge_rows, sent_rows, jnp.take(node_rows, targets, axis=0)], axis=1)

    def node_inputs(node_rows, edge_rows, targets):
        onehot = (targets[None, :] == node_iota[:, None]).astype(jnp.bfloat16)
        gathered_sum = jnp.dot(onehot, edge_rows, preferred_element_type=jnp.float32).astype(
            jnp.bfloat16
        )
        return jnp.concatenate([node_rows, gathered_sum], axis=1)

    def spare_forward(node_rows, edge_rows, sent_rows, targets):
        return (jnp.zeros_like(node_rows), jnp.zeros_like(edge_rows))

    def edge_forward(node_rows, edge_rows, sent_rows, targets):
        branch, saved = mlp_forward(edge_inputs(node_rows, edge_rows, sent_rows, targets), edge_set)
        return (node_rows, (edge_rows.astype(jnp.float32) + branch).astype(jnp.bfloat16))

    def node_forward(node_rows, edge_rows, sent_rows, targets):
        branch, saved = mlp_forward(node_inputs(node_rows, edge_rows, targets), node_set)
        return ((node_rows.astype(jnp.float32) + branch).astype(jnp.bfloat16), edge_rows)

    def spare_backward(
        node_rows, edge_rows, sent_rows, targets, grad_node, grad_edge, edge_totals, node_totals
    ):
        zero_edges = jnp.zeros(edge_rows.shape, jnp.float32)
        return (
            jnp.zeros(node_rows.shape, jnp.float32),
            zero_edges,
            zero_edges,
            edge_totals,
            node_totals,
        )

    def edge_backward(
        node_rows, edge_rows, sent_rows, targets, grad_node, grad_edge, edge_totals, node_totals
    ):
        inputs = edge_inputs(node_rows, edge_rows, sent_rows, targets)
        branch, saved = mlp_forward(inputs, edge_set)
        grad_inputs, gradients = mlp_backward(inputs, edge_set, saved, grad_edge)
        receiver_part = jax.ops.segment_sum(
            grad_inputs[:, 2 * width :], targets, num_segments=node_dev, indices_are_sorted=True
        )
        edge_totals = tuple((total + term for total, term in zip(edge_totals, gradients)))
        return (
            grad_node + receiver_part,
            grad_edge + grad_inputs[:, :width],
            grad_inputs[:, width : 2 * width],
            edge_totals,
            node_totals,
        )

    def node_backward(
        node_rows, edge_rows, sent_rows, targets, grad_node, grad_edge, edge_totals, node_totals
    ):
        inputs = node_inputs(node_rows, edge_rows, targets)
        branch, saved = mlp_forward(inputs, node_set)
        grad_inputs, gradients = mlp_backward(inputs, node_set, saved, grad_node)
        node_totals = tuple((total + term for total, term in zip(node_totals, gradients)))
        return (
            grad_node + grad_inputs[:, :width],
            grad_edge + jnp.take(grad_inputs[:, width:], targets, axis=0),
            jnp.zeros(edge_rows.shape, jnp.float32),
            edge_totals,
            node_totals,
        )

    tick_count = micro_count + sections - 1
    stash_nodes = jnp.zeros_like(node_features)
    stash_edges = jnp.zeros_like(edge_features)
    finals = jnp.zeros(node_features.shape, jnp.float32)
    arrived_rows = jnp.zeros((node_dev + edge_dev, width), jnp.bfloat16)
    for moment in range(tick_count):
        micro_raw = moment - section_index
        active = (micro_raw >= 0) & (micro_raw < micro_count)
        micro_slot = jnp.clip(micro_raw, 0, micro_count - 1)
        node_rows = jnp.where(
            from_inputs, pick_slot(node_features, micro_slot), arrived_rows[:node_dev]
        )
        edge_rows = jnp.where(
            from_inputs, pick_slot(edge_features, micro_slot), arrived_rows[node_dev:]
        )
        stash_nodes = keep_slot(stash_nodes, node_rows, micro_slot, active)
        stash_edges = keep_slot(stash_edges, edge_rows, micro_slot, active)
        targets = pick_slot(receiver_rows, micro_slot)
        sent_rows = fetch_senders(node_rows, micro_slot)
        out_nodes, out_edges = lax.switch(
            jnp.where(active, branch_kind, 0),
            [spare_forward, edge_forward, node_forward],
            node_rows,
            edge_rows,
            sent_rows,
            targets,
        )
        finals = keep_slot(finals, out_nodes.astype(jnp.float32), micro_slot, active & last_section)
        arrived_rows = passed_along(
            as_sent(jnp.concatenate([out_nodes, out_edges], axis=0)), "section", 1
        )
    edge_totals = tuple((jnp.zeros(weight_array.shape, jnp.float32) for weight_array in edge_set))
    node_totals = tuple((jnp.zeros(weight_array.shape, jnp.float32) for weight_array in node_set))
    input_nodes = jnp.zeros(node_features.shape, jnp.float32)
    input_edges = jnp.zeros(edge_features.shape, jnp.float32)
    arrived_grads = jnp.zeros((node_dev + edge_dev, width), jnp.bfloat16)
    for moment in range(tick_count):
        micro_raw = moment - (sections - 1 - section_index)
        active = (micro_raw >= 0) & (micro_raw < micro_count)
        micro_slot = jnp.clip(micro_raw, 0, micro_count - 1)
        grad_node = jnp.where(
            last_section,
            pick_slot(cotangent, micro_slot).astype(jnp.float32),
            arrived_grads[:node_dev].astype(jnp.float32),
        )
        grad_edge = jnp.where(last_section, 0.0, arrived_grads[node_dev:].astype(jnp.float32))
        node_rows = pick_slot(stash_nodes, micro_slot)
        edge_rows = pick_slot(stash_edges, micro_slot)
        targets = pick_slot(receiver_rows, micro_slot)
        sent_rows = fetch_senders(node_rows, micro_slot)
        new_nodes, new_edges, grad_sent, edge_totals, node_totals = lax.switch(
            jnp.where(active, branch_kind, 0),
            [spare_backward, edge_backward, node_backward],
            node_rows,
            edge_rows,
            sent_rows,
            targets,
            grad_node,
            grad_edge,
            edge_totals,
            node_totals,
        )
        return_outgoing = (
            jnp.zeros((shards * capacity, width), jnp.float32)
            .at[pick_slot(flat_slot, micro_slot)]
            .set(grad_sent)
        )
        arrived = lax.all_to_all(
            return_outgoing.reshape(shards, capacity, width).astype(jnp.bfloat16),
            "rows",
            split_axis=0,
            concat_axis=0,
            tiled=True,
        ).astype(jnp.float32)
        new_nodes = new_nodes + jax.ops.segment_sum(
            arrived.reshape(shards * capacity, width),
            pick_slot(wanted, micro_slot),
            num_segments=node_dev,
        )
        input_nodes = keep_slot(input_nodes, new_nodes, micro_slot, active & from_inputs)
        input_edges = keep_slot(input_edges, new_edges, micro_slot, active & from_inputs)
        arrived_grads = passed_along(
            jnp.concatenate([new_nodes, new_edges], axis=0).astype(jnp.bfloat16), "section", -1
        )

    def by_layer(term):
        return jnp.stack(
            [jnp.where(layer_index == level, term, 0.0) for level in range(layer_count)]
        )

    placed = [by_layer(term) for term in edge_totals + node_totals]
    row_sums = (
        lax.psum_scatter(placed[0], "rows", scatter_dimension=1, tiled=True),
        lax.psum_scatter(placed[1], "rows", scatter_dimension=1, tiled=True),
        lax.psum_scatter(placed[2], "rows", scatter_dimension=1, tiled=True),
        lax.psum_scatter(placed[3], "rows", scatter_dimension=1, tiled=True),
        lax.psum_scatter(placed[4], "rows", scatter_dimension=1, tiled=True),
        lax.psum_scatter(placed[5], "rows", scatter_dimension=1, tiled=True),
        lax.psum_scatter(placed[6], "rows", scatter_dimension=1, tiled=True),
        lax.psum_scatter(placed[7], "rows", scatter_dimension=1, tiled=True),
        lax.psum_scatter(placed[8], "rows", scatter_dimension=1, tiled=True),
        lax.psum_scatter(placed[9], "rows", scatter_dimension=1, tiled=True),
        lax.psum_scatter(placed[10], "rows", scatter_dimension=1, tiled=True),
        lax.psum_scatter(placed[11], "rows", scatter_dimension=1, tiled=True),
    )
    summed = (
        lax.psum(row_sums[0].astype(jnp.bfloat16), "section").astype(jnp.float32),
        lax.psum(row_sums[1].astype(jnp.bfloat16), "section").astype(jnp.float32),
        lax.psum(row_sums[2].astype(jnp.bfloat16), "section").astype(jnp.float32),
        lax.psum(row_sums[3].astype(jnp.bfloat16), "section").astype(jnp.float32),
        lax.psum(row_sums[4].astype(jnp.bfloat16), "section").astype(jnp.float32),
        lax.psum(row_sums[5].astype(jnp.bfloat16), "section").astype(jnp.float32),
        lax.psum(row_sums[6].astype(jnp.bfloat16), "section").astype(jnp.float32),
        lax.psum(row_sums[7].astype(jnp.bfloat16), "section").astype(jnp.float32),
        lax.psum(row_sums[8].astype(jnp.bfloat16), "section").astype(jnp.float32),
        lax.psum(row_sums[9].astype(jnp.bfloat16), "section").astype(jnp.float32),
        lax.psum(row_sums[10].astype(jnp.bfloat16), "section").astype(jnp.float32),
        lax.psum(row_sums[11].astype(jnp.bfloat16), "section").astype(jnp.float32),
    )
    weight_outs = tuple(summed)
    final_share, node_share, edge_share = (
        lax.psum_scatter(
            finals.astype(jnp.bfloat16), "section", scatter_dimension=0, tiled=True
        ).astype(jnp.float32),
        lax.psum_scatter(
            input_nodes.astype(jnp.bfloat16), "section", scatter_dimension=0, tiled=True
        ).astype(jnp.float32),
        lax.psum_scatter(
            input_edges.astype(jnp.bfloat16), "section", scatter_dimension=0, tiled=True
        ).astype(jnp.float32),
    )
    return (
        final_share.astype(jnp.bfloat16),
        node_share,
        edge_share,
        weight_outs[0],
        weight_outs[1],
        weight_outs[2],
        weight_outs[3],
        weight_outs[4],
        weight_outs[5],
        weight_outs[6],
        weight_outs[7],
        weight_outs[8],
        weight_outs[9],
        weight_outs[10],
        weight_outs[11],
    )


def solution(mesh):
    in_specs = (
        P(None, "rows", None),
        P(None, "rows", None),
        P(None, "rows", None, None),
        P(None, "rows", None),
        P(None, "rows", None),
        P(None, "rows", None),
        P(),
        P(),
        P(),
        P(),
        P(),
        P(),
        P(),
        P(),
        P(),
        P(),
        P(),
        P(),
    )
    out_specs = (
        P("section", "rows", None),
        P("section", "rows", None),
        P("section", "rows", None),
        P(None, "rows", None),
        P(None, "rows"),
        P(None, "rows", None),
        P(None, "rows"),
        P(None, "rows"),
        P(None, "rows"),
        P(None, "rows", None),
        P(None, "rows"),
        P(None, "rows", None),
        P(None, "rows"),
        P(None, "rows"),
        P(None, "rows"),
    )
    return jax.shard_map(body, mesh=mesh, in_specs=in_specs, out_specs=out_specs, check_vma=False)
```

profile of v0, /device:TPU:0, one launch (start us, length us, event | category | flops | bytes accessed | tf_op | source)
XLA Modules:
  0.0 1226.6 jit_solution(4498903537484962682)
XLA Ops:
  11.7 42.5 %scatter_fusion = s32[4,256]{1,0:T(4,128)S(1)} fusion(s32[4,256]{1,0:T(4,128)S(1)} %broadcast_in_dim.397, s32[512]{0:T(512)S(1)} %fusion.385, s32[512]{0:T(512)} %bitcast.882), kind=kCustom, calls=%fused_computation.67 | custom fusion | bytes 10240 | tf_op jit(solution)/shard_map/vmap()/scatter | solution.py:155
  55.0 6.3 all-to-all-start
  82.2 5.1 all-to-all-start.1
  89.9 7.2 all-to-all-done.1
  98.1 5.8 conditional.14
  116.9 8.1 all-to-all-done.2
  126.0 5.1 conditional.15
  143.7 8.1 all-to-all-done.3
  152.8 5.1 conditional.16
  170.5 8.0 all-to-all-done.4
  179.6 5.1 conditional.17
  197.2 8.1 all-to-all-done.5
  207.0 9.4 collective-permute-start.4
  226.8 8.1 all-to-all-done.6
  236.6 9.3 collective-permute-start.5
  257.4 7.0 all-to-all-done.7
  266.0 19.8 %conditional.21 = (f32[16,512]{1,0:T(8,128)S(1)}, f32[128,512]{1,0:T(8,128)S(1)}, f32[128,512]{1,0:T(8,128)}, f32[1536,512]{1,0:T(8,128)}, f32[512]{0:T(512)}, /...) conditional(s32[]{:T(128)} %clamp.49, () %tuple.220, ...), branch_computations={%region_51.55_spmd, %region_52.65_spmd, %region_62.75_spmd} | conditional | flops 811010176 | bytes 32329112 | solution.py:298
  289.9 3.4 all-to-all-start.8
  296.7 6.3 all-to-all-done.8
  303.0 3.4 all-to-all-start.9
  311.0 5.1 all-to-all-done.9
  317.5 5.4 collective-permute-done.6
  329.2 4.8 all-to-all-start.10
  336.7 7.0 all-to-all-done.10
  353.0 3.9 all-to-all-done.11
  366.9 4.8 all-to-all-start.12
  375.1 6.3 all-to-all-done.12
  390.5 4.8 all-to-all-done.13
  396.8 39.3 %collective-permute-done.8 = bf16[144,512]{1,0:T(8,128)(2,1)} collective-permute-done((bf16[144,512]{1,0:T(8,128)(2,1)S(1)}, bf16[144,512]{1,0:T(8,128)(2,1)}, u32[]{:S(2)}, u32[]{:S(2)}) %collective-permute-start.8) | collective-permute-done | bytes 147488 | tf_op jit(solution)/shard_map/ppermute | solution.py:20
  437.8 23.3 %conditional.24 = (f32[16,512]{1,0:T(8,128)S(1)}, f32[128,512]{1,0:T(8,128)S(1)}, f32[128,512]{1,0:T(8,128)}, f32[1536,512]{1,0:T(8,128)}, f32[512]{0:T(512)}, /...) conditional(s32[]{:T(128)} %clamp.52, (f32[1536,512]{1,0:T(8,128)}, ...), branch_computations={%region_117.122_spmd, %region_118.132_spmd, %region_128.141_spmd} | conditional | flops 812060800 | bytes 33394048 | solution.py:298
  448.9 4.5 convolution_add_fusion.46
  465.2 5.0 all-to-all-start.14
  472.9 7.0 all-to-all-done.14
  489.6 4.1 all-to-all-done.15
  498.4 24.0 %conditional.25 = (f32[16,512]{1,0:T(8,128)S(1)}, f32[128,512]{1,0:T(8,128)}, f32[128,512]{1,0:T(8,128)}, f32[1536,512]{1,0:T(8,128)}, f32[512]{0:T(512)}, /*ind...) conditional(s32[]{:T(128)} %clamp.53, (f32[1536,512]{1,0:T(8,128)}, ...), branch_computations={%region_139.144_spmd, %region_140.154_spmd, %region_150.163_spmd} | conditional | flops 812060800 | bytes 32345416 | solution.py:298
  510.3 4.5 convolution_add_fusion.54
  526.4 4.8 all-to-all-start.16
  533.2 7.8 all-to-all-done.16
  550.0 4.2 all-to-all-done.17
  558.7 24.3 %conditional.26 = (f32[16,512]{1,0:T(8,128)S(1)}, f32[128,512]{1,0:T(8,128)}, f32[128,512]{1,0:T(8,128)}, f32[1536,512]{1,0:T(8,128)}, f32[512]{0:T(512)}, /*ind...) conditional(s32[]{:T(128)} %clamp.54, (f32[1536,512]{1,0:T(8,128)}, ...), branch_computations={%region_161.166_spmd, %region_162.176_spmd, %region_172.185_spmd} | conditional | flops 812060800 | bytes 32345416 | solution.py:298
  570.9 4.5 convolution_add_fusion.62
  587.2 4.8 all-to-all-start.18
  593.9 7.9 all-to-all-done.18
  601.8 3.4 all-to-all-start.19
  610.8 4.1 all-to-all-done.19
  619.4 19.9 %conditional.27 = (f32[16,512]{1,0:T(8,128)S(1)}, f32[128,512]{1,0:T(8,128)}, f32[128,512]{1,0:T(8,128)}, f32[1536,512]{1,0:T(8,128)}, f32[512]{0:T(512)}, /*ind...) conditional(s32[]{:T(128)} %clamp.55, (f32[1536,512]{1,0:T(8,128)}, ...), branch_computations={%region_183.188_spmd, %region_184.198_spmd, %region_194.207_spmd} | conditional | flops 811995264 | bytes 31690020 | solution.py:298
  627.2 4.3 convolution_add_fusion.70
  661.9 4.8 all-to-all-start.20
  686.4 29.9 %reduce-scatter.44.cloned.1.call-done = f32[2,64,512]{2,1,0:T(8,128)} async-done(((f32[2,512,512]{2,1,0:T(8,128)}), f32[2,64,512]{2,1,0:T(8,128)}) %reduce-scatter.44.cloned.1.call-update) | async-done | bytes 262160 | tf_op jit(solution)/shard_map/reduce_scatter | solution.py:348
  717.9 49.5 %reduce-scatter.42.cloned.1.call-done = f32[2,128,512]{2,1,0:T(8,128)} async-done(((f32[2,1024,512]{2,1,0:T(8,128)}), f32[2,128,512]{2,1,0:T(8,128)}) %reduce-scatter.42.cloned.1.call-update) | async-done | bytes 524304 | tf_op jit(solution)/shard_map/reduce_scatter | solution.py:346
  769.2 68.4 %reduce-scatter.38.cloned.1.call-done = f32[2,192,512]{2,1,0:T(8,128)} async-done(((f32[2,1536,512]{2,1,0:T(8,128)}), f32[2,192,512]{2,1,0:T(8,128)}) %reduce-scatter.38.cloned.1.call-update) | async-done | bytes 786448 | tf_op jit(solution)/shard_map/reduce_scatter | solution.py:340
  840.4 28.7 %reduce-scatter.46.cloned.1.call-done = f32[64,2]{1,0:T(8,128)} async-done(((f32[512,2]{1,0:T(8,128)}), f32[64,2]{1,0:T(8,128)}) %reduce-scatter.46.cloned.1.call-update) | async-done | bytes 528
  869.9 29.8 %reduce-scatter.48.cloned.1.call-done = f32[64,2]{1,0:T(8,128)} async-done(((f32[512,2]{1,0:T(8,128)}), f32[64,2]{1,0:T(8,128)}) %reduce-scatter.48.cloned.1.call-update) | async-done | bytes 528
  900.6 29.9 %reduce-scatter.50.cloned.1.call-done = f32[64,2]{1,0:T(8,128)} async-done(((f32[512,2]{1,0:T(8,128)}), f32[64,2]{1,0:T(8,128)}) %reduce-scatter.50.cloned.1.call-update) | async-done | bytes 528
  931.3 30.0 %reduce-scatter.52.cloned.1.call-done = f32[64,2]{1,0:T(8,128)} async-done(((f32[512,2]{1,0:T(8,128)}), f32[64,2]{1,0:T(8,128)}) %reduce-scatter.52.cloned.1.call-update) | async-done | bytes 528
  962.1 29.9 %reduce-scatter.54.cloned.1.call-done = f32[64,2]{1,0:T(8,128)} async-done(((f32[512,2]{1,0:T(8,128)}), f32[64,2]{1,0:T(8,128)}) %reduce-scatter.54.cloned.1.call-update) | async-done | bytes 528
  992.8 29.8 %reduce-scatter.56.cloned.1.call-done = f32[64,2]{1,0:T(8,128)} async-done(((f32[512,2]{1,0:T(8,128)}), f32[64,2]{1,0:T(8,128)}) %reduce-scatter.56.cloned.1.call-update) | async-done | bytes 528
  1023.5 29.9 %reduce-scatter.58.cloned.1.call-done = f32[64,2]{1,0:T(8,128)} async-done(((f32[512,2]{1,0:T(8,128)}), f32[64,2]{1,0:T(8,128)}) %reduce-scatter.58.cloned.1.call-update) | async-done | bytes 528
  1054.2 29.8 %reduce-scatter.60.cloned.1.call-done = f32[64,2]{1,0:T(8,128)} async-done(((f32[512,2]{1,0:T(8,128)}), f32[64,2]{1,0:T(8,128)}) %reduce-scatter.60.cloned.1.call-update) | async-done | bytes 528
  1084.8 9.8 all-reduce.3
  1099.1 9.4 reduce-scatter.64.cloned.1.call-done
  1109.8 27.0 %reduce-scatter.66.cloned.1.call-done = bf16[1,128,512]{2,1,0:T(8,128)(2,1)} async-done(((bf16[4,128,512]{2,1,0:T(8,128)(2,1)}), bf16[1,128,512]{2,1,0:T(8,128)(2,1)}) %reduce-scatter.66.cloned.1.call-update) | async-done | bytes 131088
  1138.5 54.1 %all-reduce.7.cloned.1.call-done = (bf16[2,192,512]{2,1,0:T(8,128)(2,1)}, bf16[2,64,512]{2,1,0:T(8,128)(2,1)}, bf16[2,128,512]{2,1,0:T(8,128)(2,1)}, bf16[2,64,512]{2,1,0:T(8,128)(2,1)}) async-done(((bf16[2,192,512]{2,1,0:T(8,128)(2,1)}, bf16[2,64,512]{2,1,0:T(8,128)(2,1)}, bf16[2,128,512]{2,1,0:T(8,128)(2,1)}, bf16[2,64,512]{2,1,0:T(8,128)(2,1)}), (bf16[2,192,512]{2,1,0:T(8,128)(2,1)}, ...) | async-done | bytes 917520 | tf_op jit(solution)/shard_map/psum | solution.py:354
  1198.7 20.9 %reduce-scatter.62.cloned.1.call-done = bf16[1,16,512]{2,1,0:T(8,128)(2,1)} async-done(((bf16[4,16,512]{2,1,0:T(8,128)(2,1)}), bf16[1,16,512]{2,1,0:T(8,128)(2,1)}) %reduce-scatter.62.cloned.1.call-update) | async-done | bytes 16400
  (882 shorter events, 397.6 us)
Async XLA Ops:
  55.0 20.8 %all-to-all-start = ((s32[8,1,128]{2,1,0:T(1,128)}), s32[8,1,128]{2,1,0:T(1,128)S(1)}, u32[]{:S(2)}, u32[]{:S(2)}) async-start(s32[8,1,128]{2,1,0:T(1,128)} %reshape.1856), calls=%async_computation | async-start | bytes 8192 | tf_op jit(solution)/shard_map/all_to_all | solution.py:160
  73.9 287.0 %copy-start.89 = (bf16[512]{0:T(512)(128)(2,1)}, bf16[512]{0:T(512)(128)(2,1)S(1)}, u32[]{:S(2)}) copy-start(bf16[512]{0:T(512)(128)(2,1)S(1)} %get-tuple-element.2357) | copy-start | bytes 3076
  74.0 287.0 %copy-start.91 = (bf16[512]{0:T(512)(128)(2,1)}, bf16[512]{0:T(512)(128)(2,1)S(1)}, u32[]{:S(2)}) copy-start(bf16[512]{0:T(512)(128)(2,1)S(1)} %get-tuple-element.2358) | copy-start | bytes 3076
  74.6 286.4 %copy-start.94 = (bf16[512]{0:T(512)(128)(2,1)}, bf16[512]{0:T(512)(128)(2,1)S(1)}, u32[]{:S(2)}) copy-start(bf16[512]{0:T(512)(128)(2,1)S(1)} %get-tuple-element.2359) | copy-start | bytes 3076
  75.2 285.8 %copy-start.97 = (bf16[512]{0:T(512)(128)(2,1)}, bf16[512]{0:T(512)(128)(2,1)S(1)}, u32[]{:S(2)}) copy-start(bf16[512]{0:T(512)(128)(2,1)S(1)} %get-tuple-element.2353) | copy-start | bytes 3076
  75.2 285.8 %copy-start.99 = (bf16[512]{0:T(512)(128)(2,1)}, bf16[512]{0:T(512)(128)(2,1)S(1)}, u32[]{:S(2)}) copy-start(bf16[512]{0:T(512)(128)(2,1)S(1)} %get-tuple-element.2354) | copy-start | bytes 3076
  75.8 285.2 %copy-start.102 = (bf16[512]{0:T(512)(128)(2,1)}, bf16[512]{0:T(512)(128)(2,1)S(1)}, u32[]{:S(2)}) copy-start(bf16[512]{0:T(512)(128)(2,1)S(1)} %get-tuple-element.2355) | copy-start | bytes 3076
  82.2 14.8 %all-to-all-start.1 = ((bf16[8,32,512]{2,1,0:T(8,128)(2,1)}), bf16[8,32,512]{2,1,0:T(8,128)(2,1)S(1)}, u32[]{:S(2)}, u32[]{:S(2)}) async-start(bf16[8,32,512]{2,1,0:T(8,128)(2,1)} %bitcast.805), calls=%async_computation.1 | async-start | bytes 524288 | tf_op jit(solution)/shard_map/all_to_all | solution.py:171
  98.1 263.0 %copy-start.120 = (s32[128]{0:T(128)}, s32[128]{0:T(128)S(1)}, u32[]{:S(2)}) copy-start(s32[128]{0:T(128)S(1)} %lt.493) | copy-start | bytes 1540
  104.9 4.3 collective-permute-start
  111.9 13.1 %all-to-all-start.2 = ((bf16[8,32,512]{2,1,0:T(8,128)(2,1)}), bf16[8,32,512]{2,1,0:T(8,128)(2,1)S(1)}, u32[]{:S(2)}, u32[]{:S(2)}) async-start(bf16[8,32,512]{2,1,0:T(8,128)(2,1)} %bitcast.24), calls=%async_computation.2 | async-start | bytes 524288 | tf_op jit(solution)/shard_map/all_to_all | solution.py:171
  131.8 4.3 collective-permute-start.1
  138.7 13.1 %all-to-all-start.3 = ((bf16[8,32,512]{2,1,0:T(8,128)(2,1)}), bf16[8,32,512]{2,1,0:T(8,128)(2,1)S(1)}, u32[]{:S(2)}, u32[]{:S(2)}) async-start(bf16[8,32,512]{2,1,0:T(8,128)(2,1)} %bitcast.33), calls=%async_computation.3 | async-start | bytes 524288 | tf_op jit(solution)/shard_map/all_to_all | solution.py:171
  158.5 4.3 collective-permute-start.2
  165.5 13.1 %all-to-all-start.4 = ((bf16[8,32,512]{2,1,0:T(8,128)(2,1)}), bf16[8,32,512]{2,1,0:T(8,128)(2,1)S(1)}, u32[]{:S(2)}, u32[]{:S(2)}) async-start(bf16[8,32,512]{2,1,0:T(8,128)(2,1)} %bitcast.42), calls=%async_computation.4 | async-start | bytes 524288 | tf_op jit(solution)/shard_map/all_to_all | solution.py:171
  185.3 4.3 collective-permute-start.3
  192.3 13.1 %all-to-all-start.5 = ((bf16[8,32,512]{2,1,0:T(8,128)(2,1)}), bf16[8,32,512]{2,1,0:T(8,128)(2,1)S(1)}, u32[]{:S(2)}, u32[]{:S(2)}) async-start(bf16[8,32,512]{2,1,0:T(8,128)(2,1)} %bitcast.51), calls=%async_computation.5 | async-start | bytes 524288 | tf_op jit(solution)/shard_map/all_to_all | solution.py:171
  207.0 12.1 collective-permute-start.4
  221.8 13.1 %all-to-all-start.6 = ((bf16[8,32,512]{2,1,0:T(8,128)(2,1)}), bf16[8,32,512]{2,1,0:T(8,128)(2,1)S(1)}, u32[]{:S(2)}, u32[]{:S(2)}) async-start(bf16[8,32,512]{2,1,0:T(8,128)(2,1)} %bitcast.60), calls=%async_computation.6 | async-start | bytes 524288 | tf_op jit(solution)/shard_map/all_to_all | solution.py:171
  236.6 12.1 collective-permute-start.5
  251.3 13.1 %all-to-all-start.7 = ((bf16[8,32,512]{2,1,0:T(8,128)(2,1)}), bf16[8,32,512]{2,1,0:T(8,128)(2,1)S(1)}, u32[]{:S(2)}, u32[]{:S(2)}) async-start(bf16[8,32,512]{2,1,0:T(8,128)(2,1)} %bitcast.97), calls=%async_computation.7 | async-start | bytes 524288 | tf_op jit(solution)/shard_map/all_to_all | solution.py:171
  289.9 13.1 %all-to-all-start.8 = ((bf16[8,32,512]{2,1,0:T(8,128)(2,1)}), bf16[8,32,512]{2,1,0:T(8,128)(2,1)S(1)}, u32[]{:S(2)}, u32[]{:S(2)}) async-start(bf16[8,32,512]{2,1,0:T(8,128)(2,1)} %bitcast.102), calls=%async_computation.8 | async-start | bytes 524288 | tf_op jit(solution)/shard_map/all_to_all | solution.py:315
  303.0 13.1 %all-to-all-start.9 = ((bf16[8,32,512]{2,1,0:T(8,128)(2,1)}), bf16[8,32,512]{2,1,0:T(8,128)(2,1)S(1)}, u32[]{:S(2)}, u32[]{:S(2)}) async-start(bf16[8,32,512]{2,1,0:T(8,128)(2,1)} %bitcast.110), calls=%async_computation.9 | async-start | bytes 524288 | tf_op jit(solution)/shard_map/all_to_all | solution.py:171
  309.6 13.3 %collective-permute-start.6 = (bf16[144,512]{1,0:T(8,128)(2,1)S(1)}, bf16[144,512]{1,0:T(8,128)(2,1)S(1)}, u32[]{:S(2)}, u32[]{:S(2)}) collective-permute-start(bf16[144,512]{1,0:T(8,128)(2,1)S(1)} %pad_maximum_fusion.52), channel_id=1, source_target_pairs={{8,0},{16,8},{24,16},{9,1},{17,9},{25,17},{10,2},{18,10},{26,18},{... | collective-permute-start | bytes 442376 | tf_op jit(solution)/shard_map/ppermute | solution.py:20
  329.2 14.6 %all-to-all-start.10 = ((bf16[8,32,512]{2,1,0:T(8,128)(2,1)}), bf16[8,32,512]{2,1,0:T(8,128)(2,1)S(1)}, u32[]{:S(2)}, u32[]{:S(2)}) async-start(bf16[8,32,512]{2,1,0:T(8,128)(2,1)} %bitcast.115), calls=%async_computation.10 | async-start | bytes 524288 | tf_op jit(solution)/shard_map/all_to_all | solution.py:315
  343.8 13.1 %all-to-all-start.11 = ((bf16[8,32,512]{2,1,0:T(8,128)(2,1)}), bf16[8,32,512]{2,1,0:T(8,128)(2,1)S(1)}, u32[]{:S(2)}, u32[]{:S(2)}) async-start(bf16[8,32,512]{2,1,0:T(8,128)(2,1)} %bitcast.124), calls=%async_computation.11 | async-start | bytes 524288 | tf_op jit(solution)/shard_map/all_to_all | solution.py:171
  350.5 9.7 collective-permute-start.7
  366.9 14.6 %all-to-all-start.12 = ((bf16[8,32,512]{2,1,0:T(8,128)(2,1)}), bf16[8,32,512]{2,1,0:T(8,128)(2,1)S(1)}, u32[]{:S(2)}, u32[]{:S(2)}) async-start(bf16[8,32,512]{2,1,0:T(8,128)(2,1)} %bitcast.129), calls=%async_computation.12 | async-start | bytes 524288 | tf_op jit(solution)/shard_map/all_to_all | solution.py:315
  382.2 13.1 %all-to-all-start.13 = ((bf16[8,32,512]{2,1,0:T(8,128)(2,1)}), bf16[8,32,512]{2,1,0:T(8,128)(2,1)S(1)}, u32[]{:S(2)}, u32[]{:S(2)}) async-start(bf16[8,32,512]{2,1,0:T(8,128)(2,1)} %bitcast.803), calls=%async_computation.13 | async-start | bytes 524288 | tf_op jit(solution)/shard_map/all_to_all | solution.py:171
  389.1 46.9 %collective-permute-start.8 = (bf16[144,512]{1,0:T(8,128)(2,1)S(1)}, bf16[144,512]{1,0:T(8,128)(2,1)}, u32[]{:S(2)}, u32[]{:S(2)}) collective-permute-start(bf16[144,512]{1,0:T(8,128)(2,1)S(1)} %pad_maximum_fusion.54), channel_id=1, source_target_pairs={{8,0},{16,8},{24,16},{9,1},{17,9},{25,17},{10,2},{18,10},{26,18},{... | collective-permute-start | bytes 442376 | tf_op jit(solution)/shard_map/ppermute | solution.py:20
  465.2 14.7 %all-to-all-start.14 = ((bf16[8,32,512]{2,1,0:T(8,128)(2,1)}), bf16[8,32,512]{2,1,0:T(8,128)(2,1)S(1)}, u32[]{:S(2)}, u32[]{:S(2)}) async-start(bf16[8,32,512]{2,1,0:T(8,128)(2,1)} %bitcast.143), calls=%async_computation.14 | async-start | bytes 524288 | tf_op jit(solution)/shard_map/all_to_all | solution.py:315
  480.6 13.1 %all-to-all-start.15 = ((bf16[8,32,512]{2,1,0:T(8,128)(2,1)}), bf16[8,32,512]{2,1,0:T(8,128)(2,1)S(1)}, u32[]{:S(2)}, u32[]{:S(2)}) async-start(bf16[8,32,512]{2,1,0:T(8,128)(2,1)} %bitcast.802), calls=%async_computation.15 | async-start | bytes 524288 | tf_op jit(solution)/shard_map/all_to_all | solution.py:171
  488.3 8.4 collective-permute-start.9
  526.4 14.7 %all-to-all-start.16 = ((bf16[8,32,512]{2,1,0:T(8,128)(2,1)}), bf16[8,32,512]{2,1,0:T(8,128)(2,1)}, u32[]{:S(2)}, u32[]{:S(2)}) async-start(bf16[8,32,512]{2,1,0:T(8,128)(2,1)} %bitcast.157), calls=%async_computation.16 | async-start | bytes 524288 | tf_op jit(solution)/shard_map/all_to_all | solution.py:315
  541.1 13.1 %all-to-all-start.17 = ((bf16[8,32,512]{2,1,0:T(8,128)(2,1)}), bf16[8,32,512]{2,1,0:T(8,128)(2,1)S(1)}, u32[]{:S(2)}, u32[]{:S(2)}) async-start(bf16[8,32,512]{2,1,0:T(8,128)(2,1)} %bitcast.804), calls=%async_computation.17 | async-start | bytes 524288 | tf_op jit(solution)/shard_map/all_to_all | solution.py:171
  548.7 8.4 collective-permute-start.10
  587.2 14.6 %all-to-all-start.18 = ((bf16[8,32,512]{2,1,0:T(8,128)(2,1)}), bf16[8,32,512]{2,1,0:T(8,128)(2,1)}, u32[]{:S(2)}, u32[]{:S(2)}) async-start(bf16[8,32,512]{2,1,0:T(8,128)(2,1)} %bitcast.171), calls=%async_computation.18 | async-start | bytes 524288 | tf_op jit(solution)/shard_map/all_to_all | solution.py:315
  601.8 13.1 %all-to-all-start.19 = ((bf16[8,32,512]{2,1,0:T(8,128)(2,1)}), bf16[8,32,512]{2,1,0:T(8,128)(2,1)S(1)}, u32[]{:S(2)}, u32[]{:S(2)}) async-start(bf16[8,32,512]{2,1,0:T(8,128)(2,1)} %bitcast.801), calls=%async_computation.19 | async-start | bytes 524288 | tf_op jit(solution)/shard_map/all_to_all | solution.py:171
  605.2 79.6 %reduce-scatter.40.cloned.1.call-start = ((), (), s32[]{:S(2)}) async-start(), calls=%async_computation.37 | async-start | bytes 2359296 | tf_op jit(solution)/shard_map/reduce_scatter | solution.py:342
  609.4 8.3 collective-permute-start.11
  642.3 74.0 %reduce-scatter.44.cloned.1.call-start = ((), (), s32[]{:S(2)}) async-start(), calls=%async_computation.39 | async-start | bytes 2359296 | tf_op jit(solution)/shard_map/reduce_scatter | solution.py:348
  645.3 122.1 %reduce-scatter.42.cloned.1.call-start = ((), (), s32[]{:S(2)}) async-start(), calls=%async_computation.38 | async-start | bytes 4718592 | tf_op jit(solution)/shard_map/reduce_scatter | solution.py:346
  650.1 187.5 %reduce-scatter.38.cloned.1.call-start = ((), (), s32[]{:S(2)}) async-start(), calls=%async_computation.36 | async-start | bytes 7077888 | tf_op jit(solution)/shard_map/reduce_scatter | solution.py:340
  661.9 17.9 %all-to-all-start.20 = ((bf16[8,32,512]{2,1,0:T(8,128)(2,1)}), bf16[8,32,512]{2,1,0:T(8,128)(2,1)S(1)}, u32[]{:S(2)}, u32[]{:S(2)}) async-start(bf16[8,32,512]{2,1,0:T(8,128)(2,1)} %bitcast.185), calls=%async_computation.20 | async-start | bytes 524288 | tf_op jit(solution)/shard_map/all_to_all | solution.py:315
  666.8 202.3 %reduce-scatter.46.cloned.1.call-start = ((), (), s32[]{:S(2)}) async-start(), calls=%async_computation.40 | async-start | bytes 294912
  672.4 227.4 %reduce-scatter.48.cloned.1.call-start = ((), (), s32[]{:S(2)}) async-start(), calls=%async_computation.41 | async-start | bytes 294912
  673.3 257.1 %reduce-scatter.50.cloned.1.call-start = ((), (), s32[]{:S(2)}) async-start(), calls=%async_computation.42 | async-start | bytes 294912
  674.3 287.0 %reduce-scatter.52.cloned.1.call-start = ((), (), s32[]{:S(2)}) async-start(), calls=%async_computation.43 | async-start | bytes 294912
  675.3 316.7 %reduce-scatter.54.cloned.1.call-start = ((), (), s32[]{:S(2)}) async-start(), calls=%async_computation.44 | async-start | bytes 294912
  676.2 346.4 %reduce-scatter.56.cloned.1.call-start = ((), (), s32[]{:S(2)}) async-start(), calls=%async_computation.45 | async-start | bytes 294912
  677.2 376.2 %reduce-scatter.58.cloned.1.call-start = ((), (), s32[]{:S(2)}) async-start(), calls=%async_computation.46 | async-start | bytes 294912
  678.1 405.9 %reduce-scatter.60.cloned.1.call-start = ((), (), s32[]{:S(2)}) async-start(), calls=%async_computation.47 | async-start | bytes 294912
  679.8 428.7 %reduce-scatter.64.cloned.1.call-start = ((), (), s32[]{:S(2)}) async-start(), calls=%async_computation.49 | async-start | bytes 81920
  682.7 454.1 %reduce-scatter.66.cloned.1.call-start = ((), (), s32[]{:S(2)}) async-start(), calls=%async_computation.50 | async-start | bytes 655360
  683.8 155.8 %copy-start.131 = (bf16[16,512]{1,0:T(8,128)(2,1)S(1)}, bf16[16,512]{1,0:T(8,128)(2,1)}, u32[]{:S(2)}) copy-start(bf16[16,512]{1,0:T(8,128)(2,1)} %copy-done.130) | copy-start | bytes 49156
  683.8 155.8 %copy-start.133 = (bf16[16,512]{1,0:T(8,128)(2,1)S(1)}, bf16[16,512]{1,0:T(8,128)(2,1)}, u32[]{:S(2)}) copy-start(bf16[16,512]{1,0:T(8,128)(2,1)} %copy-done.132) | copy-start | bytes 49156
  684.6 155.1 %copy-start.135 = (bf16[16,512]{1,0:T(8,128)(2,1)S(1)}, bf16[16,512]{1,0:T(8,128)(2,1)}, u32[]{:S(2)}) copy-start(bf16[16,512]{1,0:T(8,128)(2,1)} %copy-done.134) | copy-start | bytes 49156
  684.6 155.1 %copy-start.137 = (bf16[16,512]{1,0:T(8,128)(2,1)S(1)}, bf16[16,512]{1,0:T(8,128)(2,1)}, u32[]{:S(2)}) copy-start(bf16[16,512]{1,0:T(8,128)(2,1)} %copy-done.136) | copy-start | bytes 49156
  684.6 155.1 %copy-start.72 = (bf16[16,512]{1,0:T(8,128)(2,1)S(1)}, bf16[16,512]{1,0:T(8,128)(2,1)}, u32[]{:S(2)}) copy-start(bf16[16,512]{1,0:T(8,128)(2,1)} %get-tuple-element.2088) | copy-start | bytes 49156
  684.6 155.1 %copy-start.119 = (bf16[128,512]{1,0:T(8,128)(2,1)S(1)}, bf16[128,512]{1,0:T(8,128)(2,1)}, u32[]{:S(2)}) copy-start(bf16[128,512]{1,0:T(8,128)(2,1)} %get-tuple-element.2076) | copy-start | bytes 393220
  684.6 155.1 %copy-start.127 = (bf16[512]{0:T(512)(128)(2,1)S(1)}, bf16[512]{0:T(512)(128)(2,1)}, u32[]{:S(2)}) copy-start(bf16[512]{0:T(512)(128)(2,1)} %get-tuple-element.2360) | copy-start | bytes 3076
  684.6 507.9 %all-reduce.7.cloned.1.call-start = ((), (), s32[]{:S(2)}) async-start(), calls=%async_computation.51 | async-start | bytes 1835008 | tf_op jit(solution)/shard_map/psum | solution.py:354
  839.5 380.1 %reduce-scatter.62.cloned.1.call-start = ((), (), s32[]{:S(2)}) async-start(), calls=%async_computation.48 | async-start | bytes 81920
  839.8 379.8 %copy-start.1 = (bf16[2,1536,512]{2,1,0:T(8,128)(2,1)S(1)}, bf16[2,1536,512]{2,1,0:T(8,128)(2,1)}, u32[]{:S(2)}) copy-start(bf16[2,1536,512]{2,1,0:T(8,128)(2,1)} %param.74) | copy-start | bytes 9437188
  (146 other events, 1849.8 us)
Sparse Core Ops, SparseCore 0:
  642.4 37.4 reduce-scatter.39
  682.2 34.1 reduce-scatter.43
  718.6 48.7 reduce-scatter.41
  769.6 67.9 reduce-scatter.37
  840.2 28.8 reduce-scatter.45
  871.3 28.4 reduce-scatter.47
  902.0 28.4 reduce-scatter.49
  932.8 28.4 reduce-scatter.51
  963.5 28.4 reduce-scatter.53
  994.2 28.3 reduce-scatter.55
  1024.9 28.4 reduce-scatter.57
  1055.6 28.3 reduce-scatter.59
  1086.7 21.7 reduce-scatter.63
  1112.0 24.8 reduce-scatter.65
  1141.2 51.2 all-reduce.6
  1195.9 23.6 reduce-scatter.61
where the time goes:
time: 1240 us; the launch traced here: 1230 us
  waiting for transfers between devices  689 us (56%)
  other arithmetic  180 us (15%)
  local copies, waits for them, and re-layouts  149 us (12%)
  starting transfers between devices  117 us (9%)
  matrix products  52.8 us (4%)
  between operations  17.2 us (1%)
    unnamed x27, waiting for transfers between devices  295 us
    all_to_all x13, waiting for transfers between devices, fetch_senders(): lax.all_to_all(as_sent(outgoing.reshape(shards, capacity, width)), 'rows'...  80.7 us
    ppermute x12, waiting for transfers between devices, passed_along(): lax.ppermute(value, axis, [(source, source + steps) for source in range(f...  68.5 us
    reduce_scatter x1, waiting for transfers between devices, body(): lax.psum_scatter(placed[0], 'rows', scatter_dimension=1, tiled=True)  68.4 us
    psum x1, waiting for transfers between devices, body(): lax.psum(row_sums[0].astype(jnp.bfloat16), 'section').astype(jnp.float32)  54.1 us
    reduce_scatter x1, waiting for transfers between devices, body(): lax.psum_scatter(placed[6], 'rows', scatter_dimension=1, tiled=True)  49.5 us
    all_to_all x13, starting transfers between devices, fetch_senders(): lax.all_to_all(as_sent(outgoing.reshape(shards, capacity, width)), 'rows'...  46 us
    scatter x1, local copies, waits for them, and re-layouts, fill_row(): return table_row.at[slot_row].set(value_row)  42.5 us
  transfers between devices with their start and end apart: 49, of which 46 were waited for; matrix products, arithmetic and copies ran while one was open for 11% of the time, Pallas kernels for 0%

commit v1 on v0

v1 whole, which is shorter than its diff:
```python
import jax
import jax.numpy as jnp
from jax import lax
from jax.sharding import PartitionSpec as P

norm_epsilon = 1e-05
f32 = jnp.float32
bf16 = jnp.bfloat16


def dot(left, right):
    return jnp.dot(left, right, preferred_element_type=f32)


def contract_rows(left, right):
    return lax.dot_general(left, right, (((0,), (0,)), ((), ())), preferred_element_type=f32)


def contract_cols(left, right):
    return lax.dot_general(left, right, (((1,), (1,)), ((), ())), preferred_element_type=f32)


def mlp_forward(hidden_pre, weights):
    b_one, w_two, b_two, gain, shift = weights
    hidden_pre = hidden_pre + b_one.astype(f32)
    hidden = jax.nn.silu(hidden_pre).astype(bf16)
    lifted = dot(hidden, w_two) + b_two.astype(f32)
    center = lifted - jnp.mean(lifted, axis=-1, keepdims=True)
    norm_scale = lax.rsqrt(jnp.mean(center * center, axis=-1, keepdims=True) + norm_epsilon)
    normed = center * norm_scale
    branch = normed * gain.astype(f32) + shift.astype(f32)
    return branch, (hidden_pre, hidden, normed, norm_scale)


def mlp_backward(weights, saved, grad_branch):
    b_one, w_two, b_two, gain, shift = weights
    hidden_pre, hidden, normed, norm_scale = saved
    grad_normed = grad_branch * gain.astype(f32)
    grad_lifted = norm_scale * (
        grad_normed
        - jnp.mean(grad_normed, axis=-1, keepdims=True)
        - normed * jnp.mean(grad_normed * normed, axis=-1, keepdims=True)
    )
    grad_lifted = grad_lifted.astype(bf16)
    grad_hidden = contract_cols(grad_lifted, w_two)
    sigma = jax.nn.sigmoid(hidden_pre)
    grad_pre = (grad_hidden * (sigma * (1.0 + hidden_pre * (1.0 - sigma)))).astype(bf16)
    terms = (
        jnp.sum(grad_pre.astype(f32), axis=0),
        contract_rows(hidden, grad_lifted),
        jnp.sum(grad_lifted.astype(f32), axis=0),
        jnp.sum(grad_branch * normed, axis=0),
        jnp.sum(grad_branch, axis=0),
    )
    return grad_pre, terms


def body(node_features, edge_features, sender_owner, sender_local, receivers, cotangent, *weights):
    micro = lax.axis_index("section")
    micro_count, node_dev, width = node_features.shape
    shards = lax.axis_size("rows")
    edge_weights, node_weights = weights[:6], weights[6:]
    layers = edge_weights[0].shape[0]

    def pick(array):
        return lax.dynamic_index_in_dim(array, micro, 0, keepdims=False)

    node = pick(node_features)
    edge = pick(edge_features)
    senders = pick(sender_owner)[0, :, 0] * node_dev + pick(sender_local)[0]
    targets = pick(receivers)[0]
    onehot_sender = (
        senders[:, None] == jnp.arange(shards * node_dev, dtype=jnp.int32)[None, :]
    ).astype(bf16)
    onehot_target = (targets[:, None] == jnp.arange(node_dev, dtype=jnp.int32)[None, :]).astype(
        bf16
    )

    stash = []
    for layer in range(layers):
        w_one, *edge_rest = (w[layer] for w in edge_weights)
        all_nodes = lax.all_gather(node, "rows", axis=0, tiled=True)
        sent = dot(onehot_sender, all_nodes).astype(bf16)
        received = dot(onehot_target, node).astype(bf16)
        pre = dot(jnp.concatenate([edge, sent, received], axis=1), w_one)
        branch, edge_saved = mlp_forward(pre, edge_rest)
        edge_in = edge
        edge = (edge.astype(f32) + branch).astype(bf16)
        v_one, *node_rest = (w[layer] for w in node_weights)
        gathered = contract_rows(onehot_target, edge).astype(bf16)
        node_in = node
        branch, node_saved = mlp_forward(
            dot(jnp.concatenate([node, gathered], axis=1), v_one), node_rest
        )
        node = (node.astype(f32) + branch).astype(bf16)
        stash.append((node_in, edge_in, gathered, edge_saved, node_saved))

    final = node
    grad_node = pick(cotangent).astype(f32)
    grad_edge = jnp.zeros(edge.shape, f32)
    edge_terms, node_terms = [], []
    for layer in reversed(range(layers)):
        node_in, edge_in, gathered, edge_saved, node_saved = stash[layer]
        w_one, *edge_rest = (w[layer] for w in edge_weights)
        v_one, *node_rest = (w[layer] for w in node_weights)
        grad_pre, terms = mlp_backward(node_rest, node_saved, grad_node)
        v_grad = contract_rows(jnp.concatenate([node_in, gathered], axis=1), grad_pre)
        node_terms.insert(0, (v_grad,) + terms)
        grad_x = contract_cols(grad_pre, v_one)
        grad_node = (grad_node + grad_x[:, :width]).astype(bf16).astype(f32)
        grad_aggregate = grad_x[:, width:].astype(bf16)
        grad_edge = (grad_edge + dot(onehot_target, grad_aggregate)).astype(bf16).astype(f32)
        grad_pre, terms = mlp_backward(edge_rest, edge_saved, grad_edge)
        by_sender = contract_rows(onehot_sender, grad_pre).astype(bf16)
        by_sender = lax.psum_scatter(by_sender, "rows", scatter_dimension=0, tiled=True)
        by_target = contract_rows(onehot_target, grad_pre).astype(bf16)
        w_grad = jnp.concatenate(
            [
                contract_rows(edge_in, grad_pre),
                contract_rows(node_in, by_sender),
                contract_rows(node_in, by_target),
            ],
            axis=0,
        )
        edge_terms.insert(0, (w_grad,) + terms)
        grad_edge = grad_edge + contract_cols(grad_pre, w_one[:width])
        grad_node = (
            grad_node
            + contract_cols(by_sender, w_one[width : 2 * width])
            + contract_cols(by_target, w_one[2 * width :])
        )
        if layer > 0:
            grad_edge = grad_edge.astype(bf16).astype(f32)
            grad_node = grad_node.astype(bf16).astype(f32)

    def totals(terms):
        stacked = [jnp.stack(parts) for parts in zip(*terms)]
        scattered = [
            lax.psum_scatter(part.astype(bf16), "rows", scatter_dimension=1, tiled=True)
            for part in stacked
        ]
        return [lax.psum(part, "section").astype(f32) for part in scattered]

    return (final, grad_node, grad_edge) + tuple(
        x for x in totals(edge_terms) + totals(node_terms)
    )


def solution(mesh):
    def whole(*args):
        out = body(*args)
        return tuple(x[None] for x in out[:3]) + out[3:]

    in_specs = (
        P(None, "rows", None),
        P(None, "rows", None),
        P(None, "rows", None, None),
        P(None, "rows", None),
        P(None, "rows", None),
        P(None, "rows", None),
    ) + (P(),) * 12
    state = P("section", "rows", None)
    matrix, vector = P(None, "rows", None), P(None, "rows")
    out_specs = (state,) * 3 + (matrix, vector, matrix, vector, vector, vector) * 2
    return jax.shard_map(whole, mesh=mesh, in_specs=in_specs, out_specs=out_specs, check_vma=False)
```

time: 1240 us -> 592 us (0.48)
  waiting for transfers between devices: 689 us -> 443 us
  other arithmetic: 180 us -> 35.3 us
  local copies, waits for them, and re-layouts: 149 us -> 25.5 us
  starting transfers between devices: 117 us -> 0.63 us
  blocking collectives: 9.75 us -> 39.7 us
  matrix products: 52.8 us -> 31.3 us
    all_to_all x21 -> x0, waiting for transfers between devices: 123 us -> none  [the longest x13 80.7 us: fetch_senders(): lax.all_to_all(as_sent(outgoing.reshape(shards, capacity, width)), 'rows'...]
    all_to_all x21 -> x0, starting transfers between devices: 84.8 us -> none  [the longest x13 46 us: fetch_senders(): lax.all_to_all(as_sent(outgoing.reshape(shards, capacity, width)), 'rows'...]
    ppermute x12 -> x0, waiting for transfers between devices: 68.5 us -> none  [passed_along(): lax.ppermute(value, axis, [(source, source + steps) for source in range(f...]
    scatter x8 -> x0, local copies, waits for them, and re-layouts: 57.7 us -> none  [the longest x1 42.5 us: fill_row(): return table_row.at[slot_row].set(value_row)]
    unnamed x27 -> x23, waiting for transfers between devices: 295 us -> 241 us
    gather x34 -> x0, local copies, waits for them, and re-layouts: 38 us -> none  [the longest x13 15.4 us: fetch_senders(): outgoing = jnp.take(node_rows, pick_slot(wanted, micro_slot), axis=0)]
    select_n x69 -> x0, other arithmetic: 37.9 us -> none  [the longest x22 13.5 us: fetch_senders(): outgoing = jnp.take(node_rows, pick_slot(wanted, micro_slot), axis=0)]
    ppermute x12 -> x0, starting transfers between devices: 31.9 us -> none  [passed_along(): lax.ppermute(value, axis, [(source, source + steps) for source in range(f...]
  transfers between devices with their start and end apart: 49 -> 15, of which waited for: 46 -> 15; matrix products, arithmetic and copies ran while one was open for 11% -> 8% of each run, Pallas kernels for 0% -> 0%
where the time goes in v1:
time: 592 us; the launch traced here: 590 us
  waiting for transfers between devices  443 us (75%)
  blocking collectives  39.7 us (7%)
  other arithmetic  35.3 us (6%)
  matrix products  31.3 us (5%)
  local copies, waits for them, and re-layouts  25.5 us (4%)
  between operations  14.6 us (2%)
    unnamed x23, waiting for transfers between devices  241 us
    reduce_scatter x4, waiting for transfers between devices, totals(): lax.psum_scatter(part.astype(bf16), 'rows', scatter_dimension=1, tiled=True)  120 us
    reduce_scatter x2, waiting for transfers between devices, body(): lax.psum_scatter(by_sender, 'rows', scatter_dimension=0, tiled=True)  45.3 us
    psum x1, waiting for transfers between devices, totals(): return [lax.psum(part, 'section').astype(f32) for part in scattered]  36.3 us
    all_gather x2, blocking collectives, body(): all_nodes = lax.all_gather(node, 'rows', axis=0, tiled=True)  29.7 us
    unnamed x92, local copies, waits for them, and re-layouts  13.2 us
    dot_general x12, matrix products, contract_cols(): lax.dot_general(left, right, (((1,), (1,)), ((), ())), preferred_element_...  13 us
  transfers between devices with their start and end apart: 15, of which 15 were waited for; matrix products, arithmetic and copies ran while one was open for 8% of the time, Pallas kernels for 0%

profile of v1, /device:TPU:0, one launch (start us, length us, event | category | flops | bytes accessed | tf_op | source)
XLA Modules:
  0.0 590.1 jit_solution(4093143618343901186)
XLA Ops:
  7.3 0.8 constant_dynamic-slice_fusion.3
  14.9 0.9 dynamic-slice_bitcast_fusion
  15.8 15.7 %all-gather = bf16[1,128,512]{2,1,0:T(8,128)(2,1)S(1)} all-gather(bf16[1,16,512]{2,1,0:T(8,128)(2,1)S(1)} %constant_dynamic-slice_fusion.3), channel_id=2, replica_groups=mesh['section'=4,'rows'=8] {'rows'}, dimensions={1}, use_global_device_ids=true | all-gather | bytes 147456 | tf_op jit(solution)/shard_map/all_gather | solution.py:82
  32.7 1.9 fusion.13
  35.3 1.4 add_convert_fusion.1
  37.7 0.8 add_convert_fusion.4
  38.8 14.0 %all_gather.7 = bf16[128,512]{1,0:T(8,128)(2,1)S(1)} all-gather(bf16[16,512]{1,0:T(8,128)(2,1)S(1)} %add_convert_fusion.4), channel_id=1, replica_groups=mesh['section'=4,'rows'=8] {'rows'}, dimensions={0}, use_global_device_ids=true | all-gather | bytes 147456 | tf_op jit(solution)/shard_map/all_gather | solution.py:82
  55.0 1.3 fusion.114
  56.9 0.8 fusion.156
  58.1 0.8 fusion.90
  59.7 0.9 fusion.154
  60.6 0.9 convolution_convert_fusion.13
  61.6 0.9 convolution_convert_fusion.20
  62.5 2.1 fusion.11
  64.6 1.4 fusion.21
  65.9 26.9 %reduce-scatter.31.cloned.1.call-done = bf16[16,512]{1,0:T(8,128)(2,1)} async-done(((bf16[128,512]{1,0:T(8,128)(2,1)}), bf16[16,512]{1,0:T(8,128)(2,1)}) %reduce-scatter.31.cloned.1.call-update) | async-done | bytes 16400 | tf_op jit(solution)/shard_map/reduce_scatter | solution.py:115
  92.8 1.4 convolution_add_fusion.10
  94.2 1.9 fusion.112
  96.8 1.9 fusion.157
  99.1 1.5 fusion.91
  100.6 1.4 fusion.146
  102.0 1.9 fusion.155
  103.9 1.0 convolution_convert_fusion.12
  104.9 1.3 fusion.10
  106.2 2.2 pad_maximum_fusion.2
  109.1 1.1 pad_maximum_fusion.3
  111.3 1.6 pad_maximum_fusion.1
  114.9 18.5 %reduce-scatter.33.cloned.1.call-done = bf16[16,512]{1,0:T(8,128)(2,1)} async-done(((bf16[128,512]{1,0:T(8,128)(2,1)}), bf16[16,512]{1,0:T(8,128)(2,1)}) %reduce-scatter.33.cloned.1.call-update) | async-done | bytes 16400 | tf_op jit(solution)/shard_map/reduce_scatter | solution.py:115
  133.4 1.0 convolution_convert_fusion.10
  134.5 1.9 pad_maximum_fusion
  136.6 0.9 dynamic-slice_reduce_fusion
  138.2 1.3 stack.157
  140.8 1.3 stack.156
  142.8 0.8 copy.39
  144.4 1.3 stack.153
  145.7 0.8 copy.37
  147.9 0.8 copy.35
  149.5 0.8 copy.41
  151.1 0.8 copy.47
  152.7 0.8 copy.45
  153.6 0.8 copy.43
  155.1 0.8 copy.33
  156.0 10.1 %reduce-scatter.37.cloned.1.call-done = bf16[2,64,512]{2,1,0:T(8,128)(2,1)} async-done(((bf16[2,512,512]{2,1,0:T(8,128)(2,1)}), bf16[2,64,512]{2,1,0:T(8,128)(2,1)}) %reduce-scatter.37.cloned.1.call-update) | async-done | bytes 131088 | tf_op jit(solution)/shard_map/reduce_scatter | solution.py:139
  166.1 32.6 %reduce-scatter.41.cloned.1.call-done = bf16[2,64,512]{2,1,0:T(8,128)(2,1)} async-done(((bf16[2,512,512]{2,1,0:T(8,128)(2,1)}), bf16[2,64,512]{2,1,0:T(8,128)(2,1)}) %reduce-scatter.41.cloned.1.call-update) | async-done | bytes 131088 | tf_op jit(solution)/shard_map/reduce_scatter | solution.py:139
  198.8 36.4 %reduce-scatter.39.cloned.1.call-done = bf16[2,128,512]{2,1,0:T(8,128)(2,1)} async-done(((bf16[2,1024,512]{2,1,0:T(8,128)(2,1)}), bf16[2,128,512]{2,1,0:T(8,128)(2,1)}) %reduce-scatter.39.cloned.1.call-update) | async-done | bytes 262160 | tf_op jit(solution)/shard_map/reduce_scatter | solution.py:139
  235.2 41.1 %reduce-scatter.35.cloned.1.call-done = bf16[2,192,512]{2,1,0:T(8,128)(2,1)} async-done(((bf16[2,1536,512]{2,1,0:T(8,128)(2,1)}), bf16[2,192,512]{2,1,0:T(8,128)(2,1)}) %reduce-scatter.35.cloned.1.call-update) | async-done | bytes 393232 | tf_op jit(solution)/shard_map/reduce_scatter | solution.py:139
  276.3 1.0 fusion.12
  277.4 31.1 %reduce-scatter.49.cloned.1.call-done = bf16[64,2]{1,0:T(8,128)(2,1)} async-done(((bf16[512,2]{1,0:T(8,128)(2,1)}), bf16[64,2]{1,0:T(8,128)(2,1)}) %reduce-scatter.49.cloned.1.call-update) | async-done | bytes 272
  309.2 30.4 %reduce-scatter.47.cloned.1.call-done = bf16[64,2]{1,0:T(8,128)(2,1)} async-done(((bf16[512,2]{1,0:T(8,128)(2,1)}), bf16[64,2]{1,0:T(8,128)(2,1)}) %reduce-scatter.47.cloned.1.call-update) | async-done | bytes 272
  340.4 30.3 %reduce-scatter.45.cloned.1.call-done = bf16[64,2]{1,0:T(8,128)(2,1)} async-done(((bf16[512,2]{1,0:T(8,128)(2,1)}), bf16[64,2]{1,0:T(8,128)(2,1)}) %reduce-scatter.45.cloned.1.call-update) | async-done | bytes 272
  371.5 29.7 %reduce-scatter.51.cloned.1.call-done = bf16[64,2]{1,0:T(8,128)(2,1)} async-done(((bf16[512,2]{1,0:T(8,128)(2,1)}), bf16[64,2]{1,0:T(8,128)(2,1)}) %reduce-scatter.51.cloned.1.call-update) | async-done | bytes 272
  401.2 0.8 copy.42
  402.0 29.7 %reduce-scatter.57.cloned.1.call-done = bf16[64,2]{1,0:T(8,128)(2,1)} async-done(((bf16[512,2]{1,0:T(8,128)(2,1)}), bf16[64,2]{1,0:T(8,128)(2,1)}) %reduce-scatter.57.cloned.1.call-update) | async-done | bytes 272
  432.5 29.7 %reduce-scatter.55.cloned.1.call-done = bf16[64,2]{1,0:T(8,128)(2,1)} async-done(((bf16[512,2]{1,0:T(8,128)(2,1)}), bf16[64,2]{1,0:T(8,128)(2,1)}) %reduce-scatter.55.cloned.1.call-update) | async-done | bytes 272
  462.2 0.8 copy.46
  463.0 29.7 %reduce-scatter.53.cloned.1.call-done = bf16[64,2]{1,0:T(8,128)(2,1)} async-done(((bf16[512,2]{1,0:T(8,128)(2,1)}), bf16[64,2]{1,0:T(8,128)(2,1)}) %reduce-scatter.53.cloned.1.call-update) | async-done | bytes 272
  493.5 30.3 %reduce-scatter.43.cloned.1.call-done = bf16[64,2]{1,0:T(8,128)(2,1)} async-done(((bf16[512,2]{1,0:T(8,128)(2,1)}), bf16[64,2]{1,0:T(8,128)(2,1)}) %reduce-scatter.43.cloned.1.call-update) | async-done | bytes 272
  524.6 10.0 %all-reduce = (bf16[2,64]{1,0:T(2,128)(2,1)S(1)}, bf16[2,64]{1,0:T(2,128)(2,1)S(1)}, bf16[2,64]{1,0:T(2,128)(2,1)S(1)}, bf16[2,64]{1,0:T(2,128)(2,1)S(1)}, bf16[...) all-reduce(bf16[2,64]{1,0:T(2,128)(2,1)S(1)} %copy.34, ...), channel_id=1, replica_groups=mesh['section'=4,'rows'=8] {'section'}, use_global_device_ids=true, to_apply=%region_23.24 | all-reduce | flops 1024 | bytes 4096 | tf_op jit(solution)/shard_map/psum | solution.py:142
  539.3 0.9 fusion.24
  540.2 36.3 %all-reduce.4.cloned.1.call-done = (bf16[2,192,512]{2,1,0:T(8,128)(2,1)}, bf16[2,64,512]{2,1,0:T(8,128)(2,1)}, bf16[2,128,512]{2,1,0:T(8,128)(2,1)}, bf16[2,64,512]{2,1,0:T(8,128)(2,1)}) async-done(((bf16[2,192,512]{2,1,0:T(8,128)(2,1)}, bf16[2,64,512]{2,1,0:T(8,128)(2,1)}, bf16[2,128,512]{2,1,0:T(8,128)(2,1)}, bf16[2,64,512]{2,1,0:T(8,128)(2,1)}), (bf16[2,192,512]{2,1,0:T(8,128)(2,1)}, ...) | async-done | bytes 917520 | tf_op jit(solution)/shard_map/psum | solution.py:142
  576.6 1.6 convert_element_type.292
  578.2 1.6 convert_element_type.302
  579.8 2.0 convert_element_type.288
  581.8 1.8 convert_element_type.298
  (202 shorter events, 36.5 us)
Async XLA Ops:
  7.2 1.6 copy-start
  7.2 85.6 %reduce-scatter.31.cloned.1.call-start = ((), (), s32[]{:S(2)}) async-start(), calls=%async_computation.14 | async-start | bytes 147456 | tf_op jit(solution)/shard_map/reduce_scatter | solution.py:115
  7.2 27.4 %copy-start.34 = (bf16[2,512,512]{2,1,0:T(8,128)(2,1)S(1)}, bf16[2,512,512]{2,1,0:T(8,128)(2,1)}, u32[]{:S(2)}) copy-start(bf16[2,512,512]{2,1,0:T(8,128)(2,1)} %param.26) | copy-start | bytes 3145732
  8.8 52.8 %copy-start.22 = (s32[128]{0:T(128)}, s32[128]{0:T(128)S(1)}, u32[]{:S(2)}) copy-start(s32[128]{0:T(128)S(1)} %fusion.128) | copy-start | bytes 1540
  32.7 4.3 copy-start.1
  32.7 4.5 copy-start.33
  34.6 0.7 copy-start.36
  34.6 18.3 %copy-start.2 = (bf16[2,1536,512]{2,1,0:T(8,128)(2,1)S(1)}, bf16[2,1536,512]{2,1,0:T(8,128)(2,1)}, u32[]{:S(2)}) copy-start(bf16[2,1536,512]{2,1,0:T(8,128)(2,1)} %param.24) | copy-start | bytes 9437188
  35.2 2.3 copy-start.27
  36.9 16.8 %copy-start.6 = (bf16[16,512]{1,0:T(8,128)(2,1)}, bf16[16,512]{1,0:T(8,128)(2,1)S(1)}, u32[]{:S(2)}) copy-start(bf16[16,512]{1,0:T(8,128)(2,1)S(1)} %convolution_convert_fusion.22) | copy-start | bytes 49156
  37.5 16.7 %copy-start.25 = (f32[16]{0:T(128)}, f32[16]{0:T(128)S(1)}, u32[]{:S(2)}) copy-start(f32[16]{0:T(128)S(1)} %broadcast_multiply_fusion.5) | copy-start | bytes 196
  37.7 16.5 %copy-start.30 = (f32[16]{0:T(128)}, f32[16]{0:T(128)S(1)}, u32[]{:S(2)}) copy-start(f32[16]{0:T(128)S(1)} %add_rsqrt_fusion.2) | copy-start | bytes 196
  53.0 2.0 copy-start.16
  53.4 6.3 %copy-start.37 = (f32[128,512]{1,0:T(8,128)}, f32[128,512]{1,0:T(8,128)S(1)}, u32[]{:S(2)}) copy-start(f32[128,512]{1,0:T(8,128)S(1)} %fusion.16) | copy-start | bytes 786436
  54.2 3.5 copy-start.8
  54.5 3.3 copy-start.4
  56.9 0.8 copy-start.14
  57.7 2.0 copy-start.10
  59.0 35.2 %copy-start.26 = (f32[16]{0:T(128)S(1)}, f32[16]{0:T(128)}, u32[]{:S(2)}) copy-start(f32[16]{0:T(128)} %copy-done.25) | copy-start | bytes 196
  59.0 35.3 %copy-start.31 = (f32[16]{0:T(128)S(1)}, f32[16]{0:T(128)}, u32[]{:S(2)}) copy-start(f32[16]{0:T(128)} %copy-done.30) | copy-start | bytes 196
  61.6 71.8 %reduce-scatter.33.cloned.1.call-start = ((), (), s32[]{:S(2)}) async-start(), calls=%async_computation.15 | async-start | bytes 147456 | tf_op jit(solution)/shard_map/reduce_scatter | solution.py:115
  64.6 34.5 %copy-start.23 = (s32[128]{0:T(128)S(1)}, s32[128]{0:T(128)}, u32[]{:S(2)}) copy-start(s32[128]{0:T(128)} %copy-done.22) | copy-start | bytes 1540
  92.8 9.2 %copy-start.35 = (bf16[2,512,512]{2,1,0:T(8,128)(2,1)S(1)}, bf16[2,512,512]{2,1,0:T(8,128)(2,1)}, u32[]{:S(2)}) copy-start(bf16[2,512,512]{2,1,0:T(8,128)(2,1)} %param.26) | copy-start | bytes 3145732
  96.1 2.6 copy-start.17
  96.8 5.2 copy-start.19
  102.0 6.4 %copy-start.5 = (f32[16,512]{1,0:T(8,128)S(1)}, f32[16,512]{1,0:T(8,128)}, u32[]{:S(2)}) copy-start(f32[16,512]{1,0:T(8,128)} %copy-done.4) | copy-start | bytes 98308
  102.0 6.5 %copy-start.15 = (bf16[16,512]{1,0:T(8,128)(2,1)S(1)}, bf16[16,512]{1,0:T(8,128)(2,1)}, u32[]{:S(2)}) copy-start(bf16[16,512]{1,0:T(8,128)(2,1)} %copy-done.14) | copy-start | bytes 49156
  103.9 4.9 copy-start.20
  104.9 61.3 %reduce-scatter.37.cloned.1.call-start = ((), (), s32[]{:S(2)}) async-start(), calls=%async_computation.17 | async-start | bytes 1179648 | tf_op jit(solution)/shard_map/reduce_scatter | solution.py:139
  108.4 2.0 copy-start.9
  108.4 2.0 copy-start.11
  108.4 2.4 copy-start.7
  108.4 90.4 %reduce-scatter.41.cloned.1.call-start = ((), (), s32[]{:S(2)}) async-start(), calls=%async_computation.19 | async-start | bytes 1179648 | tf_op jit(solution)/shard_map/reduce_scatter | solution.py:139
  110.3 124.9 %reduce-scatter.39.cloned.1.call-start = ((), (), s32[]{:S(2)}) async-start(), calls=%async_computation.18 | async-start | bytes 2359296 | tf_op jit(solution)/shard_map/reduce_scatter | solution.py:139
  111.2 1.7 copy-start.21
  111.3 2.3 copy-start.24
  111.3 2.9 copy-start.13
  112.9 163.5 %reduce-scatter.35.cloned.1.call-start = ((), (), s32[]{:S(2)}) async-start(), calls=%async_computation.16 | async-start | bytes 3538944 | tf_op jit(solution)/shard_map/reduce_scatter | solution.py:139
  136.4 1.0 copy-start.28
  136.4 1.0 copy-start.29
  136.5 1.0 copy-start.32
  136.5 139.9 %copy-start.3 = (bf16[2,1536,512]{2,1,0:T(8,128)(2,1)S(1)}, bf16[2,1536,512]{2,1,0:T(8,128)(2,1)}, u32[]{:S(2)}) copy-start(bf16[2,1536,512]{2,1,0:T(8,128)(2,1)} %param.24) | copy-start | bytes 9437188
  136.5 402.7 %copy-start.12 = (bf16[16,512]{1,0:T(8,128)(2,1)S(1)}, bf16[16,512]{1,0:T(8,128)(2,1)}, u32[]{:S(2)}) copy-start(bf16[16,512]{1,0:T(8,128)(2,1)} %reduce-scatter.33.cloned.1.call-done) | copy-start | bytes 49156
  136.5 402.6 %copy-start.18 = (bf16[16,512]{1,0:T(8,128)(2,1)S(1)}, bf16[16,512]{1,0:T(8,128)(2,1)}, u32[]{:S(2)}) copy-start(bf16[16,512]{1,0:T(8,128)(2,1)} %copy-done.17) | copy-start | bytes 49156
  136.5 171.9 %reduce-scatter.49.cloned.1.call-start = ((), (), s32[]{:S(2)}) async-start(), calls=%async_computation.23 | async-start | bytes 147456
  143.6 196.0 %reduce-scatter.47.cloned.1.call-start = ((), (), s32[]{:S(2)}) async-start(), calls=%async_computation.22 | async-start | bytes 147456
  146.5 224.2 %reduce-scatter.45.cloned.1.call-start = ((), (), s32[]{:S(2)}) async-start(), calls=%async_computation.21 | async-start | bytes 147456
  148.8 252.5 %reduce-scatter.51.cloned.1.call-start = ((), (), s32[]{:S(2)}) async-start(), calls=%async_computation.24 | async-start | bytes 147456
  150.4 281.3 %reduce-scatter.57.cloned.1.call-start = ((), (), s32[]{:S(2)}) async-start(), calls=%async_computation.27 | async-start | bytes 147456
  151.9 310.2 %reduce-scatter.55.cloned.1.call-start = ((), (), s32[]{:S(2)}) async-start(), calls=%async_computation.26 | async-start | bytes 147456
  153.5 339.2 %reduce-scatter.53.cloned.1.call-start = ((), (), s32[]{:S(2)}) async-start(), calls=%async_computation.25 | async-start | bytes 147456
  155.1 368.7 %reduce-scatter.43.cloned.1.call-start = ((), (), s32[]{:S(2)}) async-start(), calls=%async_computation.20 | async-start | bytes 147456
  156.0 420.6 %all-reduce.4.cloned.1.call-start = ((), (), s32[]{:S(2)}) async-start(), calls=%async_computation.28 | async-start | bytes 1835008 | tf_op jit(solution)/shard_map/psum | solution.py:142
Sparse Core Ops, SparseCore 0:
  61.7 31.0 reduce-scatter.30
  105.0 28.3 reduce-scatter.32
  135.6 30.4 reduce-scatter.36
  168.3 30.4 reduce-scatter.40
  200.9 34.2 reduce-scatter.38
  237.3 38.9 reduce-scatter.34
  279.1 29.2 reduce-scatter.48
  311.3 28.2 reduce-scatter.46
  342.5 28.2 reduce-scatter.44
  372.9 28.2 reduce-scatter.50
  403.5 28.1 reduce-scatter.56
  433.9 28.2 reduce-scatter.54
  464.4 28.2 reduce-scatter.52
  495.5 28.3 reduce-scatter.42
  527.1 49.4 all-reduce.3

commit v2 on v1

v2 whole, which is shorter than its diff:
```python
import functools
from types import SimpleNamespace

import jax
import jax.numpy as jnp
from jax import lax
from jax.experimental import pallas as pl
from jax.experimental.pallas import tpu as pltpu
from jax.sharding import PartitionSpec as P

f32 = jnp.float32
bf16 = jnp.bfloat16
MESH = pl.DeviceIdType.MESH
norm_epsilon = 1e-05
vector_rows = 16
w_one, b_one, w_two, b_two, gain, shift = range(6)


def dot(left, right):
    return jnp.dot(left, right, preferred_element_type=f32)


def contract_rows(left, right):
    return lax.dot_general(left, right, (((0,), (0,)), ((), ())), preferred_element_type=f32)


def contract_cols(left, right):
    return lax.dot_general(left, right, (((1,), (1,)), ((), ())), preferred_element_type=f32)


def whole_tiles(rows):
    return -(-rows // 16) * 16


def each(count, visit):
    if count <= 8:
        for i in range(count):
            visit(i)
    else:

        def step(i, carry):
            visit(i)
            return carry

        lax.fori_loop(0, count, step, 0)


def layer_norm(lifted):
    center = lifted - jnp.mean(lifted, axis=-1, keepdims=True)
    scale = lax.rsqrt(jnp.mean(center * center, axis=-1, keepdims=True) + norm_epsilon)
    return center * scale, scale


def activate(pre):
    sigma = jax.nn.sigmoid(pre)
    return (pre * sigma).astype(bf16), sigma * (1.0 + pre * (1.0 - sigma))


def branch_back(grad_branch, gain_row, normed, scale):
    grad_normed = grad_branch * gain_row
    return (
        scale
        * (
            grad_normed
            - jnp.mean(grad_normed, axis=-1, keepdims=True)
            - normed * jnp.mean(grad_normed * normed, axis=-1, keepdims=True)
        )
    ).astype(bf16)


def column_sums(grad_pre, grad_lifted, grad_branch, normed):
    rows = [
        jnp.sum(grad_pre.astype(f32), axis=0, keepdims=True),
        jnp.sum(grad_lifted.astype(f32), axis=0, keepdims=True),
        jnp.sum(grad_branch * normed, axis=0, keepdims=True),
        jnp.sum(grad_branch, axis=0, keepdims=True),
    ]
    rows.append(jnp.zeros((vector_rows - 4, grad_branch.shape[1]), f32))
    return jnp.concatenate(rows, axis=0).astype(bf16)


def send(source, target, send_sem, recv_sem, device):
    pltpu.make_async_remote_copy(
        src_ref=source,
        dst_ref=target,
        send_sem=send_sem,
        recv_sem=recv_sem,
        device_id=device,
        device_id_type=MESH,
    ).start()


def ended(buffer, sem):
    pltpu.make_async_copy(buffer, buffer, sem).wait()


def kernel(plan, *refs):
    v = SimpleNamespace(**dict(zip(plan.names, refs)))
    layers, sections, shards = plan.layers, plan.sections, plan.shards
    node_dev, edge_dev, width = plan.node_dev, plan.edge_dev, plan.width
    quarter, pairs, plane = width // sections, shards // 2, 2 * sections
    nodes_total = shards * node_dev
    three_rows, two_rows, one_rows = (part * width // shards for part in (3, 2, 1))
    edge_weights, node_weights = refs[plan.weights : plan.weights + 6], refs[
        plan.weights + 6 : plan.weights + 12
    ]
    edge_v, node_v = refs[plan.weights_v : plan.weights_v + 6], refs[
        plan.weights_v + 6 : plan.weights_v + 12
    ]
    grads = refs[plan.grads : plan.grads + 12]
    section, row = lax.axis_index("section"), lax.axis_index("rows")
    pair, core = row // 2, row % 2
    plane_slot = section * 2 + core

    def group(data, send_sem, recv_sem):
        return SimpleNamespace(data=data, send=send_sem, recv=recv_sem)

    def pair_group(own, come, send_sem, recv_sem, total, full, full_send, full_recv):
        return SimpleNamespace(
            own=own,
            come=come,
            send=send_sem,
            recv=recv_sem,
            total=total,
            full=full,
            full_send=full_send,
            full_recv=full_recv,
        )

    lefts = group(v.lefts, v.lefts_send, v.lefts_recv)
    rights = group(v.rights, v.rights_send, v.rights_recv)
    node_lefts = group(v.node_lefts, v.node_lefts_send, v.node_lefts_recv)
    node_rights = group(v.node_rights, v.node_rights_send, v.node_rights_recv)
    sum_rights = group(v.sum_rights, v.sum_rights_send, v.sum_rights_recv)
    edge_pairs, lift_pairs, node_pairs = (
        pair_group(*refs[start : start + 8])
        for start in range(plan.pair_groups, plan.pair_groups + 24, 8)
    )

    loads = {}

    def load(key, source, target):
        copy = pltpu.make_async_copy(source, target, v.load_sem.at[len(loads)])
        copy.start()
        loads[key] = copy

    load(0, v.node_features.at[section], v.nodes.at[0, row])
    load(1, v.owner.at[section], v.owner_v)
    load(2, v.local.at[section], v.local_v)
    load(3, v.receivers.at[section], v.receivers_v)
    load(4, v.edge_features.at[section], v.edge_in.at[0])
    for kind in (b_one, b_two, gain, shift):
        load((0, kind), edge_weights[kind], edge_v[kind])
        load((1, kind), node_weights[kind], node_v[kind])
    for layer in range(layers):
        for kind in (w_one, w_two):
            load((0, kind, layer), edge_weights[kind].at[layer], edge_v[kind].at[layer])
        for kind in (w_one, w_two):
            load((1, kind, layer), node_weights[kind].at[layer], node_v[kind].at[layer])
    load(5, v.cotangent.at[section], v.cotangent_v)

    barrier = pltpu.get_barrier_semaphore()

    def greet(device):
        pl.semaphore_signal(barrier, inc=1, device_id=device, device_id_type=MESH)

    each(shards - 1, lambda i: greet((section, (row + 1 + i) % shards)))
    for step in range(1, sections):
        for other in range(2):
            greet(((section + step) % sections, pair * 2 + other))

    def peer_rows(visit):
        each(shards - 1, lambda i: visit((row + 1 + i) % shards))

    def send_nodes(layer):
        def one(peer):
            send(
                v.nodes.at[layer, row],
                v.nodes.at[layer, row],
                v.nodes_send.at[layer, peer],
                v.nodes_recv.at[layer, row],
                (section, peer),
            )

        peer_rows(one)

    def send_sums(layer):
        def one(peer):
            send(
                v.sums.at[layer, peer],
                v.sums_in.at[layer, row],
                v.sums_send.at[layer, peer],
                v.sums_recv.at[layer, row],
                (section, peer),
            )

        peer_rows(one)

    def from_rows(data, sem, layer):
        peer_rows(lambda peer: ended(data.at[layer, peer], sem.at[layer, peer]))

    def to_plane(group, layer, sources):
        def one(target_section, other):
            source = sources[other](target_section)
            send(
                source,
                group.data.at[layer, plane_slot, pl.ds(0, source.shape[0])],
                group.send.at[layer, target_section * 2 + other],
                group.recv.at[layer, plane_slot],
                (target_section, pair * 2 + other),
            )

        for step in range(1, sections):
            for other in range(2):
                if sources[other] is not None:
                    one((section + step) % sections, other)
        for other in range(2):
            if sources[other] is None:
                continue

            @pl.when(core != other)
            def _(other=other):
                one(section, other)

            @pl.when(core == other)
            def _(other=other):
                source = sources[other](section)
                group.data[layer, plane_slot, 0 : source.shape[0]] = source[...]

    def from_plane(group, layer, rows):
        for step in range(1, plane):
            slot = (plane_slot + step) % plane
            ended(group.data.at[layer, slot, pl.ds(0, rows)], group.recv.at[layer, slot])

    def plane_left(group, layer, rows):
        def one(target_section, other):
            ended(
                group.data.at[layer, 0, pl.ds(0, rows[other])],
                group.send.at[layer, target_section * 2 + other],
            )

        for other in range(2):
            if rows[other]:
                for step in range(1, sections):
                    one((section + step) % sections, other)
                pl.when(core != other)(functools.partial(one, section, other))

    def peer_pairs(visit):
        each(pairs - 1, lambda i: visit((pair + 1 + i) % pairs))

    def send_pairs(group, layer):
        def one(peer):
            send(
                group.own.at[layer, peer],
                group.come.at[layer, pair],
                group.send.at[layer, peer],
                group.recv.at[layer, pair],
                (section, peer * 2 + core),
            )

        peer_pairs(one)

    def share(group, layer, target_section, other):
        send(
            group.total.at[layer, other],
            group.full.at[layer, section],
            group.full_send.at[layer, target_section * 2 + other],
            group.full_recv.at[layer, section],
            (target_section, pair * 2 + other),
        )

    def add_pairs(group, layer):
        peer_pairs(lambda peer: ended(group.come.at[layer, peer], group.recv.at[layer, peer]))
        group.come[layer, pair] = group.own[layer, pair]
        total = group.come[layer, 0].astype(f32)
        for peer in range(1, pairs):
            total = total + group.come[layer, peer].astype(f32)
        group.total[layer] = total.astype(bf16)
        for step in range(1, sections):
            for other in range(2):
                share(group, layer, (section + step) % sections, other)
        share(group, layer, section, 1 - core)
        group.full[layer, section] = group.total[layer, core]

    def pairs_left(group, layer):
        peer_pairs(lambda peer: ended(group.own.at[layer, peer], group.send.at[layer, peer]))
        for step in range(1, plane):
            ended(group.total.at[layer, 0], group.full_send.at[layer, (plane_slot + step) % plane])

    def from_givers(group, layer, giver):
        for step in range(1, sections):
            slot = (section + step) % sections
            ended(group.full.at[layer, slot], group.full_recv.at[layer, slot])

        @pl.when(core != giver)
        def _():
            ended(group.full.at[layer, section], group.full_recv.at[layer, section])

    def store_blocks(target, product, offset, rows):
        padded = whole_tiles(rows)
        for owner in range(shards):
            block = product[owner * rows : (owner + 1) * rows]
            if padded != rows:
                block = jnp.concatenate([block, jnp.zeros((padded - rows, quarter), f32)], axis=0)
            target[owner // 2, owner % 2, offset : offset + padded] = block.astype(bf16)

    def store_vectors(target, total, offset):
        for owner in range(shards):
            target[owner // 2, owner % 2, offset : offset + vector_rows] = total.astype(bf16)

    def quarters(target, offset, value):
        rows = value.shape[0]
        for part in range(sections):
            target[part, offset : offset + rows] = value[
                :, part * quarter : (part + 1) * quarter
            ].astype(bf16)

    def vector(ref, layer):
        return ref[...].astype(f32)[layer : layer + 1]

    pl.semaphore_wait(barrier, shards - 1 + 2 * (sections - 1))
    loads[0].wait()
    send_nodes(0)
    loads[4].wait()
    to_plane(lefts, 0, (lambda s: v.edge_in.at[0], None))

    for key in (1, 2, 3):
        loads[key].wait()
    sender_row = v.owner_v[...] * node_dev + v.local_v[...]
    target_row = v.receivers_v[...]
    eye = lax.broadcasted_iota(jnp.int32, (edge_dev, edge_dev), 0) == lax.broadcasted_iota(
        jnp.int32, (edge_dev, edge_dev), 1
    )

    def to_column(values):
        spread = jnp.broadcast_to(values, (edge_dev, edge_dev))
        column = jnp.sum(jnp.where(eye, spread, 0).astype(f32), axis=1, keepdims=True)
        return column.astype(jnp.int32)

    def one_hot(values, count, axis):
        places = (count, edge_dev) if axis == 0 else (edge_dev, count)
        match = lax.broadcasted_iota(jnp.int32, places, axis) == values
        return jnp.where(match, 1.0, 0.0).astype(bf16)

    v.from_nodes[...] = one_hot(to_column(sender_row), nodes_total, 1)
    v.to_nodes[...] = one_hot(sender_row, nodes_total, 0)
    v.from_targets[...] = one_hot(to_column(target_row), node_dev, 1)
    v.to_targets[...] = one_hot(target_row, node_dev, 0)
    for kind in (b_one, b_two, gain, shift):
        loads[(0, kind)].wait()
        loads[(1, kind)].wait()

    def edge_forward(layer):
        node = v.nodes[layer, row]
        edge = v.edge_in[layer]
        loads[(0, w_one, layer)].wait()
        received = dot(v.from_targets[...], node).astype(bf16)
        v.work[...] = (
            dot(edge, edge_v[w_one][layer, 0:width])
            + dot(received, edge_v[w_one][layer, 2 * width : 3 * width])
            + vector(edge_v[b_one], layer)
        )
        from_rows(v.nodes, v.nodes_recv, layer)
        sent = dot(v.from_nodes[...], v.nodes[layer].reshape(nodes_total, width)).astype(bf16)
        hidden, slope = activate(
            v.work[...] + dot(sent, edge_v[w_one][layer, width : 2 * width])
        )
        v.edge_hidden[layer] = hidden
        v.edge_slope[layer] = slope
        to_plane(lefts, layer, (None, lambda s: v.edge_hidden.at[layer]))
        loads[(0, w_two, layer)].wait()
        normed, scale = layer_norm(
            dot(hidden, edge_v[w_two][layer]) + vector(edge_v[b_two], layer)
        )
        v.edge_normed[layer] = normed
        v.edge_scale[layer] = scale
        edge = (
            edge.astype(f32)
            + (normed * vector(edge_v[gain], layer) + vector(edge_v[shift], layer))
        ).astype(bf16)
        if layer + 1 < layers:
            v.edge_in[layer + 1] = edge
            to_plane(lefts, layer + 1, (lambda s: v.edge_in.at[layer + 1], None))
        return node, dot(v.to_targets[...], edge).astype(bf16)

    def node_forward(layer, node, gathered):
        loads[(1, w_one, layer)].wait()
        hidden, slope = activate(
            dot(node, node_v[w_one][layer, 0:width])
            + dot(gathered, node_v[w_one][layer, width : 2 * width])
            + vector(node_v[b_one], layer)
        )
        v.node_slope[layer] = slope
        loads[(1, w_two, layer)].wait()
        normed, scale = layer_norm(
            dot(hidden, node_v[w_two][layer]) + vector(node_v[b_two], layer)
        )
        v.node_normed[layer] = normed
        v.node_scale[layer] = scale
        new_node = (
            node.astype(f32)
            + (normed * vector(node_v[gain], layer) + vector(node_v[shift], layer))
        ).astype(bf16)
        if layer + 1 < layers:
            v.nodes[layer + 1, row] = new_node
            send_nodes(layer + 1)
        else:
            v.final[0] = new_node
        v.node_lefts_own[layer, 0:node_dev] = node
        v.node_lefts_own[layer, node_dev : 2 * node_dev] = gathered
        v.node_lefts_own[layer, 2 * node_dev : 3 * node_dev] = hidden
        to_plane(
            node_lefts,
            layer,
            (
                lambda s: v.node_lefts_own.at[layer, pl.ds(0, node_dev)],
                lambda s: v.node_lefts_own.at[layer],
            ),
        )

    for layer in range(layers):
        node, gathered = edge_forward(layer)
        node_forward(layer, node, gathered)

    def node_products(layer):
        @pl.when(core == 1)
        def _():
            from_plane(node_lefts, layer, 3 * node_dev)
            from_plane(node_rights, layer, 2 * node_dev + vector_rows)
            own = plane * node_dev
            state = v.node_lefts[layer, :, 0:node_dev].reshape(own, width)
            gathered = v.node_lefts[layer, :, node_dev : 2 * node_dev].reshape(own, width)
            hidden = v.node_lefts[layer, :, 2 * node_dev : 3 * node_dev].reshape(own, width)
            grad_pre = v.node_rights[layer, :, 0:node_dev].reshape(own, quarter)
            grad_lifted = v.node_rights[layer, :, node_dev : 2 * node_dev].reshape(own, quarter)
            vectors = v.node_rights[layer, :, 2 * node_dev : 2 * node_dev + vector_rows]
            v.product[0:width] = contract_rows(state, grad_pre)
            v.product[width : 2 * width] = contract_rows(gathered, grad_pre)
            v.product[2 * width : 3 * width] = contract_rows(hidden, grad_lifted)
            target = node_pairs.own.at[layer]
            store_blocks(target, v.product, 0, two_rows)
            start = whole_tiles(two_rows)
            store_blocks(target, v.product.at[pl.ds(2 * width, width)], start, one_rows)
            start += whole_tiles(one_rows)
            store_vectors(target, jnp.sum(vectors.astype(f32), axis=0), start)
            send_pairs(node_pairs, layer)

    def edge_products(layer):
        own = plane * edge_dev

        @pl.when(core == 0)
        def _():
            from_plane(lefts, layer, edge_dev)
            from_plane(rights, layer, edge_dev)
            v.product[0:width] = contract_rows(
                v.lefts[layer].reshape(own, width),
                v.rights[layer, :, 0:edge_dev].reshape(own, quarter),
            )
            from_plane(node_lefts, layer, node_dev)
            from_plane(sum_rights, layer, 2 * node_dev)
            own_nodes = plane * node_dev
            state = v.node_lefts[layer, :, 0:node_dev].reshape(own_nodes, width)
            for part in range(2):
                start = part * node_dev
                v.product[(1 + part) * width : (2 + part) * width] = contract_rows(
                    state,
                    v.sum_rights[layer, :, start : start + node_dev].reshape(own_nodes, quarter),
                )
            store_blocks(edge_pairs.own.at[layer], v.product, 0, three_rows)
            send_pairs(edge_pairs, layer)

        @pl.when(core == 1)
        def _():
            from_plane(lefts, layer, edge_dev)
            from_plane(rights, layer, edge_dev + vector_rows)
            v.product[0:width] = contract_rows(
                v.lefts[layer].reshape(own, width),
                v.rights[layer, :, 0:edge_dev].reshape(own, quarter),
            )
            vectors = v.rights[layer, :, edge_dev : edge_dev + vector_rows]
            target = lift_pairs.own.at[layer]
            store_blocks(target, v.product, 0, one_rows)
            store_vectors(target, jnp.sum(vectors.astype(f32), axis=0), whole_tiles(one_rows))
            send_pairs(lift_pairs, layer)

    def add_node_products(layer):
        pl.when(core == 1)(lambda: add_pairs(node_pairs, layer))

    def add_edge_products(layer):
        pl.when(core == 0)(lambda: add_pairs(edge_pairs, layer))
        pl.when(core == 1)(lambda: add_pairs(lift_pairs, layer))

    def take_columns(value):
        per = quarter // one_rows
        taken = jnp.zeros((vector_rows, one_rows), f32)
        for place in range(per):
            taken = taken + jnp.where(
                row % per == place, value[:, place * one_rows : (place + 1) * one_rows], 0.0
            )
        return taken

    def write_outputs(layer):
        from_givers(edge_pairs, layer, 0)
        from_givers(lift_pairs, layer, 1)
        from_givers(node_pairs, layer, 1)
        node_start = whole_tiles(two_rows)
        for part in range(sections):
            columns = slice(part * quarter, (part + 1) * quarter)

            def put(target, group, start, rows):
                value = group.full[layer, part, start : start + whole_tiles(rows)]
                target[layer, :, columns] = value.astype(f32)[0:rows]

            put(grads[w_one], edge_pairs, 0, three_rows)
            put(grads[w_two], lift_pairs, 0, one_rows)
            put(grads[6 + w_one], node_pairs, 0, two_rows)
            put(grads[6 + w_two], node_pairs, node_start, one_rows)
        holder = row // (quarter // one_rows)
        start = whole_tiles(one_rows)
        edge_vectors = take_columns(
            lift_pairs.full[layer, holder, start : start + vector_rows].astype(f32)
        )
        start += node_start
        node_vectors = take_columns(
            node_pairs.full[layer, holder, start : start + vector_rows].astype(f32)
        )
        for place, kind in enumerate((b_one, b_two, gain, shift)):
            grads[kind][layer : layer + 1] = edge_vectors[place : place + 1]
            grads[6 + kind][layer : layer + 1] = node_vectors[place : place + 1]

    def node_backward(layer):
        grad_branch = v.grad_node[...]
        normed = v.node_normed[layer]
        grad_lifted = branch_back(
            grad_branch, vector(node_v[gain], layer), normed, v.node_scale[layer]
        )
        grad_hidden = contract_cols(grad_lifted, node_v[w_two][layer])
        grad_pre = (grad_hidden * v.node_slope[layer]).astype(bf16)
        aggregate = contract_cols(grad_pre, node_v[w_one][layer, width : 2 * width])
        high = aggregate.astype(bf16)
        low = (aggregate - high.astype(f32)).astype(bf16)
        grad_edge = dot(v.from_targets[...], high) + dot(v.from_targets[...], low)
        if layer + 1 < layers:
            grad_edge = grad_edge + v.grad_edge[...]
        v.grad_edge[...] = grad_edge.astype(bf16).astype(f32)
        grad_node = grad_branch + contract_cols(grad_pre, node_v[w_one][layer, 0:width])
        v.grad_node[...] = grad_node.astype(bf16).astype(f32)
        target = v.node_rights_own.at[layer]
        quarters(target, 0, grad_pre)
        quarters(target, node_dev, grad_lifted)
        quarters(target, 2 * node_dev, column_sums(grad_pre, grad_lifted, grad_branch, normed))
        to_plane(node_rights, layer, (None, lambda s: v.node_rights_own.at[layer, s]))

    def edge_backward(layer):
        grad_branch = v.grad_edge[...]
        normed = v.edge_normed[layer]
        grad_lifted = branch_back(
            grad_branch, vector(edge_v[gain], layer), normed, v.edge_scale[layer]
        )
        grad_hidden = contract_cols(grad_lifted, edge_v[w_two][layer])
        grad_pre = (grad_hidden * v.edge_slope[layer]).astype(bf16)
        sums = dot(v.to_nodes[...], grad_pre).astype(bf16)
        v.sums[layer] = sums.reshape(shards, node_dev, width)
        send_sums(layer)
        target = v.lift_rights_own.at[layer]
        quarters(target, 0, grad_lifted)
        quarters(target, edge_dev, column_sums(grad_pre, grad_lifted, grad_branch, normed))
        quarters(v.pre_rights_own.at[layer], 0, grad_pre)
        to_plane(
            rights,
            layer,
            (
                lambda s: v.pre_rights_own.at[layer, s],
                lambda s: v.lift_rights_own.at[layer, s],
            ),
        )
        grad_edge = grad_branch + contract_cols(grad_pre, edge_v[w_one][layer, 0:width])
        by_target = dot(v.to_targets[...], grad_pre).astype(bf16)
        v.grad_node[...] = v.grad_node[...] + contract_cols(
            by_target, edge_v[w_one][layer, 2 * width : 3 * width]
        )
        if layer > 0:
            v.grad_edge[...] = grad_edge.astype(bf16).astype(f32)
        else:
            v.grad_edges[0] = grad_edge
        return by_target

    def sender_backward(layer, by_target):
        from_rows(v.sums_in, v.sums_recv, layer)
        v.sums_in[layer, row] = v.sums[layer, row]
        by_sender = jnp.sum(v.sums_in[layer].astype(f32), axis=0).astype(bf16)
        target = v.sum_rights_own.at[layer]
        quarters(target, 0, by_sender)
        quarters(target, node_dev, by_target)
        to_plane(sum_rights, layer, (lambda s: v.sum_rights_own.at[layer, s], None))
        grad_node = v.grad_node[...] + contract_cols(
            by_sender, edge_v[w_one][layer, width : 2 * width]
        )
        if layer > 0:
            v.grad_node[...] = grad_node.astype(bf16).astype(f32)
        else:
            v.grad_nodes[0] = grad_node

    loads[5].wait()
    v.grad_node[...] = v.cotangent_v[...].astype(f32)
    for layer in reversed(range(layers)):
        node_backward(layer)
        by_target = edge_backward(layer)
        node_products(layer)
        sender_backward(layer, by_target)
        edge_products(layer)
        add_node_products(layer)
        add_edge_products(layer)

    for layer in range(layers):
        write_outputs(layer)

    for layer in range(layers):
        from_rows(v.nodes, v.nodes_send, layer)
        from_rows(v.sums, v.sums_send, layer)
        plane_left(lefts, layer, (edge_dev, edge_dev))
        plane_left(node_lefts, layer, (node_dev, 3 * node_dev))
        plane_left(node_rights, layer, (0, 2 * node_dev + vector_rows))
        plane_left(rights, layer, (edge_dev, edge_dev + vector_rows))
        plane_left(sum_rights, layer, (2 * node_dev, 0))

        @pl.when(core == 0)
        def _():
            pairs_left(edge_pairs, layer)

        @pl.when(core == 1)
        def _():
            pairs_left(node_pairs, layer)
            pairs_left(lift_pairs, layer)


def copy_kernel(count, *refs):
    for source, target in zip(refs[:count], refs[count:]):
        target[...] = source[...]


def fused(sections, shards, node_features, edge_features, owner, local, receivers, cotangent, *weights):
    micro_count, node_dev, width = node_features.shape
    edge_dev = edge_features.shape[1]
    layers = weights[0].shape[0]
    quarter, pairs, plane = width // sections, shards // 2, 2 * sections
    nodes_total = shards * node_dev

    def shape(*dims, kind=f32):
        return jax.ShapeDtypeStruct(dims, kind)

    def vmem(*dims, kind=bf16):
        return pltpu.VMEM(dims, kind)

    def sems(*dims):
        return pltpu.SemaphoreType.DMA(dims)

    inputs = dict(
        node_features=node_features,
        edge_features=edge_features,
        owner=owner,
        local=local,
        receivers=receivers,
        cotangent=cotangent,
    )
    outputs = dict(
        final=shape(1, node_dev, width, kind=bf16),
        grad_nodes=shape(1, node_dev, width),
        grad_edges=shape(1, edge_dev, width),
    )
    weight_grads = [
        shape(layers, weight.shape[1] // shards, *weight.shape[2:]) for weight in weights
    ]
    blank = SimpleNamespace(
        load_sem=sems(14 + 4 * layers),
        owner_v=vmem(1, edge_dev, kind=jnp.int32),
        local_v=vmem(1, edge_dev, kind=jnp.int32),
        receivers_v=vmem(1, edge_dev, kind=jnp.int32),
        cotangent_v=vmem(node_dev, width),
        from_nodes=vmem(edge_dev, nodes_total),
        to_nodes=vmem(nodes_total, edge_dev),
        from_targets=vmem(edge_dev, node_dev),
        to_targets=vmem(node_dev, edge_dev),
        work=vmem(edge_dev, width, kind=f32),
        grad_node=vmem(node_dev, width, kind=f32),
        grad_edge=vmem(edge_dev, width, kind=f32),
        product=vmem(3 * width, quarter, kind=f32),
        edge_in=vmem(layers, edge_dev, width),
        edge_hidden=vmem(layers, edge_dev, width),
        edge_slope=vmem(layers, edge_dev, width, kind=f32),
        edge_normed=vmem(layers, edge_dev, width, kind=f32),
        edge_scale=vmem(layers, edge_dev, 1, kind=f32),
        node_slope=vmem(layers, node_dev, width, kind=f32),
        node_normed=vmem(layers, node_dev, width, kind=f32),
        node_scale=vmem(layers, node_dev, 1, kind=f32),
        nodes=vmem(layers, shards, node_dev, width),
        nodes_send=sems(layers, shards),
        nodes_recv=sems(layers, shards),
        sums=vmem(layers, shards, node_dev, width),
        sums_in=vmem(layers, shards, node_dev, width),
        sums_send=sems(layers, shards),
        sums_recv=sems(layers, shards),
        lefts=vmem(layers, plane, edge_dev, width),
        lefts_send=sems(layers, plane),
        lefts_recv=sems(layers, plane),
        pre_rights_own=vmem(layers, sections, edge_dev, quarter),
        lift_rights_own=vmem(layers, sections, edge_dev + vector_rows, quarter),
        rights=vmem(layers, plane, edge_dev + vector_rows, quarter),
        rights_send=sems(layers, plane),
        rights_recv=sems(layers, plane),
        node_lefts_own=vmem(layers, 3 * node_dev, width),
        node_lefts=vmem(layers, plane, 3 * node_dev, width),
        node_lefts_send=sems(layers, plane),
        node_lefts_recv=sems(layers, plane),
        node_rights_own=vmem(layers, sections, 2 * node_dev + vector_rows, quarter),
        node_rights=vmem(layers, plane, 2 * node_dev + vector_rows, quarter),
        node_rights_send=sems(layers, plane),
        node_rights_recv=sems(layers, plane),
        sum_rights_own=vmem(layers, sections, 2 * node_dev, quarter),
        sum_rights=vmem(layers, plane, 2 * node_dev, quarter),
        sum_rights_send=sems(layers, plane),
        sum_rights_recv=sems(layers, plane),
    )
    scratch = vars(blank)
    lift_block = whole_tiles(width // shards) + vector_rows
    pair_groups = []
    for block in (
        whole_tiles(3 * width // shards),
        lift_block,
        whole_tiles(2 * width // shards) + lift_block,
    ):
        pair_groups += [
            vmem(layers, pairs, 2, block, quarter),
            vmem(layers, pairs, 2, block, quarter),
            sems(layers, pairs),
            sems(layers, pairs),
            vmem(layers, 2, block, quarter),
            vmem(layers, sections, block, quarter),
            sems(layers, plane),
            sems(layers, sections),
        ]
    weights_v = [pltpu.VMEM(weight.shape, weight.dtype) for weight in weights]
    out_shape = list(outputs.values()) + weight_grads
    ins = len(inputs) + len(weights)
    outs = ins + len(out_shape)
    plan = SimpleNamespace(
        names=list(inputs)
        + list(range(len(weights)))
        + list(outputs)
        + list(range(len(weights)))
        + list(scratch),
        weights=len(inputs),
        grads=ins + len(outputs),
        pair_groups=outs + len(scratch),
        weights_v=outs + len(scratch) + len(pair_groups),
        layers=layers,
        sections=sections,
        shards=shards,
        node_dev=node_dev,
        edge_dev=edge_dev,
        width=width,
    )
    plan.names = [str(name) for name in plan.names]
    results = pl.pallas_call(
        functools.partial(kernel, plan),
        out_shape=out_shape,
        in_specs=[pl.BlockSpec(memory_space=pltpu.HBM)] * ins,
        out_specs=[pl.BlockSpec(memory_space=pltpu.VMEM)] * len(out_shape),
        scratch_shapes=list(scratch.values()) + pair_groups + weights_v,
        compiler_params=pltpu.CompilerParams(
            collective_id=0, has_side_effects=True, vmem_limit_bytes=60 << 20
        ),
    )(*inputs.values(), *weights)
    return pl.pallas_call(
        functools.partial(copy_kernel, len(out_shape)),
        out_shape=out_shape,
        in_specs=[pl.BlockSpec(memory_space=pltpu.VMEM)] * len(out_shape),
        out_specs=[pl.BlockSpec(memory_space=pltpu.VMEM)] * len(out_shape),
    )(*results)


def solution(mesh):
    sections, shards = mesh.shape["section"], mesh.shape["rows"]

    def body(node_features, edge_features, owner, *rest):
        owner = owner.reshape(owner.shape[:-1])
        return fused(sections, shards, node_features, edge_features, owner, *rest)

    in_specs = (
        P(None, "rows", None),
        P(None, "rows", None),
        P(None, "rows", None, None),
        P(None, "rows", None),
        P(None, "rows", None),
        P(None, "rows", None),
    ) + (P(),) * 12
    state = P("section", "rows", None)
    matrix, vector = P(None, "rows", None), P(None, "rows")
    out_specs = (state,) * 3 + (matrix, vector, matrix, vector, vector, vector) * 2
    return jax.shard_map(body, mesh=mesh, in_specs=in_specs, out_specs=out_specs, check_vma=False)
```

time: 592 us -> 81 us (0.14)
  the two profiles are of different devices: /device:TPU:0 before, /device:TPU:25 now
where the time goes in v2:
time: 81 us; the launch traced here: 80.8 us
  Pallas kernels  80.2 us (99%)
    pallas_call x1, Pallas kernels, fused(): pl.pallas_call(functools.partial(kernel, plan), out_shape=out_shape, in_s...  77.2 us
    pallas_call x1, Pallas kernels, fused(): pl.pallas_call(functools.partial(copy_kernel, len(out_shape)), out_shape=...  2.99 us

profile of v2, /device:TPU:25, one launch (start us, length us, event | category | flops | bytes accessed | tf_op | source)
XLA Modules:
  0.0 80.8 jit_solution(6281821896841740735)
XLA Ops:
  0.7 77.2 %shard_map.289 = (bf16[1,16,512]{2,1,0:T(8,128)(2,1)}, f32[1,16,512]{2,1,0:T(8,128)}, f32[1,128,512]{2,1,0:T(8,128)}, f32[2,192,512]{2,1,0:T(8,128)}, f32[2,64]{...) custom-call(bf16[4,16,512]{2,1,0:T(8,128)(2,1)} %refs_0_.1, ...), custom_call_target="tpu_custom_call" | custom-call | tf_op jit(solution)/shard_map/pallas_call | solution.py:764
  77.8 3.0 %shard_map.290 = (bf16[1,16,512]{2,1,0:T(8,128)(2,1)}, f32[1,16,512]{2,1,0:T(8,128)}, f32[1,128,512]{2,1,0:T(8,128)}, f32[2,192,512]{2,1,0:T(8,128)}, f32[2,64]{...) custom-call(bf16[1,16,512]{2,1,0:T(8,128)(2,1)} %get-tuple-element.3, ...), custom_call_target="tpu_custom_call" | custom-call | tf_op jit(solution)/shard_map/pallas_call | solution.py:774

commit v3 on v2

--- a/solution.py
+++ b/solution.py
@@ -107,7 +107,6 @@
     edge_v, node_v = refs[plan.weights_v : plan.weights_v + 6], refs[
         plan.weights_v + 6 : plan.weights_v + 12
     ]
-    grads = refs[plan.grads : plan.grads + 12]
     section, row = lax.axis_index("section"), lax.axis_index("rows")
     pair, core = row // 2, row % 2
     plane_slot = section * 2 + core
@@ -115,8 +114,9 @@
     def group(data, send_sem, recv_sem):
         return SimpleNamespace(data=data, send=send_sem, recv=recv_sem)
 
-    def pair_group(own, come, send_sem, recv_sem, total, full, full_send, full_recv):
+    def pair_group(place, full, own, come, send_sem, recv_sem, total, full_send, full_recv):
         return SimpleNamespace(
+            place=place,
             own=own,
             come=come,
             send=send_sem,
@@ -127,14 +127,16 @@
             full_recv=full_recv,
         )
 
-    lefts = group(v.lefts, v.lefts_send, v.lefts_recv)
-    rights = group(v.rights, v.rights_send, v.rights_recv)
     node_lefts = group(v.node_lefts, v.node_lefts_send, v.node_lefts_recv)
     node_rights = group(v.node_rights, v.node_rights_send, v.node_rights_recv)
     sum_rights = group(v.sum_rights, v.sum_rights_send, v.sum_rights_recv)
     edge_pairs, lift_pairs, node_pairs = (
-        pair_group(*refs[start : start + 8])
-        for start in range(plan.pair_groups, plan.pair_groups + 24, 8)
+        pair_group(
+            place,
+            refs[plan.fulls + place],
+            *refs[plan.pair_groups + 7 * place : plan.pair_groups + 7 * place + 7],
+        )
+        for place in range(3)
     )
 
     loads = {}
@@ -172,10 +174,10 @@
     def peer_rows(visit):
         each(shards - 1, lambda i: visit((row + 1 + i) % shards))
 
-    def send_nodes(layer):
+    def send_nodes(layer, source):
         def one(peer):
             send(
-                v.nodes.at[layer, row],
+                source,
                 v.nodes.at[layer, row],
                 v.nodes_send.at[layer, peer],
                 v.nodes_recv.at[layer, row],
@@ -244,6 +246,55 @@
                 for step in range(1, sections):
                     one((section + step) % sections, other)
                 pl.when(core != other)(functools.partial(one, section, other))
+
+    def to_mate(taker, buffer, send_sem, recv_sem, source):
+        @pl.when(core != taker)
+        def _():
+            send(
+                source,
+                buffer.at[pl.ds(0, source.shape[0])],
+                send_sem,
+                recv_sem,
+                (section, row + 1 - 2 * core),
+            )
+
+    def to_mate_left(taker, layer, states):
+        to_mate(
+            taker,
+            v.mate_left.at[layer],
+            v.mate_left_send.at[layer],
+            v.mate_left_recv.at[layer],
+            states.at[layer],
+        )
+
+    def to_mate_right(taker, layer, source):
+        to_mate(
+            taker,
+            v.mate_right.at[layer],
+            v.mate_right_send.at[layer],
+            v.mate_right_recv.at[layer],
+            source.at[layer],
+        )
+
+    def from_mate(layer, rows):
+        ended(v.mate_left.at[layer], v.mate_left_recv.at[layer])
+        ended(v.mate_right.at[layer, pl.ds(0, rows)], v.mate_right_recv.at[layer])
+
+    def send_parts(layer, rows):
+        for step in range(1, sections):
+            target = (section + step) % sections
+            send(
+                v.parts.at[layer, target, pl.ds(0, rows)],
+                v.parts_in.at[layer, section, pl.ds(0, rows)],
+                v.parts_send.at[layer, target],
+                v.parts_recv.at[layer, section],
+                (target, row),
+            )
+
+    def from_sections(buffer, sem, layer, rows):
+        for step in range(1, sections):
+            other = (section + step) % sections
+            ended(buffer.at[layer, other, pl.ds(0, rows)], sem.at[layer, other])
 
     def peer_pairs(visit):
         each(pairs - 1, lambda i: visit((pair + 1 + i) % pairs))
@@ -280,7 +331,11 @@
             for other in range(2):
                 share(group, layer, (section + step) % sections, other)
         share(group, layer, section, 1 - core)
-        group.full[layer, section] = group.total[layer, core]
+        copy = pltpu.make_async_copy(
+            group.total.at[layer, core], group.full.at[layer, section], v.own_sem.at[group.place]
+        )
+        copy.start()
+        copy.wait()
 
     def pairs_left(group, layer):
         peer_pairs(lambda peer: ended(group.own.at[layer, peer], group.send.at[layer, peer]))
@@ -315,14 +370,18 @@
                 :, part * quarter : (part + 1) * quarter
             ].astype(bf16)
 
+    def write(place, value, staged, target):
+        staged[0] = value
+        pltpu.make_async_copy(staged, target, v.write_sem.at[place]).start()
+
     def vector(ref, layer):
         return ref[...].astype(f32)[layer : layer + 1]
 
     pl.semaphore_wait(barrier, shards - 1 + 2 * (sections - 1))
+    send_nodes(0, v.node_features.at[section])
     loads[0].wait()
-    send_nodes(0)
     loads[4].wait()
-    to_plane(lefts, 0, (lambda s: v.edge_in.at[0], None))
+    to_mate_left(0, 0, v.edge_in)
 
     for key in (1, 2, 3):
         loads[key].wait()
@@ -367,7 +426,7 @@
         )
         v.edge_hidden[layer] = hidden
         v.edge_slope[layer] = slope
-        to_plane(lefts, layer, (None, lambda s: v.edge_hidden.at[layer]))
+        to_mate_left(1, layer, v.edge_hidden)
         loads[(0, w_two, layer)].wait()
         normed, scale = layer_norm(
             dot(hidden, edge_v[w_two][layer]) + vector(edge_v[b_two], layer)
@@ -380,7 +439,7 @@
         ).astype(bf16)
         if layer + 1 < layers:
             v.edge_in[layer + 1] = edge
-            to_plane(lefts, layer + 1, (lambda s: v.edge_in.at[layer + 1], None))
+            to_mate_left(0, layer + 1, v.edge_in)
         return node, dot(v.to_targets[...], edge).astype(bf16)
 
     def node_forward(layer, node, gathered):
@@ -403,9 +462,9 @@
         ).astype(bf16)
         if layer + 1 < layers:
             v.nodes[layer + 1, row] = new_node
-            send_nodes(layer + 1)
+            send_nodes(layer + 1, v.nodes.at[layer + 1, row])
         else:
-            v.final[0] = new_node
+            write(0, new_node, v.final_v, v.final)
         v.node_lefts_own[layer, 0:node_dev] = node
         v.node_lefts_own[layer, node_dev : 2 * node_dev] = gathered
         v.node_lefts_own[layer, 2 * node_dev : 3 * node_dev] = hidden
@@ -445,17 +504,46 @@
             store_vectors(target, jnp.sum(vectors.astype(f32), axis=0), start)
             send_pairs(node_pairs, layer)
 
-    def edge_products(layer):
-        own = plane * edge_dev
+    def edge_parts(layer):
+        def multiply(own_left, own_right):
+            left = jnp.concatenate([own_left[layer], v.mate_left[layer]], axis=0)
+            right = jnp.concatenate(
+                [own_right[layer, 0:edge_dev], v.mate_right[layer, 0:edge_dev]], axis=0
+            )
+            for part in range(sections):
+                columns = slice(part * quarter, (part + 1) * quarter)
+                v.parts[layer, part, 0:width] = contract_rows(left, right[:, columns]).astype(bf16)
 
         @pl.when(core == 0)
         def _():
-            from_plane(lefts, layer, edge_dev)
-            from_plane(rights, layer, edge_dev)
-            v.product[0:width] = contract_rows(
-                v.lefts[layer].reshape(own, width),
-                v.rights[layer, :, 0:edge_dev].reshape(own, quarter),
-            )
+            from_mate(layer, edge_dev)
+            multiply(v.edge_in, v.pre_own)
+            send_parts(layer, width)
+
+        @pl.when(core == 1)
+        def _():
+            from_mate(layer, edge_dev + vector_rows)
+            multiply(v.edge_hidden, v.lift_own)
+            vectors = (
+                v.lift_own[layer, edge_dev : edge_dev + vector_rows].astype(f32)
+                + v.mate_right[layer, edge_dev : edge_dev + vector_rows].astype(f32)
+            ).astype(bf16)
+            for part in range(sections):
+                v.parts[layer, part, width : width + vector_rows] = vectors[
+                    :, part * quarter : (part + 1) * quarter
+                ]
+            send_parts(layer, width + vector_rows)
+
+    def add_parts(layer, start, rows):
+        total = v.parts[layer, section, start : start + rows].astype(f32)
+        for step in range(1, sections):
+            other = (section + step) % sections
+            total = total + v.parts_in[layer, other, start : start + rows].astype(f32)
+        return total
+
+    def edge_products(layer):
+        @pl.when(core == 0)
+        def _():
             from_plane(node_lefts, layer, node_dev)
             from_plane(sum_rights, layer, 2 * node_dev)
             own_nodes = plane * node_dev
@@ -466,21 +554,18 @@
                     state,
                     v.sum_rights[layer, :, start : start + node_dev].reshape(own_nodes, quarter),
                 )
+            from_sections(v.parts_in, v.parts_recv, layer, width)
+            v.product[0:width] = add_parts(layer, 0, width)
             store_blocks(edge_pairs.own.at[layer], v.product, 0, three_rows)
             send_pairs(edge_pairs, layer)
 
         @pl.when(core == 1)
         def _():
-            from_plane(lefts, layer, edge_dev)
-            from_plane(rights, layer, edge_dev + vector_rows)
-            v.product[0:width] = contract_rows(
-                v.lefts[layer].reshape(own, width),
-                v.rights[layer, :, 0:edge_dev].reshape(own, quarter),
-            )
-            vectors = v.rights[layer, :, edge_dev : edge_dev + vector_rows]
+            from_sections(v.parts_in, v.parts_recv, layer, width + vector_rows)
+            v.product[0:width] = add_parts(layer, 0, width)
             target = lift_pairs.own.at[layer]
             store_blocks(target, v.product, 0, one_rows)
-            store_vectors(target, jnp.sum(vectors.astype(f32), axis=0), whole_tiles(one_rows))
+            store_vectors(target, add_parts(layer, width, vector_rows), whole_tiles(one_rows))
             send_pairs(lift_pairs, layer)
 
     def add_node_products(layer):
@@ -489,44 +574,6 @@
     def add_edge_products(layer):
         pl.when(core == 0)(lambda: add_pairs(edge_pairs, layer))
         pl.when(core == 1)(lambda: add_pairs(lift_pairs, layer))
-
-    def take_columns(value):
-        per = quarter // one_rows
-        taken = jnp.zeros((vector_rows, one_rows), f32)
-        for place in range(per):
-            taken = taken + jnp.where(
-                row % per == place, value[:, place * one_rows : (place + 1) * one_rows], 0.0
-            )
-        return taken
-
-    def write_outputs(layer):
-        from_givers(edge_pairs, layer, 0)
-        from_givers(lift_pairs, layer, 1)
-        from_givers(node_pairs, layer, 1)
-        node_start = whole_tiles(two_rows)
-        for part in range(sections):
-            columns = slice(part * quarter, (part + 1) * quarter)
-
-            def put(target, group, start, rows):
-                value = group.full[layer, part, start : start + whole_tiles(rows)]
-                target[layer, :, columns] = value.astype(f32)[0:rows]
-
-            put(grads[w_one], edge_pairs, 0, three_rows)
-            put(grads[w_two], lift_pairs, 0, one_rows)
-            put(grads[6 + w_one], node_pairs, 0, two_rows)
-            put(grads[6 + w_two], node_pairs, node_start, one_rows)
-        holder = row // (quarter // one_rows)
-        start = whole_tiles(one_rows)
-        edge_vectors = take_columns(
-            lift_pairs.full[layer, holder, start : start + vector_rows].astype(f32)
-        )
-        start += node_start
-        node_vectors = take_columns(
-            node_pairs.full[layer, holder, start : start + vector_rows].astype(f32)
-        )
-        for place, kind in enumerate((b_one, b_two, gain, shift)):
-            grads[kind][layer : layer + 1] = edge_vectors[place : place + 1]
-            grads[6 + kind][layer : layer + 1] = node_vectors[place : place + 1]
 
     def node_backward(layer):
         grad_branch = v.grad_node[...]
@@ -562,18 +609,13 @@
         sums = dot(v.to_nodes[...], grad_pre).astype(bf16)
         v.sums[layer] = sums.reshape(shards, node_dev, width)
         send_sums(layer)
-        target = v.lift_rights_own.at[layer]
-        quarters(target, 0, grad_lifted)
-        quarters(target, edge_dev, column_sums(grad_pre, grad_lifted, grad_branch, normed))
-        quarters(v.pre_rights_own.at[layer], 0, grad_pre)
-        to_plane(
-            rights,
-            layer,
-            (
-                lambda s: v.pre_rights_own.at[layer, s],
-                lambda s: v.lift_rights_own.at[layer, s],
-            ),
-        )
+        v.pre_own[layer] = grad_pre
+        v.lift_own[layer, 0:edge_dev] = grad_lifted
+        v.lift_own[layer, edge_dev : edge_dev + vector_rows] = column_sums(
+            grad_pre, grad_lifted, grad_branch, normed
+        )
+        to_mate_right(0, layer, v.pre_own)
+        to_mate_right(1, layer, v.lift_own)
         grad_edge = grad_branch + contract_cols(grad_pre, edge_v[w_one][layer, 0:width])
         by_target = dot(v.to_targets[...], grad_pre).astype(bf16)
         v.grad_node[...] = v.grad_node[...] + contract_cols(
@@ -582,7 +624,7 @@
         if layer > 0:
             v.grad_edge[...] = grad_edge.astype(bf16).astype(f32)
         else:
-            v.grad_edges[0] = grad_edge
+            write(1, grad_edge, v.grad_edges_v, v.grad_edges)
         return by_target
 
     def sender_backward(layer, by_target):
@@ -599,44 +641,96 @@
         if layer > 0:
             v.grad_node[...] = grad_node.astype(bf16).astype(f32)
         else:
-            v.grad_nodes[0] = grad_node
+            write(2, grad_node, v.grad_nodes_v, v.grad_nodes)
 
     loads[5].wait()
     v.grad_node[...] = v.cotangent_v[...].astype(f32)
     for layer in reversed(range(layers)):
         node_backward(layer)
         by_target = edge_backward(layer)
+        if layer + 1 < layers:
+            edge_products(layer + 1)
+        edge_parts(layer)
         node_products(layer)
         sender_backward(layer, by_target)
-        edge_products(layer)
-        add_node_products(layer)
-        add_edge_products(layer)
-
+        if layer + 1 < layers:
+            add_node_products(layer + 1)
+            add_edge_products(layer + 1)
+    edge_products(0)
+    add_node_products(0)
+    add_edge_products(0)
+
+    for place, (staged, target) in enumerate(
+        ((v.final_v, v.final), (v.grad_edges_v, v.grad_edges), (v.grad_nodes_v, v.grad_nodes))
+    ):
+        pltpu.make_async_copy(staged, target, v.write_sem.at[place]).wait()
     for layer in range(layers):
-        write_outputs(layer)
-
-    for layer in range(layers):
+        from_givers(edge_pairs, layer, 0)
+        from_givers(lift_pairs, layer, 1)
+        from_givers(node_pairs, layer, 1)
         from_rows(v.nodes, v.nodes_send, layer)
         from_rows(v.sums, v.sums_send, layer)
-        plane_left(lefts, layer, (edge_dev, edge_dev))
         plane_left(node_lefts, layer, (node_dev, 3 * node_dev))
         plane_left(node_rights, layer, (0, 2 * node_dev + vector_rows))
-        plane_left(rights, layer, (edge_dev, edge_dev + vector_rows))
         plane_left(sum_rights, layer, (2 * node_dev, 0))
+        ended(v.mate_left.at[layer], v.mate_left_send.at[layer])
 
         @pl.when(core == 0)
         def _():
+            ended(v.mate_right.at[layer], v.mate_right_send.at[layer])
+            from_sections(v.parts, v.parts_send, layer, width)
             pairs_left(edge_pairs, layer)
 
         @pl.when(core == 1)
         def _():
+            ended(v.mate_right.at[layer, pl.ds(0, edge_dev)], v.mate_right_send.at[layer])
+            from_sections(v.parts, v.parts_send, layer, width + vector_rows)
             pairs_left(node_pairs, layer)
             pairs_left(lift_pairs, layer)
 
 
-def copy_kernel(count, *refs):
-    for source, target in zip(refs[:count], refs[count:]):
-        target[...] = source[...]
+def write_kernel(shards, *refs):
+    final, grad_nodes, grad_edges, edge_full, lift_full, node_full = refs[:6]
+    out_final, out_nodes, out_edges = refs[6:9]
+    grads = refs[9:]
+    row = lax.axis_index("rows")
+    layers, sections, quarter = edge_full.shape[0], edge_full.shape[1], edge_full.shape[3]
+    width = sections * quarter
+    three_rows, two_rows, one_rows = (part * width // shards for part in (3, 2, 1))
+    node_start = whole_tiles(two_rows)
+    out_final[...] = final[...]
+    out_nodes[...] = grad_nodes[...]
+    out_edges[...] = grad_edges[...]
+
+    def put(target, full, start, rows):
+        for layer in range(layers):
+            for part in range(sections):
+                value = full[layer, part, start : start + whole_tiles(rows)]
+                target[layer, :, part * quarter : (part + 1) * quarter] = value.astype(f32)[0:rows]
+
+    put(grads[w_one], edge_full, 0, three_rows)
+    put(grads[w_two], lift_full, 0, one_rows)
+    put(grads[6 + w_one], node_full, 0, two_rows)
+    put(grads[6 + w_two], node_full, node_start, one_rows)
+
+    def take_columns(value):
+        per = quarter // one_rows
+        taken = jnp.zeros((vector_rows, one_rows), f32)
+        for place in range(per):
+            taken = taken + jnp.where(
+                row % per == place, value[:, place * one_rows : (place + 1) * one_rows], 0.0
+            )
+        return taken
+
+    holder = row // (quarter // one_rows)
+    for layer in range(layers):
+        for first, full, start in (
+            (0, lift_full, whole_tiles(one_rows)),
+            (6, node_full, node_start + whole_tiles(one_rows)),
+        ):
+            vectors = take_columns(full[layer, holder, start : start + vector_rows].astype(f32))
+            for place, kind in enumerate((b_one, b_two, gain, shift)):
+                grads[first + kind][layer : layer + 1] = vectors[place : place + 1]
 
 
 def fused(sections, shards, node_features, edge_features, owner, local, receivers, cotangent, *weights):
@@ -671,6 +765,13 @@
     weight_grads = [
         shape(layers, weight.shape[1] // shards, *weight.shape[2:]) for weight in weights
     ]
+    lift_block = whole_tiles(width // shards) + vector_rows
+    blocks = (
+        whole_tiles(3 * width // shards),
+        lift_block,
+        whole_tiles(2 * width // shards) + lift_block,
+    )
+    fulls = [shape(layers, sections, block, quarter, kind=bf16) for block in blocks]
     blank = SimpleNamespace(
         load_sem=sems(14 + 4 * layers),
         owner_v=vmem(1, edge_dev, kind=jnp.int32),
@@ -700,14 +801,23 @@
         sums_in=vmem(layers, shards, node_dev, width),
         sums_send=sems(layers, shards),
         sums_recv=sems(layers, shards),
-        lefts=vmem(layers, plane, edge_dev, width),
-        lefts_send=sems(layers, plane),
-        lefts_recv=sems(layers, plane),
-        pre_rights_own=vmem(layers, sections, edge_dev, quarter),
-        lift_rights_own=vmem(layers, sections, edge_dev + vector_rows, quarter),
-        rights=vmem(layers, plane, edge_dev + vector_rows, quarter),
-        rights_send=sems(layers, plane),
-        rights_recv=sems(layers, plane),
+        final_v=vmem(1, node_dev, width),
+        grad_nodes_v=vmem(1, node_dev, width, kind=f32),
+        grad_edges_v=vmem(1, edge_dev, width, kind=f32),
+        write_sem=sems(3),
+        own_sem=sems(3),
+        mate_left=vmem(layers, edge_dev, width),
+        mate_left_send=sems(layers),
+        mate_left_recv=sems(layers),
+        mate_right=vmem(layers, edge_dev + vector_rows, width),
+        mate_right_send=sems(layers),
+        mate_right_recv=sems(layers),
+        pre_own=vmem(layers, edge_dev, width),
+        lift_own=vmem(layers, edge_dev + vector_rows, width),
+        parts=vmem(layers, sections, width + vector_rows, quarter),
+        parts_in=vmem(layers, sections, width + vector_rows, quarter),
+        parts_send=sems(layers, sections),
+        parts_recv=sems(layers, sections),
         node_lefts_own=vmem(layers, 3 * node_dev, width),
         node_lefts=vmem(layers, plane, 3 * node_dev, width),
         node_lefts_send=sems(layers, plane),
@@ -722,37 +832,32 @@
         sum_rights_recv=sems(layers, plane),
     )
     scratch = vars(blank)
-    lift_block = whole_tiles(width // shards) + vector_rows
     pair_groups = []
-    for block in (
-        whole_tiles(3 * width // shards),
-        lift_block,
-        whole_tiles(2 * width // shards) + lift_block,
-    ):
+    for block in blocks:
         pair_groups += [
             vmem(layers, pairs, 2, block, quarter),
             vmem(layers, pairs, 2, block, quarter),
             sems(layers, pairs),
             sems(layers, pairs),
             vmem(layers, 2, block, quarter),
-            vmem(layers, sections, block, quarter),
             sems(layers, plane),
             sems(layers, sections),
         ]
     weights_v = [pltpu.VMEM(weight.shape, weight.dtype) for weight in weights]
-    out_shape = list(outputs.values()) + weight_grads
-    ins = len(inputs) + len(weights)
-    outs = ins + len(out_shape)
-    plan = SimpleNamespace(
-        names=list(inputs)
+    ins, outs = len(inputs) + len(weights), len(outputs) + len(fulls)
+    names = (
+        list(inputs)
         + list(range(len(weights)))
         + list(outputs)
-        + list(range(len(weights)))
-        + list(scratch),
+        + list(range(len(fulls)))
+        + list(scratch)
+    )
+    plan = SimpleNamespace(
+        names=[str(name) for name in names],
         weights=len(inputs),
-        grads=ins + len(outputs),
-        pair_groups=outs + len(scratch),
-        weights_v=outs + len(scratch) + len(pair_groups),
+        fulls=ins + len(outputs),
+        pair_groups=ins + outs + len(scratch),
+        weights_v=ins + outs + len(scratch) + len(pair_groups),
         layers=layers,
         sections=sections,
         shards=shards,
@@ -760,22 +865,21 @@
         edge_dev=edge_dev,
         width=width,
     )
-    plan.names = [str(name) for name in plan.names]
     results = pl.pallas_call(
         functools.partial(kernel, plan),
-        out_shape=out_shape,
+        out_shape=list(outputs.values()) + fulls,
         in_specs=[pl.BlockSpec(memory_space=pltpu.HBM)] * ins,
-        out_specs=[pl.BlockSpec(memory_space=pltpu.VMEM)] * len(out_shape),
+        out_specs=[pl.BlockSpec(memory_space=pltpu.HBM)] * outs,
         scratch_shapes=list(scratch.values()) + pair_groups + weights_v,
         compiler_params=pltpu.CompilerParams(
             collective_id=0, has_side_effects=True, vmem_limit_bytes=60 << 20
         ),
     )(*inputs.values(), *weights)
     return pl.pallas_call(
-        functools.partial(copy_kernel, len(out_shape)),
-        out_shape=out_shape,
-        in_specs=[pl.BlockSpec(memory_space=pltpu.VMEM)] * len(out_shape),
-        out_specs=[pl.BlockSpec(memory_space=pltpu.VMEM)] * len(out_shape),
+        functools.partial(write_kernel, shards),
+        out_shape=list(outputs.values()) + weight_grads,
+        in_specs=[pl.BlockSpec(memory_space=pltpu.VMEM)] * outs,
+        out_specs=[pl.BlockSpec(memory_space=pltpu.VMEM)] * (len(outputs) + len(weight_grads)),
     )(*results)
 
 

time: 81 us -> 59.7 us (0.74)
  the two profiles are of different devices: /device:TPU:25 before, /device:TPU:0 now
where the time goes in v3:
time: 59.7 us; the launch traced here: 59.6 us
  Pallas kernels  58.9 us (99%)
  between operations  0.66 us (1%)
    pallas_call x1, Pallas kernels, fused(): pl.pallas_call(functools.partial(kernel, plan), out_shape=list(outputs.va...  56.2 us
    pallas_call x1, Pallas kernels, fused(): pl.pallas_call(functools.partial(write_kernel, shards), out_shape=list(ou...  2.7 us

profile of v3, /device:TPU:0, one launch (start us, length us, event | category | flops | bytes accessed | tf_op | source)
XLA Modules:
  0.0 59.6 jit_solution(2830131075631651085)
XLA Ops:
  0.7 56.2 %shard_map.289 = (bf16[1,16,512]{2,1,0:T(8,128)(2,1)}, f32[1,16,512]{2,1,0:T(8,128)}, f32[1,128,512]{2,1,0:T(8,128)}, bf16[2,4,192,128]{3,2,1,0:T(8,128)(2,1)}, ...) custom-call(bf16[4,16,512]{2,1,0:T(8,128)(2,1)} %refs_0_.1, bf16[4,128,512]{2,1,0:T(8,128)(2,1)} %refs_1_.1, ...), custom_call_target="tpu_custom_call" | custom-call | tf_op jit(solution)/shard_map/pallas_call | solution.py:868
  56.9 2.7 %shard_map.290 = (bf16[1,16,512]{2,1,0:T(8,128)(2,1)}, f32[1,16,512]{2,1,0:T(8,128)}, f32[1,128,512]{2,1,0:T(8,128)}, f32[2,192,512]{2,1,0:T(8,128)}, f32[2,64]{...) custom-call(bf16[1,16,512]{2,1,0:T(8,128)(2,1)} %get-tuple-element.2, ...), custom_call_target="tpu_custom_call" | custom-call | tf_op jit(solution)/shard_map/pallas_call | solution.py:878

commit v4 on v3

v4 whole, which is shorter than its diff:
```python
import functools
from types import SimpleNamespace

import jax
import jax.numpy as jnp
import numpy as np
from jax import lax
from jax.experimental import pallas as pl
from jax.experimental.pallas import tpu as pltpu
from jax.sharding import PartitionSpec as P

f32 = jnp.float32
bf16 = jnp.bfloat16
MESH = pl.DeviceIdType.MESH
norm_epsilon = 1e-05
vector_rows = 16
e_one, e_bias_one, e_two, e_bias_two, e_gain, e_shift = range(6)
n_one, n_bias_one, n_two, n_bias_two, n_gain, n_shift = range(6, 12)
matrix_kinds = (e_one, e_two, n_one, n_two)
vector_kinds = (e_bias_one, e_bias_two, e_gain, e_shift, n_bias_one, n_bias_two, n_gain, n_shift)
lanes = 128


def dot(left, right):
    return jnp.dot(left, right, preferred_element_type=f32)


def contract_rows(left, right):
    return lax.dot_general(left, right, (((0,), (0,)), ((), ())), preferred_element_type=f32)


def contract_cols(left, right):
    return lax.dot_general(left, right, (((1,), (1,)), ((), ())), preferred_element_type=f32)


def whole_tiles(rows):
    return -(-rows // 16) * 16


def layer_norm(lifted):
    center = lifted - jnp.mean(lifted, axis=-1, keepdims=True)
    scale = lax.rsqrt(jnp.mean(center * center, axis=-1, keepdims=True) + norm_epsilon)
    return center * scale, scale


def activate(pre):
    sigma = jax.nn.sigmoid(pre)
    return (pre * sigma).astype(bf16), sigma * (1.0 + pre * (1.0 - sigma))


def branch_back(grad_branch, gain_row, normed, scale):
    grad_normed = grad_branch * gain_row
    return (
        scale
        * (
            grad_normed
            - jnp.mean(grad_normed, axis=-1, keepdims=True)
            - normed * jnp.mean(grad_normed * normed, axis=-1, keepdims=True)
        )
    ).astype(bf16)


def column_sums(grad_pre, grad_lifted, grad_branch, normed):
    rows = [
        jnp.sum(grad_pre.astype(f32), axis=0, keepdims=True),
        jnp.sum(grad_lifted.astype(f32), axis=0, keepdims=True),
        jnp.sum(grad_branch * normed, axis=0, keepdims=True),
        jnp.sum(grad_branch, axis=0, keepdims=True),
    ]
    rows.append(jnp.zeros((vector_rows - 4, grad_branch.shape[1]), f32))
    return jnp.concatenate(rows, axis=0).astype(bf16)


def ended(buffer, sem):
    pltpu.make_async_copy(buffer, buffer, sem).wait()


def kernel(plan, *refs):
    v = SimpleNamespace(**dict(zip(plan.names, refs)))
    layers, sections, shards = plan.layers, plan.sections, plan.shards
    node_dev, edge_dev, width = plan.node_dev, plan.edge_dev, plan.width
    quarter, pairs, plane = width // sections, shards // 2, 2 * sections
    nodes_total = shards * node_dev
    three_rows, two_rows, one_rows = (part * width // shards for part in (3, 2, 1))
    weights = refs[plan.weights : plan.weights + 12]
    section, row = lax.axis_index("section"), lax.axis_index("rows")
    pair, core = row // 2, row % 2
    plane_slot = section * 2 + core
    edge_pairs, lift_pairs, node_pairs = (
        SimpleNamespace(
            full=refs[plan.fulls + place],
            **dict(zip(plan.pair_names, refs[plan.pair_groups + 5 * place :])),
        )
        for place in range(3)
    )
    node_lefts = SimpleNamespace(data=v.node_lefts, recv=v.node_lefts_recv)
    node_rights = SimpleNamespace(data=v.node_rights, recv=v.node_rights_recv)
    sum_rights = SimpleNamespace(data=v.sum_rights, recv=v.sum_rights_recv)

    def drained(count, sem):
        ended(v.drain.at[pl.ds(0, count // lanes)], sem)

    started = SimpleNamespace(total=[0, 0], cores=(0, 1), times=1)

    def count_start(source):
        for one in started.cores:
            started.total[one] += started.times * source.size * source.dtype.itemsize // 2

    def send(source, target, recv_sem, device):
        count_start(source)
        pltpu.make_async_remote_copy(
            src_ref=source,
            dst_ref=target,
            send_sem=v.done,
            recv_sem=recv_sem,
            device_id=device,
            device_id_type=MESH,
        ).start()

    def write(source, target):
        count_start(source)
        pltpu.make_async_copy(source, target, v.done).start()

    def on_core(one, act):
        before = started.cores
        started.cores = tuple(x for x in before if x == one)
        pl.when(core == one)(act)
        started.cores = before

    def each(count, visit):
        if count <= 8:
            for i in range(count):
                visit(i)
        else:
            before = started.times

            def step(i, carry):
                started.times = before * count
                visit(i)
                started.times = before
                return carry

            lax.fori_loop(0, count, step, 0)

    barrier = pltpu.get_barrier_semaphore()

    def greet(device):
        pl.semaphore_signal(barrier, inc=1, device_id=device, device_id_type=MESH)

    each(shards - 1, lambda i: greet((section, (row + 1 + i) % shards)))
    for step in range(1, sections):
        for other in range(2):
            greet(((section + step) % sections, pair * 2 + other))

    def peer_rows(visit):
        each(shards - 1, lambda i: visit((row + 1 + i) % shards))

    def send_nodes(layer, source):
        def one(peer):
            send(source, v.nodes.at[layer, row], v.nodes_recv.at[layer], (section, peer))

        peer_rows(one)

    def send_sums(layer):
        def one(peer):
            send(
                v.sums.at[layer, peer],
                v.sums_in.at[layer, row],
                v.sums_recv.at[layer],
                (section, peer),
            )

        peer_rows(one)

    def from_rows(data, sem, layer):
        ended(data.at[layer, pl.ds(0, shards - 1)], sem.at[layer])

    def to_plane(group, layer, sources):
        def one(target_section, other):
            source = sources[other](target_section)
            send(
                source,
                group.data.at[layer, plane_slot, pl.ds(0, source.shape[0])],
                group.recv.at[layer],
                (target_section, pair * 2 + other),
            )

        def keep(other):
            source = sources[other](section)
            group.data[layer, plane_slot, 0 : source.shape[0]] = source[...]

        for other in range(2):
            if sources[other] is not None:
                for step in range(1, sections):
                    one((section + step) % sections, other)
                on_core(1 - other, functools.partial(one, section, other))
                on_core(other, functools.partial(keep, other))

    def from_plane(group, layer, rows):
        drained((plane - 1) * rows * group.data.shape[-1], group.recv.at[layer])

    def to_mate(taker, target, recv_sem, source):
        target = target.at[pl.ds(0, source.shape[0])]
        mate = (section, row + 1 - 2 * core)
        on_core(1 - taker, lambda: send(source, target, recv_sem, mate))

    def send_parts(layer, rows):
        for step in range(1, sections):
            target = (section + step) % sections
            send(
                v.parts.at[layer, target, pl.ds(0, rows)],
                v.parts_in.at[layer, section, pl.ds(0, rows)],
                v.parts_recv.at[layer],
                (target, row),
            )

    def send_pairs(group, layer, relay):
        def one(peer):
            send(
                group.own.at[layer, peer],
                group.come.at[layer, pair],
                group.recv.at[0, layer],
                (section, peer * 2 + core),
            )

        if not relay:
            each(pairs - 1, lambda i: one((pair + 1 + i) % pairs))
            return
        mirror = pairs - 1 - pair

        @pl.when(pair % 3 == 0)
        def _():
            near = (pair + 3) // 3
            send(
                group.own.at[layer, mirror],
                group.relay.at[layer],
                group.recv.at[2, layer],
                (section, near * 2 + core),
            )
            one(near)
            one(3 - near)

        before, started.cores = started.cores, ()

        @pl.when(pair % 3 != 0)
        def _():
            beyond = 3 * (pair - 1)
            one(beyond)
            one(mirror)
            far = 3 - beyond
            ended(group.relay.at[layer], group.recv.at[2, layer])
            group.own[layer, far] = (
                group.own[layer, far].astype(f32) + group.relay[layer].astype(f32)
            ).astype(bf16)
            one(far)

        started.cores = before

    def add_pairs(group, layer, relay):
        def add(peers):
            ended(group.come.at[layer, pl.ds(0, len(peers))], group.recv.at[0, layer])
            total = group.own[layer, pair].astype(f32)
            for peer in peers:
                total = total + group.come[layer, peer].astype(f32)
            group.total[layer] = total.astype(bf16)

        if relay:
            pl.when(pair % 3 == 0)(lambda: add([1, 2]))
            pl.when(pair % 3 != 0)(lambda: add([(pair + step) % 4 for step in (1, 2, 3)]))
        else:
            add([(pair + step) % pairs for step in range(1, pairs)])

        def share(target_section, other):
            send(
                group.total.at[layer, other],
                group.full.at[layer, section],
                group.recv.at[1, layer],
                (target_section, pair * 2 + other),
            )

        for step in range(1, sections):
            for other in range(2):
                share((section + step) % sections, other)
        share(section, 1 - core)
        write(group.total.at[layer, core], group.full.at[layer, section])

    def from_givers(group, layer, giver):
        def wait(other):
            slots = sections - 1 if other == giver else sections
            ended(group.full.at[layer, pl.ds(0, slots)], group.recv.at[1, layer])

        for other in range(2):
            on_core(other, functools.partial(wait, other))

    def store_blocks(target, product, offset, rows):
        padded = whole_tiles(rows)
        for owner in range(shards):
            block = product[owner * rows : (owner + 1) * rows]
            if padded != rows:
                block = jnp.concatenate([block, jnp.zeros((padded - rows, quarter), f32)], axis=0)
            target[owner // 2, owner % 2, offset : offset + padded] = block.astype(bf16)

    def store_vectors(target, total, offset):
        for owner in range(shards):
            target[owner // 2, owner % 2, offset : offset + vector_rows] = total.astype(bf16)

    def quarters(target, offset, value):
        rows = value.shape[0]
        for part in range(sections):
            target[part, offset : offset + rows] = value[
                :, part * quarter : (part + 1) * quarter
            ].astype(bf16)

    def vector(kind, layer):
        return v.vectors[vector_kinds.index(kind)].astype(f32)[layer : layer + 1]

    pl.semaphore_wait(barrier, shards - 1 + 2 * (sections - 1))
    send_nodes(0, v.node_features.at[section])

    def load(source, target, sem):
        pltpu.make_async_copy(source, target, v.load_sem.at[sem]).start()

    def load_matrix(kind, layer, sem):
        rows = weights[kind].shape[1]
        target = v.matrices.at[layer, pl.ds(plan.start[kind], rows)]
        load(weights[kind].at[layer], target, sem)

    def matrix(kind, layer, first=0, count=None):
        rows = weights[kind].shape[1] if count is None else count * width
        start = plan.start[kind] + first * width
        return v.matrices[layer, start : start + rows]

    def loaded(target, sem):
        ended(target, v.load_sem.at[sem])

    load(v.node_features.at[section], v.nodes.at[0, row], 0)
    load(v.edge_features.at[section], v.edge_in.at[0], 1)
    load_matrix(e_one, 0, 2)
    for place, source in enumerate((v.owner, v.local, v.receivers)):
        load(source.at[section], v.index.at[place], 3 + place)
    for place, kind in enumerate(vector_kinds):
        load(weights[kind], v.vectors.at[place], 6 + place)
    for kind in (e_two, n_one, n_two):
        load_matrix(kind, 0, 14)
    for layer in range(1, layers):
        for kind in matrix_kinds:
            load_matrix(kind, layer, 14 + layer)
    load(v.cotangent.at[section], v.cotangent_v, 14 + layers)

    loaded(v.nodes.at[0, row], 0)
    loaded(v.edge_in.at[0], 1)
    to_mate(0, v.mate_left.at[0], v.mate_recv.at[0], v.edge_in.at[0])

    for place in range(3):
        loaded(v.index.at[place], 3 + place)
    sender_row, target_row = v.index[0] * node_dev + v.index[1], v.index[2]
    eye = lax.broadcasted_iota(jnp.int32, (edge_dev, edge_dev), 0) == lax.broadcasted_iota(
        jnp.int32, (edge_dev, edge_dev), 1
    )

    def to_column(values):
        spread = jnp.broadcast_to(values, (edge_dev, edge_dev))
        column = jnp.sum(jnp.where(eye, spread, 0).astype(f32), axis=1, keepdims=True)
        return column.astype(jnp.int32)

    def one_hot(values, count, axis):
        places = (count, edge_dev) if axis == 0 else (edge_dev, count)
        match = lax.broadcasted_iota(jnp.int32, places, axis) == values
        return jnp.where(match, 1.0, 0.0).astype(bf16)

    v.from_nodes[...] = one_hot(to_column(sender_row), nodes_total, 1)
    v.to_nodes[...] = one_hot(sender_row, nodes_total, 0)
    v.from_targets[...] = one_hot(to_column(target_row), node_dev, 1)
    v.to_targets[...] = one_hot(target_row, node_dev, 0)
    for place in range(len(vector_kinds)):
        loaded(v.vectors.at[place], 6 + place)

    def edge_forward(layer):
        node = v.nodes[layer, row]
        edge = v.edge_in[layer]
        if layer == 0:
            loaded(v.matrices.at[0, pl.ds(0, 3 * width)], 2)
        else:
            loaded(v.matrices.at[layer], 14 + layer)
        received = dot(v.from_targets[...], node).astype(bf16)
        v.work[...] = (
            dot(edge, matrix(e_one, layer, 0, 1))
            + dot(received, matrix(e_one, layer, 2, 1))
            + vector(e_bias_one, layer)
        )
        from_rows(v.nodes, v.nodes_recv, layer)
        sent = dot(v.from_nodes[...], v.nodes[layer].reshape(nodes_total, width)).astype(bf16)
        hidden, slope = activate(
            v.work[...] + dot(sent, matrix(e_one, layer, 1, 1))
        )
        v.edge_hidden[layer] = hidden
        v.edge_slope[layer] = slope
        to_mate(1, v.mate_left.at[layer], v.mate_recv.at[layer], v.edge_hidden.at[layer])
        if layer == 0:
            loaded(v.matrices.at[0, pl.ds(3 * width, v.matrices.shape[1] - 3 * width)], 14)
        normed, scale = layer_norm(
            dot(hidden, matrix(e_two, layer)) + vector(e_bias_two, layer)
        )
        v.edge_normed[layer] = normed
        v.edge_scale[layer] = scale
        edge = (
            edge.astype(f32)
            + (normed * vector(e_gain, layer) + vector(e_shift, layer))
        ).astype(bf16)
        if layer + 1 < layers:
            v.edge_in[layer + 1] = edge
            to_mate(
                0, v.mate_left.at[layer + 1], v.mate_recv.at[layer + 1], v.edge_in.at[layer + 1]
            )
        return node, dot(v.to_targets[...], edge).astype(bf16)

    def node_forward(layer, node, gathered):
        hidden, slope = activate(
            dot(node, matrix(n_one, layer, 0, 1))
            + dot(gathered, matrix(n_one, layer, 1, 1))
            + vector(n_bias_one, layer)
        )
        v.node_slope[layer] = slope
        normed, scale = layer_norm(
            dot(hidden, matrix(n_two, layer)) + vector(n_bias_two, layer)
        )
        v.node_normed[layer] = normed
        v.node_scale[layer] = scale
        new_node = (
            node.astype(f32)
            + (normed * vector(n_gain, layer) + vector(n_shift, layer))
        ).astype(bf16)
        if layer + 1 < layers:
            v.nodes[layer + 1, row] = new_node
            send_nodes(layer + 1, v.nodes.at[layer + 1, row])
        else:
            v.final_v[0] = new_node
            write(v.final_v, v.final)
        v.node_lefts_own[layer, 0:node_dev] = node
        v.node_lefts_own[layer, node_dev : 2 * node_dev] = gathered
        v.node_lefts_own[layer, 2 * node_dev : 3 * node_dev] = hidden
        to_plane(
            node_lefts,
            layer,
            (
                lambda s: v.node_lefts_own.at[layer, pl.ds(0, node_dev)],
                lambda s: v.node_lefts_own.at[layer],
            ),
        )

    for layer in range(layers):
        node, gathered = edge_forward(layer)
        node_forward(layer, node, gathered)

    def node_products(layer, relay):
        def act():
            from_plane(node_lefts, layer, 3 * node_dev)
            from_plane(node_rights, layer, 2 * node_dev + vector_rows)
            own = plane * node_dev
            state = v.node_lefts[layer, :, 0:node_dev].reshape(own, width)
            gathered = v.node_lefts[layer, :, node_dev : 2 * node_dev].reshape(own, width)
            hidden = v.node_lefts[layer, :, 2 * node_dev : 3 * node_dev].reshape(own, width)
            grad_pre = v.node_rights[layer, :, 0:node_dev].reshape(own, quarter)
            grad_lifted = v.node_rights[layer, :, node_dev : 2 * node_dev].reshape(own, quarter)
            vectors = v.node_rights[layer, :, 2 * node_dev : 2 * node_dev + vector_rows]
            v.product[0:width] = contract_rows(state, grad_pre)
            v.product[width : 2 * width] = contract_rows(gathered, grad_pre)
            v.product[2 * width : 3 * width] = contract_rows(hidden, grad_lifted)
            target = node_pairs.own.at[layer]
            store_blocks(target, v.product, 0, two_rows)
            start = whole_tiles(two_rows)
            store_blocks(target, v.product.at[pl.ds(2 * width, width)], start, one_rows)
            start += whole_tiles(one_rows)
            store_vectors(target, jnp.sum(vectors.astype(f32), axis=0), start)
            send_pairs(node_pairs, layer, relay)

        on_core(1, act)

    def edge_parts(layer):
        def multiply(own_left, own_right):
            left = jnp.concatenate([own_left[layer], v.mate_left[layer]], axis=0)
            right = jnp.concatenate(
                [own_right[layer, 0:edge_dev], v.mate_right[layer, 0:edge_dev]], axis=0
            )
            for part in range(sections):
                columns = slice(part * quarter, (part + 1) * quarter)
                v.parts[layer, part, 0:width] = contract_rows(left, right[:, columns]).astype(bf16)

        def act_one():
            drained(2 * edge_dev * width, v.mate_recv.at[layer])
            multiply(v.edge_in, v.pre_own)
            send_parts(layer, width)

        def act_two():
            drained((2 * edge_dev + vector_rows) * width, v.mate_recv.at[layer])
            multiply(v.edge_hidden, v.lift_own)
            vectors = (
                v.lift_own[layer, edge_dev : edge_dev + vector_rows].astype(f32)
                + v.mate_right[layer, edge_dev : edge_dev + vector_rows].astype(f32)
            ).astype(bf16)
            for part in range(sections):
                v.parts[layer, part, width : width + vector_rows] = vectors[
                    :, part * quarter : (part + 1) * quarter
                ]
            send_parts(layer, width + vector_rows)

        on_core(0, act_one)
        on_core(1, act_two)

    def from_parts(layer, rows):
        drained((sections - 1) * rows * quarter, v.parts_recv.at[layer])

    def add_parts(layer, start, rows):
        total = v.parts[layer, section, start : start + rows].astype(f32)
        for step in range(1, sections):
            other = (section + step) % sections
            total = total + v.parts_in[layer, other, start : start + rows].astype(f32)
        return total

    def edge_products(layer, relay):
        def act_one():
            from_plane(node_lefts, layer, node_dev)
            from_plane(sum_rights, layer, 2 * node_dev)
            own = plane * node_dev
            state = v.node_lefts[layer, :, 0:node_dev].reshape(own, width)
            for part in range(2):
                start = part * node_dev
                v.product[(1 + part) * width : (2 + part) * width] = contract_rows(
                    state, v.sum_rights[layer, :, start : start + node_dev].reshape(own, quarter)
                )
            from_parts(layer, width)
            v.product[0:width] = add_parts(layer, 0, width)
            store_blocks(edge_pairs.own.at[layer], v.product, 0, three_rows)
            send_pairs(edge_pairs, layer, relay)

        def act_two():
            from_parts(layer, width + vector_rows)
            v.product[0:width] = add_parts(layer, 0, width)
            target = lift_pairs.own.at[layer]
            store_blocks(target, v.product, 0, one_rows)
            store_vectors(target, add_parts(layer, width, vector_rows), whole_tiles(one_rows))
            send_pairs(lift_pairs, layer, relay)

        on_core(0, act_one)
        on_core(1, act_two)

    def add_node_products(layer, relay):
        on_core(1, lambda: add_pairs(node_pairs, layer, relay))

    def add_edge_products(layer, relay):
        on_core(0, lambda: add_pairs(edge_pairs, layer, relay))
        on_core(1, lambda: add_pairs(lift_pairs, layer, relay))

    def node_backward(layer):
        grad_branch = v.grad_node[...]
        normed = v.node_normed[layer]
        grad_lifted = branch_back(
            grad_branch, vector(n_gain, layer), normed, v.node_scale[layer]
        )
        grad_hidden = contract_cols(grad_lifted, matrix(n_two, layer))
        grad_pre = (grad_hidden * v.node_slope[layer]).astype(bf16)
        aggregate = contract_cols(grad_pre, matrix(n_one, layer, 1, 1))
        high = aggregate.astype(bf16)
        low = (aggregate - high.astype(f32)).astype(bf16)
        grad_edge = dot(v.from_targets[...], high) + dot(v.from_targets[...], low)
        if layer + 1 < layers:
            grad_edge = grad_edge + v.grad_edge[...]
        v.grad_edge[...] = grad_edge.astype(bf16).astype(f32)
        grad_node = grad_branch + contract_cols(grad_pre, matrix(n_one, layer, 0, 1))
        v.grad_node[...] = grad_node.astype(bf16).astype(f32)
        target = v.node_rights_own.at[layer]
        quarters(target, 0, grad_pre)
        quarters(target, node_dev, grad_lifted)
        quarters(target, 2 * node_dev, column_sums(grad_pre, grad_lifted, grad_branch, normed))
        to_plane(node_rights, layer, (None, lambda s: v.node_rights_own.at[layer, s]))

    def edge_backward(layer):
        grad_branch = v.grad_edge[...]
        normed = v.edge_normed[layer]
        grad_lifted = branch_back(
            grad_branch, vector(e_gain, layer), normed, v.edge_scale[layer]
        )
        grad_hidden = contract_cols(grad_lifted, matrix(e_two, layer))
        grad_pre = (grad_hidden * v.edge_slope[layer]).astype(bf16)
        sums = dot(v.to_nodes[...], grad_pre).astype(bf16)
        v.sums[layer] = sums.reshape(shards, node_dev, width)
        send_sums(layer)
        v.pre_own[layer] = grad_pre
        v.lift_own[layer, 0:edge_dev] = grad_lifted
        v.lift_own[layer, edge_dev : edge_dev + vector_rows] = column_sums(
            grad_pre, grad_lifted, grad_branch, normed
        )
        to_mate(0, v.mate_right.at[layer], v.mate_recv.at[layer], v.pre_own.at[layer])
        to_mate(1, v.mate_right.at[layer], v.mate_recv.at[layer], v.lift_own.at[layer])
        grad_edge = grad_branch + contract_cols(grad_pre, matrix(e_one, layer, 0, 1))
        by_target = dot(v.to_targets[...], grad_pre).astype(bf16)
        v.grad_node[...] = v.grad_node[...] + contract_cols(
            by_target, matrix(e_one, layer, 2, 1)
        )
        if layer > 0:
            v.grad_edge[...] = grad_edge.astype(bf16).astype(f32)
        else:
            v.grad_edges_v[0] = grad_edge
            write(v.grad_edges_v, v.grad_edges)
        return by_target

    def sender_backward(layer, by_target):
        from_rows(v.sums_in, v.sums_recv, layer)
        v.sums_in[layer, row] = v.sums[layer, row]
        by_sender = jnp.sum(v.sums_in[layer].astype(f32), axis=0).astype(bf16)
        target = v.sum_rights_own.at[layer]
        quarters(target, 0, by_sender)
        quarters(target, node_dev, by_target)
        to_plane(sum_rights, layer, (lambda s: v.sum_rights_own.at[layer, s], None))
        grad_node = v.grad_node[...] + contract_cols(
            by_sender, matrix(e_one, layer, 1, 1)
        )
        if layer > 0:
            v.grad_node[...] = grad_node.astype(bf16).astype(f32)
        else:
            v.grad_nodes_v[0] = grad_node
            write(v.grad_nodes_v, v.grad_nodes)

    loaded(v.cotangent_v, 14 + layers)
    v.grad_node[...] = v.cotangent_v[...].astype(f32)
    relay = pairs == 4
    for layer in reversed(range(layers)):
        node_backward(layer)
        by_target = edge_backward(layer)
        edge_parts(layer)
        node_products(layer, False)
        sender_backward(layer, by_target)
    edge_products(1, relay)
    add_node_products(1, False)
    edge_products(0, relay)
    add_edge_products(1, relay)
    add_node_products(0, False)
    add_edge_products(0, relay)

    for layer in range(layers):
        from_givers(edge_pairs, layer, 0)
        from_givers(lift_pairs, layer, 1)
        from_givers(node_pairs, layer, 1)
    for one in range(2):
        pl.when(core == one)(
            lambda: drained(started.total[one], v.done)
        )


def write_kernel(shards, *refs):
    final, grad_nodes, grad_edges, edge_full, lift_full, node_full = refs[:6]
    out_final, out_nodes, out_edges = refs[6:9]
    grads = refs[9:]
    row = lax.axis_index("rows")
    layers, sections, quarter = edge_full.shape[0], edge_full.shape[1], edge_full.shape[3]
    width = sections * quarter
    three_rows, two_rows, one_rows = (part * width // shards for part in (3, 2, 1))
    node_start = whole_tiles(two_rows)
    out_final[...] = final[...]
    out_nodes[...] = grad_nodes[...]
    out_edges[...] = grad_edges[...]

    def put(target, full, start, rows):
        for layer in range(layers):
            for part in range(sections):
                value = full[layer, part, start : start + whole_tiles(rows)]
                target[layer, :, part * quarter : (part + 1) * quarter] = value.astype(f32)[0:rows]

    put(grads[e_one], edge_full, 0, three_rows)
    put(grads[e_two], lift_full, 0, one_rows)
    put(grads[n_one], node_full, 0, two_rows)
    put(grads[n_two], node_full, node_start, one_rows)

    def take_columns(value):
        per = quarter // one_rows
        taken = jnp.zeros((vector_rows, one_rows), f32)
        for place in range(per):
            taken = taken + jnp.where(
                row % per == place, value[:, place * one_rows : (place + 1) * one_rows], 0.0
            )
        return taken

    holder = row // (quarter // one_rows)
    for layer in range(layers):
        for kinds, full, start in (
            (vector_kinds[:4], lift_full, whole_tiles(one_rows)),
            (vector_kinds[4:], node_full, node_start + whole_tiles(one_rows)),
        ):
            vectors = take_columns(full[layer, holder, start : start + vector_rows].astype(f32))
            for place, kind in enumerate(kinds):
                grads[kind][layer : layer + 1] = vectors[place : place + 1]


def fused(sections, shards, node_features, edge_features, owner, local, receivers, cotangent, *weights):
    micro_count, node_dev, width = node_features.shape
    edge_dev = edge_features.shape[1]
    layers = weights[0].shape[0]
    quarter, pairs, plane = width // sections, shards // 2, 2 * sections
    nodes_total = shards * node_dev

    def shape(*dims, kind=f32):
        return jax.ShapeDtypeStruct(dims, kind)

    def vmem(*dims, kind=bf16):
        return pltpu.VMEM(dims, kind)

    def sems(*dims):
        return pltpu.SemaphoreType.DMA(dims)

    inputs = dict(
        node_features=node_features,
        edge_features=edge_features,
        owner=owner,
        local=local,
        receivers=receivers,
        cotangent=cotangent,
    )
    outputs = dict(
        final=shape(1, node_dev, width, kind=bf16),
        grad_nodes=shape(1, node_dev, width),
        grad_edges=shape(1, edge_dev, width),
    )
    weight_grads = [
        shape(layers, weight.shape[1] // shards, *weight.shape[2:]) for weight in weights
    ]
    lift_block = whole_tiles(width // shards) + vector_rows
    blocks = (
        whole_tiles(3 * width // shards),
        lift_block,
        whole_tiles(2 * width // shards) + lift_block,
    )
    fulls = [shape(layers, sections, block, quarter, kind=bf16) for block in blocks]
    starts = np.cumsum([0] + [weights[kind].shape[1] for kind in matrix_kinds])
    scratch = dict(
        done=pltpu.SemaphoreType.DMA,
        drain=vmem(1024 * (24 + shards // 2), lanes),
        load_sem=sems(15 + layers),
        index=vmem(3, 1, edge_dev, kind=jnp.int32),
        vectors=vmem(len(vector_kinds), layers, width),
        matrices=vmem(layers, int(starts[-1]), width),
        cotangent_v=vmem(node_dev, width),
        from_nodes=vmem(edge_dev, nodes_total),
        to_nodes=vmem(nodes_total, edge_dev),
        from_targets=vmem(edge_dev, node_dev),
        to_targets=vmem(node_dev, edge_dev),
        work=vmem(edge_dev, width, kind=f32),
        grad_node=vmem(node_dev, width, kind=f32),
        grad_edge=vmem(edge_dev, width, kind=f32),
        product=vmem(3 * width, quarter, kind=f32),
        edge_in=vmem(layers, edge_dev, width),
        edge_hidden=vmem(layers, edge_dev, width),
        edge_slope=vmem(layers, edge_dev, width, kind=f32),
        edge_normed=vmem(layers, edge_dev, width, kind=f32),
        edge_scale=vmem(layers, edge_dev, 1, kind=f32),
        node_slope=vmem(layers, node_dev, width, kind=f32),
        node_normed=vmem(layers, node_dev, width, kind=f32),
        node_scale=vmem(layers, node_dev, 1, kind=f32),
        nodes=vmem(layers, shards, node_dev, width),
        nodes_recv=sems(layers),
        sums=vmem(layers, shards, node_dev, width),
        sums_in=vmem(layers, shards, node_dev, width),
        sums_recv=sems(layers),
        final_v=vmem(1, node_dev, width),
        grad_nodes_v=vmem(1, node_dev, width, kind=f32),
        grad_edges_v=vmem(1, edge_dev, width, kind=f32),
        mate_left=vmem(layers, edge_dev, width),
        mate_right=vmem(layers, edge_dev + vector_rows, width),
        mate_recv=sems(layers),
        pre_own=vmem(layers, edge_dev, width),
        lift_own=vmem(layers, edge_dev + vector_rows, width),
        parts=vmem(layers, sections, width + vector_rows, quarter),
        parts_in=vmem(layers, sections, width + vector_rows, quarter),
        parts_recv=sems(layers),
        node_lefts_own=vmem(layers, 3 * node_dev, width),
        node_lefts=vmem(layers, plane, 3 * node_dev, width),
        node_lefts_recv=sems(layers),
        node_rights_own=vmem(layers, sections, 2 * node_dev + vector_rows, quarter),
        node_rights=vmem(layers, plane, 2 * node_dev + vector_rows, quarter),
        node_rights_recv=sems(layers),
        sum_rights_own=vmem(layers, sections, 2 * node_dev, quarter),
        sum_rights=vmem(layers, plane, 2 * node_dev, quarter),
        sum_rights_recv=sems(layers),
    )
    pair_groups = []
    for block in blocks:
        group = dict(
            own=vmem(layers, pairs, 2, block, quarter),
            come=vmem(layers, pairs, 2, block, quarter),
            total=vmem(layers, 2, block, quarter),
            relay=vmem(layers, 2, block, quarter),
            recv=sems(3, layers),
        )
        pair_groups += group.values()
    ins, outs = len(inputs) + len(weights), len(outputs) + len(fulls)
    names = (
        list(inputs)
        + list(range(len(weights)))
        + list(outputs)
        + list(range(len(fulls)))
        + list(scratch)
    )
    plan = SimpleNamespace(
        names=[str(name) for name in names],
        weights=len(inputs),
        fulls=ins + len(outputs),
        pair_groups=ins + outs + len(scratch),
        pair_names=list(group),
        start=dict(zip(matrix_kinds, map(int, starts))),
        layers=layers,
        sections=sections,
        shards=shards,
        node_dev=node_dev,
        edge_dev=edge_dev,
        width=width,
    )
    results = pl.pallas_call(
        functools.partial(kernel, plan),
        out_shape=list(outputs.values()) + fulls,
        in_specs=[pl.BlockSpec(memory_space=pltpu.HBM)] * ins,
        out_specs=[pl.BlockSpec(memory_space=pltpu.HBM)] * outs,
        scratch_shapes=list(scratch.values()) + pair_groups,
        compiler_params=pltpu.CompilerParams(
            collective_id=0, has_side_effects=True, vmem_limit_bytes=60 << 20
        ),
    )(*inputs.values(), *weights)
    return pl.pallas_call(
        functools.partial(write_kernel, shards),
        out_shape=list(outputs.values()) + weight_grads,
        in_specs=[pl.BlockSpec(memory_space=pltpu.VMEM)] * outs,
        out_specs=[pl.BlockSpec(memory_space=pltpu.VMEM)] * (len(outputs) + len(weight_grads)),
    )(*results)


def solution(mesh):
    sections, shards = mesh.shape["section"], mesh.shape["rows"]

    def body(node_features, edge_features, owner, *rest):
        owner = owner.reshape(owner.shape[:-1])
        return fused(sections, shards, node_features, edge_features, owner, *rest)

    in_specs = (
        P(None, "rows", None),
        P(None, "rows", None),
        P(None, "rows", None, None),
        P(None, "rows", None),
        P(None, "rows", None),
        P(None, "rows", None),
    ) + (P(),) * 12
    state = P("section", "rows", None)
    matrix, vector = P(None, "rows", None), P(None, "rows")
    out_specs = (state,) * 3 + (matrix, vector, matrix, vector, vector, vector) * 2
    return jax.shard_map(body, mesh=mesh, in_specs=in_specs, out_specs=out_specs, check_vma=False)
```

time: 59.7 us -> 55.4 us (0.928)
  Pallas kernels: 58.9 us -> 54.5 us
    pallas_call x1, Pallas kernels: 56.2 us -> 51.8 us  [fused(): pl.pallas_call(functools.partial(kernel, plan), out_shape=list(outputs.va...]
where the time goes in v4:
time: 55.4 us; the launch traced here: 55.2 us
  Pallas kernels  54.5 us (98%)
  between operations  0.66 us (1%)
    pallas_call x1, Pallas kernels, fused(): pl.pallas_call(functools.partial(kernel, plan), out_shape=list(outputs.va...  51.8 us
    pallas_call x1, Pallas kernels, fused(): pl.pallas_call(functools.partial(write_kernel, shards), out_shape=list(ou...  2.7 us

profile of v4, /device:TPU:0, one launch (start us, length us, event | category | flops | bytes accessed | tf_op | source)
XLA Modules:
  0.0 55.2 jit_solution(2814522798743877602)
XLA Ops:
  0.7 51.8 %shard_map.289 = (bf16[1,16,512]{2,1,0:T(8,128)(2,1)}, f32[1,16,512]{2,1,0:T(8,128)}, f32[1,128,512]{2,1,0:T(8,128)}, bf16[2,4,192,128]{3,2,1,0:T(8,128)(2,1)}, ...) custom-call(bf16[4,16,512]{2,1,0:T(8,128)(2,1)} %refs_0_.1, bf16[4,128,512]{2,1,0:T(8,128)(2,1)} %refs_1_.1, ...), custom_call_target="tpu_custom_call" | custom-call | tf_op jit(solution)/shard_map/pallas_call | solution.py:816
  52.5 2.7 %shard_map.290 = (bf16[1,16,512]{2,1,0:T(8,128)(2,1)}, f32[1,16,512]{2,1,0:T(8,128)}, f32[1,128,512]{2,1,0:T(8,128)}, f32[2,192,512]{2,1,0:T(8,128)}, f32[2,64]{...) custom-call(bf16[1,16,512]{2,1,0:T(8,128)(2,1)} %get-tuple-element.2, ...), custom_call_target="tpu_custom_call" | custom-call | tf_op jit(solution)/shard_map/pallas_call | solution.py:826

commit v5 on v4

--- a/solution.py
+++ b/solution.py
@@ -60,14 +60,15 @@
     ).astype(bf16)
 
 
-def column_sums(grad_pre, grad_lifted, grad_branch, normed):
+def column_sums(grad_pre, grad_lifted, grad_branch, normed, first):
     rows = [
         jnp.sum(grad_pre.astype(f32), axis=0, keepdims=True),
         jnp.sum(grad_lifted.astype(f32), axis=0, keepdims=True),
         jnp.sum(grad_branch * normed, axis=0, keepdims=True),
         jnp.sum(grad_branch, axis=0, keepdims=True),
     ]
-    rows.append(jnp.zeros((vector_rows - 4, grad_branch.shape[1]), f32))
+    zeros = jnp.zeros((vector_rows, grad_branch.shape[1]), f32)
+    rows = ([zeros[:first]] if first else []) + rows + [zeros[first + 4 :]]
     return jnp.concatenate(rows, axis=0).astype(bf16)
 
 
@@ -85,7 +86,7 @@
     weights = refs[plan.weights : plan.weights + 12]
     section, row = lax.axis_index("section"), lax.axis_index("rows")
     pair, core = row // 2, row % 2
-    plane_slot = section * 2 + core
+    plane_slot = core * sections + section
     edge_pairs, lift_pairs, node_pairs = (
         SimpleNamespace(
             full=refs[plan.fulls + place],
@@ -93,6 +94,7 @@
         )
         for place in range(3)
     )
+    rights = SimpleNamespace(data=v.rights, recv=v.rights_recv)
     node_lefts = SimpleNamespace(data=v.node_lefts, recv=v.node_lefts_recv)
     node_rights = SimpleNamespace(data=v.node_rights, recv=v.node_rights_recv)
     sum_rights = SimpleNamespace(data=v.sum_rights, recv=v.sum_rights_recv)
@@ -153,7 +155,13 @@
             greet(((section + step) % sections, pair * 2 + other))
 
     def peer_rows(visit):
-        each(shards - 1, lambda i: visit((row + 1 + i) % shards))
+        if pairs == 4:
+            for peer in (3 - pair, (pair + 2) % 4, pair + 1 - 2 * (pair % 2)):
+                visit(2 * peer + core)
+                visit(2 * peer + 1 - core)
+            visit(row + 1 - 2 * core)
+        else:
+            each(shards - 1, lambda i: visit((row + 1 + i) % shards))
 
     def send_nodes(layer, source):
         def one(peer):
@@ -162,15 +170,26 @@
         peer_rows(one)
 
     def send_sums(layer):
+        ended(v.mate_sums.at[layer], v.mate_sums_recv.at[layer])
+        both = v.sums[layer, core].astype(f32) + v.mate_sums[layer].astype(f32)
+        v.both_sums[layer] = both.astype(bf16)
+
         def one(peer):
             send(
-                v.sums.at[layer, peer],
-                v.sums_in.at[layer, row],
+                v.both_sums.at[layer, peer],
+                v.sums_in.at[layer, pair],
                 v.sums_recv.at[layer],
-                (section, peer),
-            )
-
-        peer_rows(one)
+                (section, peer * 2 + core),
+            )
+
+        peer_pairs(one)
+
+    def peer_pairs(visit):
+        if pairs == 4:
+            for peer in (3 - pair, (pair + 2) % 4, pair + 1 - 2 * (pair % 2)):
+                visit(peer)
+        else:
+            each(pairs - 1, lambda i: visit((pair + 1 + i) % pairs))
 
     def from_rows(data, sem, layer):
         ended(data.at[layer, pl.ds(0, shards - 1)], sem.at[layer])
@@ -224,7 +243,7 @@
             )
 
         if not relay:
-            each(pairs - 1, lambda i: one((pair + 1 + i) % pairs))
+            peer_pairs(one)
             return
         mirror = pairs - 1 - pair
 
@@ -244,15 +263,27 @@
 
         @pl.when(pair % 3 != 0)
         def _():
-            beyond = 3 * (pair - 1)
-            one(beyond)
+            one(3 * (pair - 1))
             one(mirror)
-            far = 3 - beyond
+
+        started.cores = before
+
+    def relay_pairs(group, layer):
+        before, started.cores = started.cores, ()
+
+        @pl.when(pair % 3 != 0)
+        def _():
+            far = 3 - 3 * (pair - 1)
             ended(group.relay.at[layer], group.recv.at[2, layer])
             group.own[layer, far] = (
                 group.own[layer, far].astype(f32) + group.relay[layer].astype(f32)
             ).astype(bf16)
-            one(far)
+            send(
+                group.own.at[layer, far],
+                group.come.at[layer, pair],
+                group.recv.at[0, layer],
+                (section, far * 2 + core),
+            )
 
         started.cores = before
 
@@ -347,9 +378,11 @@
             load_matrix(kind, layer, 14 + layer)
     load(v.cotangent.at[section], v.cotangent_v, 14 + layers)
 
+    on_core(0, lambda: load(v.edge_features, v.lefts.at[pl.ds(0, sections)], 15 + layers))
+    to_mate(0, v.lefts.at[pl.ds(sections, sections)], v.lefts_recv, v.edge_features)
+
     loaded(v.nodes.at[0, row], 0)
     loaded(v.edge_in.at[0], 1)
-    to_mate(0, v.mate_left.at[0], v.mate_recv.at[0], v.edge_in.at[0])
 
     for place in range(3):
         loaded(v.index.at[place], 3 + place)
@@ -410,7 +443,7 @@
         if layer + 1 < layers:
             v.edge_in[layer + 1] = edge
             to_mate(
-                0, v.mate_left.at[layer + 1], v.mate_recv.at[layer + 1], v.edge_in.at[layer + 1]
+                0, v.pre_left.at[layer + 1], v.pre_recv.at[layer + 1], v.edge_in.at[layer + 1]
             )
         return node, dot(v.to_targets[...], edge).astype(bf16)
 
@@ -439,22 +472,26 @@
         v.node_lefts_own[layer, 0:node_dev] = node
         v.node_lefts_own[layer, node_dev : 2 * node_dev] = gathered
         v.node_lefts_own[layer, 2 * node_dev : 3 * node_dev] = hidden
-        to_plane(
-            node_lefts,
-            layer,
-            (
-                lambda s: v.node_lefts_own.at[layer, pl.ds(0, node_dev)],
-                lambda s: v.node_lefts_own.at[layer],
-            ),
-        )
+        to_plane(node_lefts, layer, (None, lambda s: v.node_lefts_own.at[layer]))
 
     for layer in range(layers):
         node, gathered = edge_forward(layer)
         node_forward(layer, node, gathered)
 
+    def hand_states(layer):
+        def act():
+            from_plane(node_lefts, layer, 3 * node_dev)
+            send(
+                v.node_lefts.at[layer, :, pl.ds(0, node_dev)],
+                v.states.at[layer],
+                v.states_recv.at[layer],
+                (section, row + 1 - 2 * core),
+            )
+
+        on_core(1, act)
+
     def node_products(layer, relay):
         def act():
-            from_plane(node_lefts, layer, 3 * node_dev)
             from_plane(node_rights, layer, 2 * node_dev + vector_rows)
             own = plane * node_dev
             state = v.node_lefts[layer, :, 0:node_dev].reshape(own, width)
@@ -470,41 +507,41 @@
             store_blocks(target, v.product, 0, two_rows)
             start = whole_tiles(two_rows)
             store_blocks(target, v.product.at[pl.ds(2 * width, width)], start, one_rows)
-            start += whole_tiles(one_rows)
-            store_vectors(target, jnp.sum(vectors.astype(f32), axis=0), start)
+            v.node_vectors[layer] = jnp.sum(vectors.astype(f32), axis=0)
             send_pairs(node_pairs, layer, relay)
 
         on_core(1, act)
 
     def edge_parts(layer):
-        def multiply(own_left, own_right):
-            left = jnp.concatenate([own_left[layer], v.mate_left[layer]], axis=0)
-            right = jnp.concatenate(
-                [own_right[layer, 0:edge_dev], v.mate_right[layer, 0:edge_dev]], axis=0
-            )
+        def multiply(lefts, rights):
+            left = jnp.concatenate(lefts, axis=0)
+            right = jnp.concatenate(rights, axis=0)
             for part in range(sections):
                 columns = slice(part * quarter, (part + 1) * quarter)
                 v.parts[layer, part, 0:width] = contract_rows(left, right[:, columns]).astype(bf16)
 
         def act_one():
-            drained(2 * edge_dev * width, v.mate_recv.at[layer])
-            multiply(v.edge_in, v.pre_own)
+            drained(2 * edge_dev * width, v.pre_recv.at[layer])
+            multiply([v.edge_in[layer], v.pre_left[layer]], [v.pre_own[layer], v.pre_right[layer]])
             send_parts(layer, width)
 
         def act_two():
             drained((2 * edge_dev + vector_rows) * width, v.mate_recv.at[layer])
-            multiply(v.edge_hidden, v.lift_own)
+            multiply(
+                [v.edge_hidden[layer], v.mate_left[layer]],
+                [v.lift_own[layer, 0:edge_dev], v.mate_right[layer, 0:edge_dev]],
+            )
             vectors = (
                 v.lift_own[layer, edge_dev : edge_dev + vector_rows].astype(f32)
                 + v.mate_right[layer, edge_dev : edge_dev + vector_rows].astype(f32)
             ).astype(bf16)
             for part in range(sections):
-                v.parts[layer, part, width : width + vector_rows] = vectors[
-                    :, part * quarter : (part + 1) * quarter
-                ]
+                columns = slice(part * quarter, (part + 1) * quarter)
+                v.parts[layer, part, width : width + vector_rows] = vectors[:, columns]
             send_parts(layer, width + vector_rows)
 
-        on_core(0, act_one)
+        if layer > 0:
+            on_core(0, act_one)
         on_core(1, act_two)
 
     def from_parts(layer, rows):
@@ -518,38 +555,50 @@
         return total
 
     def edge_products(layer, relay):
-        def act_one():
-            from_plane(node_lefts, layer, node_dev)
+        def act():
+            if layer == 0:
+                loaded(v.lefts.at[pl.ds(0, sections)], 15 + layers)
+                ended(v.lefts.at[pl.ds(sections, sections)], v.lefts_recv)
+                from_plane(rights, 0, edge_dev)
+                v.product[0:width] = contract_rows(
+                    v.lefts[...].reshape(plane * edge_dev, width),
+                    v.rights[0].reshape(plane * edge_dev, quarter),
+                )
+            ended(v.states.at[layer], v.states_recv.at[layer])
             from_plane(sum_rights, layer, 2 * node_dev)
             own = plane * node_dev
-            state = v.node_lefts[layer, :, 0:node_dev].reshape(own, width)
+            state = v.states[layer].reshape(own, width)
             for part in range(2):
                 start = part * node_dev
                 v.product[(1 + part) * width : (2 + part) * width] = contract_rows(
                     state, v.sum_rights[layer, :, start : start + node_dev].reshape(own, quarter)
                 )
-            from_parts(layer, width)
-            v.product[0:width] = add_parts(layer, 0, width)
+            if layer > 0:
+                from_parts(layer, width)
+                v.product[0:width] = add_parts(layer, 0, width)
             store_blocks(edge_pairs.own.at[layer], v.product, 0, three_rows)
             send_pairs(edge_pairs, layer, relay)
 
-        def act_two():
+        on_core(0, act)
+
+    def lift_products(layer, relay):
+        def act():
             from_parts(layer, width + vector_rows)
             v.product[0:width] = add_parts(layer, 0, width)
             target = lift_pairs.own.at[layer]
             store_blocks(target, v.product, 0, one_rows)
-            store_vectors(target, add_parts(layer, width, vector_rows), whole_tiles(one_rows))
+            vectors = add_parts(layer, width, vector_rows) + v.node_vectors[layer]
+            store_vectors(target, vectors, whole_tiles(one_rows))
             send_pairs(lift_pairs, layer, relay)
 
-        on_core(0, act_one)
-        on_core(1, act_two)
-
-    def add_node_products(layer, relay):
-        on_core(1, lambda: add_pairs(node_pairs, layer, relay))
-
-    def add_edge_products(layer, relay):
-        on_core(0, lambda: add_pairs(edge_pairs, layer, relay))
-        on_core(1, lambda: add_pairs(lift_pairs, layer, relay))
+        on_core(1, act)
+
+    def relay_products(group, giver, layer, relay):
+        if relay:
+            on_core(giver, lambda: relay_pairs(group, layer))
+
+    def add_products(group, giver, layer, relay):
+        on_core(giver, lambda: add_pairs(group, layer, relay))
 
     def node_backward(layer):
         grad_branch = v.grad_node[...]
@@ -571,7 +620,7 @@
         target = v.node_rights_own.at[layer]
         quarters(target, 0, grad_pre)
         quarters(target, node_dev, grad_lifted)
-        quarters(target, 2 * node_dev, column_sums(grad_pre, grad_lifted, grad_branch, normed))
+        quarters(target, 2 * node_dev, column_sums(grad_pre, grad_lifted, grad_branch, normed, 4))
         to_plane(node_rights, layer, (None, lambda s: v.node_rights_own.at[layer, s]))
 
     def edge_backward(layer):
@@ -583,15 +632,23 @@
         grad_hidden = contract_cols(grad_lifted, matrix(e_two, layer))
         grad_pre = (grad_hidden * v.edge_slope[layer]).astype(bf16)
         sums = dot(v.to_nodes[...], grad_pre).astype(bf16)
-        v.sums[layer] = sums.reshape(shards, node_dev, width)
-        send_sums(layer)
-        v.pre_own[layer] = grad_pre
+        for place in range(shards):
+            block = sums[place * node_dev : (place + 1) * node_dev]
+            v.sums[layer, place % 2, place // 2] = block
+        mate = (section, row + 1 - 2 * core)
+        send(v.sums.at[layer, 1 - core], v.mate_sums.at[layer], v.mate_sums_recv.at[layer], mate)
+        if layer == 0:
+            quarters(v.pre_rights_own, 0, grad_pre)
+            to_plane(rights, 0, (lambda s: v.pre_rights_own.at[s], None))
+        else:
+            v.pre_own[layer] = grad_pre
+            to_mate(0, v.pre_right.at[layer], v.pre_recv.at[layer], v.pre_own.at[layer])
         v.lift_own[layer, 0:edge_dev] = grad_lifted
         v.lift_own[layer, edge_dev : edge_dev + vector_rows] = column_sums(
-            grad_pre, grad_lifted, grad_branch, normed
-        )
-        to_mate(0, v.mate_right.at[layer], v.mate_recv.at[layer], v.pre_own.at[layer])
+            grad_pre, grad_lifted, grad_branch, normed, 0
+        )
         to_mate(1, v.mate_right.at[layer], v.mate_recv.at[layer], v.lift_own.at[layer])
+        send_sums(layer)
         grad_edge = grad_branch + contract_cols(grad_pre, matrix(e_one, layer, 0, 1))
         by_target = dot(v.to_targets[...], grad_pre).astype(bf16)
         v.grad_node[...] = v.grad_node[...] + contract_cols(
@@ -605,8 +662,8 @@
         return by_target
 
     def sender_backward(layer, by_target):
-        from_rows(v.sums_in, v.sums_recv, layer)
-        v.sums_in[layer, row] = v.sums[layer, row]
+        ended(v.sums_in.at[layer, pl.ds(0, pairs - 1)], v.sums_recv.at[layer])
+        v.sums_in[layer, pair] = v.both_sums[layer, pair]
         by_sender = jnp.sum(v.sums_in[layer].astype(f32), axis=0).astype(bf16)
         target = v.sum_rights_own.at[layer]
         quarters(target, 0, by_sender)
@@ -624,18 +681,37 @@
     loaded(v.cotangent_v, 14 + layers)
     v.grad_node[...] = v.cotangent_v[...].astype(f32)
     relay = pairs == 4
-    for layer in reversed(range(layers)):
+    for layer in reversed(range(1, layers)):
         node_backward(layer)
         by_target = edge_backward(layer)
         edge_parts(layer)
-        node_products(layer, False)
         sender_backward(layer, by_target)
-    edge_products(1, relay)
-    add_node_products(1, False)
+        hand_states(layer)
+        node_products(layer, relay)
+    node_backward(0)
+    by_target = edge_backward(0)
+    edge_parts(0)
+    hand_states(0)
+    for layer in reversed(range(1, layers)):
+        edge_products(layer, relay)
+        lift_products(layer, relay)
+        relay_products(node_pairs, 1, layer, relay)
+        relay_products(lift_pairs, 1, layer, relay)
+    node_products(0, relay)
+    sender_backward(0, by_target)
     edge_products(0, relay)
-    add_edge_products(1, relay)
-    add_node_products(0, False)
-    add_edge_products(0, relay)
+    for layer in reversed(range(layers)):
+        relay_products(edge_pairs, 0, layer, relay)
+    for layer in reversed(range(1, layers)):
+        add_products(node_pairs, 1, layer, relay)
+        add_products(lift_pairs, 1, layer, relay)
+    for layer in reversed(range(layers)):
+        add_products(edge_pairs, 0, layer, relay)
+    lift_products(0, relay)
+    relay_products(node_pairs, 1, 0, relay)
+    relay_products(lift_pairs, 1, 0, relay)
+    add_products(node_pairs, 1, 0, relay)
+    add_products(lift_pairs, 1, 0, relay)
 
     for layer in range(layers):
         from_givers(edge_pairs, layer, 0)
@@ -682,13 +758,10 @@
 
     holder = row // (quarter // one_rows)
     for layer in range(layers):
-        for kinds, full, start in (
-            (vector_kinds[:4], lift_full, whole_tiles(one_rows)),
-            (vector_kinds[4:], node_full, node_start + whole_tiles(one_rows)),
-        ):
-            vectors = take_columns(full[layer, holder, start : start + vector_rows].astype(f32))
-            for place, kind in enumerate(kinds):
-                grads[kind][layer : layer + 1] = vectors[place : place + 1]
+        start = whole_tiles(one_rows)
+        taken = take_columns(lift_full[layer, holder, start : start + vector_rows].astype(f32))
+        for place, kind in enumerate(vector_kinds):
+            grads[kind][layer : layer + 1] = taken[place : place + 1]
 
 
 def fused(sections, shards, node_features, edge_features, owner, local, receivers, cotangent, *weights):
@@ -727,14 +800,14 @@
     blocks = (
         whole_tiles(3 * width // shards),
         lift_block,
-        whole_tiles(2 * width // shards) + lift_block,
+        whole_tiles(2 * width // shards) + whole_tiles(width // shards),
     )
     fulls = [shape(layers, sections, block, quarter, kind=bf16) for block in blocks]
     starts = np.cumsum([0] + [weights[kind].shape[1] for kind in matrix_kinds])
     scratch = dict(
         done=pltpu.SemaphoreType.DMA,
         drain=vmem(1024 * (24 + shards // 2), lanes),
-        load_sem=sems(15 + layers),
+        load_sem=sems(16 + layers),
         index=vmem(3, 1, edge_dev, kind=jnp.int32),
         vectors=vmem(len(vector_kinds), layers, width),
         matrices=vmem(layers, int(starts[-1]), width),
@@ -757,16 +830,30 @@
         node_scale=vmem(layers, node_dev, 1, kind=f32),
         nodes=vmem(layers, shards, node_dev, width),
         nodes_recv=sems(layers),
-        sums=vmem(layers, shards, node_dev, width),
-        sums_in=vmem(layers, shards, node_dev, width),
+        sums=vmem(layers, 2, pairs, node_dev, width),
+        mate_sums=vmem(layers, pairs, node_dev, width),
+        mate_sums_recv=sems(layers),
+        both_sums=vmem(layers, pairs, node_dev, width),
+        sums_in=vmem(layers, pairs, node_dev, width),
         sums_recv=sems(layers),
         final_v=vmem(1, node_dev, width),
         grad_nodes_v=vmem(1, node_dev, width, kind=f32),
         grad_edges_v=vmem(1, edge_dev, width, kind=f32),
+        node_vectors=vmem(layers, vector_rows, quarter, kind=f32),
         mate_left=vmem(layers, edge_dev, width),
         mate_right=vmem(layers, edge_dev + vector_rows, width),
         mate_recv=sems(layers),
+        lefts=vmem(plane, edge_dev, width),
+        lefts_recv=pltpu.SemaphoreType.DMA,
+        pre_rights_own=vmem(sections, edge_dev, quarter),
+        rights=vmem(1, plane, edge_dev, quarter),
+        rights_recv=sems(1),
         pre_own=vmem(layers, edge_dev, width),
+        pre_left=vmem(layers, edge_dev, width),
+        pre_right=vmem(layers, edge_dev, width),
+        pre_recv=sems(layers),
+        states=vmem(layers, plane, node_dev, width),
+        states_recv=sems(layers),
         lift_own=vmem(layers, edge_dev + vector_rows, width),
         parts=vmem(layers, sections, width + vector_rows, quarter),
         parts_in=vmem(layers, sections, width + vector_rows, quarter),
@@ -817,17 +904,18 @@
         functools.partial(kernel, plan),
         out_shape=list(outputs.values()) + fulls,
         in_specs=[pl.BlockSpec(memory_space=pltpu.HBM)] * ins,
-        out_specs=[pl.BlockSpec(memory_space=pltpu.HBM)] * outs,
+        out_specs=[pl.BlockSpec(memory_space=pl.ANY)] * outs,
         scratch_shapes=list(scratch.values()) + pair_groups,
         compiler_params=pltpu.CompilerParams(
-            collective_id=0, has_side_effects=True, vmem_limit_bytes=60 << 20
+            collective_id=0, has_side_effects=True, vmem_limit_bytes=40 << 20
         ),
-    )(*inputs.values(), *weights)
+    )(*(pltpu.with_memory_space_constraint(x, pltpu.HBM) for x in (*inputs.values(), *weights)))
     return pl.pallas_call(
         functools.partial(write_kernel, shards),
         out_shape=list(outputs.values()) + weight_grads,
         in_specs=[pl.BlockSpec(memory_space=pltpu.VMEM)] * outs,
         out_specs=[pl.BlockSpec(memory_space=pltpu.VMEM)] * (len(outputs) + len(weight_grads)),
+        compiler_params=pltpu.CompilerParams(vmem_limit_bytes=16 << 20),
     )(*results)
 
 

time: 55.4 us -> 52.9 us (0.955)
  Pallas kernels: 54.5 us -> 52 us
    pallas_call x1, Pallas kernels: 2.7 us -> 1.43 us  [fused(): pl.pallas_call(functools.partial(write_kernel, shards), out_shape=list(ou...]
    pallas_call x1, Pallas kernels: 51.8 us -> 50.6 us  [fused(): pl.pallas_call(functools.partial(kernel, plan), out_shape=list(outputs.va...]
where the time goes in v5:
time: 52.9 us; the launch traced here: 52.7 us
  Pallas kernels  52 us (98%)
  between operations  0.66 us (1%)
    pallas_call x1, Pallas kernels, fused(): pl.pallas_call(functools.partial(kernel, plan), out_shape=list(outputs.va...  50.6 us
    pallas_call x1, Pallas kernels, fused(): pl.pallas_call(functools.partial(write_kernel, shards), out_shape=list(ou...  1.43 us

profile of v5, /device:TPU:0, one launch (start us, length us, event | category | flops | bytes accessed | tf_op | source)
XLA Modules:
  0.0 52.7 jit_solution(9201865154477921704)
XLA Ops:
  0.7 50.6 %shard_map.289 = (bf16[1,16,512]{2,1,0:T(8,128)(2,1)S(1)}, f32[1,16,512]{2,1,0:T(8,128)S(1)}, f32[1,128,512]{2,1,0:T(8,128)S(1)}, bf16[2,4,192,128]{3,2,1,0:T(8,...) custom-call(bf16[4,16,512]{2,1,0:T(8,128)(2,1)} %refs_0_.1, ...), custom_call_target="tpu_custom_call" | custom-call | tf_op jit(solution)/shard_map/pallas_call | solution.py:903
  51.3 1.4 %shard_map.290 = (bf16[1,16,512]{2,1,0:T(8,128)(2,1)}, f32[1,16,512]{2,1,0:T(8,128)}, f32[1,128,512]{2,1,0:T(8,128)}, f32[2,192,512]{2,1,0:T(8,128)}, f32[2,64]{...) custom-call(bf16[1,16,512]{2,1,0:T(8,128)(2,1)S(1)} %get-tuple-eleme, ...), custom_call_target="tpu_custom_call" | custom-call | tf_op jit(solution)/shard_map/pallas_call | solution.py:913

commit v6 on v5

--- a/solution.py
+++ b/solution.py
@@ -98,6 +98,7 @@
     node_lefts = SimpleNamespace(data=v.node_lefts, recv=v.node_lefts_recv)
     node_rights = SimpleNamespace(data=v.node_rights, recv=v.node_rights_recv)
     sum_rights = SimpleNamespace(data=v.sum_rights, recv=v.sum_rights_recv)
+    target_rights = SimpleNamespace(data=v.target_rights, recv=v.target_rights_recv)
 
     def drained(count, sem):
         ended(v.drain.at[pl.ds(0, count // lanes)], sem)
@@ -191,6 +192,22 @@
         else:
             each(pairs - 1, lambda i: visit((pair + 1 + i) % pairs))
 
+    def send_sums_alone():
+        def one(peer, other):
+            send(
+                v.sums.at[0, other, peer],
+                v.sums_all.at[row],
+                v.sums_recv.at[0],
+                (section, peer * 2 + other),
+            )
+
+        def both(peer):
+            one(peer, core)
+            one(peer, 1 - core)
+
+        peer_pairs(both)
+        one(pair, 1 - core)
+
     def from_rows(data, sem, layer):
         ended(data.at[layer, pl.ds(0, shards - 1)], sem.at[layer])
 
@@ -233,7 +250,7 @@
                 (target, row),
             )
 
-    def send_pairs(group, layer, relay):
+    def send_pairs(group, layer, relay, outer=True, inner=True):
         def one(peer):
             send(
                 group.own.at[layer, peer],
@@ -250,21 +267,25 @@
         @pl.when(pair % 3 == 0)
         def _():
             near = (pair + 3) // 3
-            send(
-                group.own.at[layer, mirror],
-                group.relay.at[layer],
-                group.recv.at[2, layer],
-                (section, near * 2 + core),
-            )
-            one(near)
-            one(3 - near)
+            if outer:
+                send(
+                    group.own.at[layer, mirror],
+                    group.relay.at[layer],
+                    group.recv.at[2, layer],
+                    (section, near * 2 + core),
+                )
+            if inner:
+                one(near)
+                one(3 - near)
 
         before, started.cores = started.cores, ()
 
         @pl.when(pair % 3 != 0)
         def _():
-            one(3 * (pair - 1))
-            one(mirror)
+            if outer:
+                one(3 * (pair - 1))
+            if inner:
+                one(mirror)
 
         started.cores = before
 
@@ -323,9 +344,9 @@
         for other in range(2):
             on_core(other, functools.partial(wait, other))
 
-    def store_blocks(target, product, offset, rows):
+    def store_blocks(target, product, offset, rows, owners=range(shards)):
         padded = whole_tiles(rows)
-        for owner in range(shards):
+        for owner in owners:
             block = product[owner * rows : (owner + 1) * rows]
             if padded != rows:
                 block = jnp.concatenate([block, jnp.zeros((padded - rows, quarter), f32)], axis=0)
@@ -421,6 +442,9 @@
             + dot(received, matrix(e_one, layer, 2, 1))
             + vector(e_bias_one, layer)
         )
+        if layer == 0:
+            loaded(v.matrices.at[0, pl.ds(3 * width, v.matrices.shape[1] - 3 * width)], 14)
+        v.node_work[...] = dot(node, matrix(n_one, layer, 0, 1)) + vector(n_bias_one, layer)
         from_rows(v.nodes, v.nodes_recv, layer)
         sent = dot(v.from_nodes[...], v.nodes[layer].reshape(nodes_total, width)).astype(bf16)
         hidden, slope = activate(
@@ -429,8 +453,6 @@
         v.edge_hidden[layer] = hidden
         v.edge_slope[layer] = slope
         to_mate(1, v.mate_left.at[layer], v.mate_recv.at[layer], v.edge_hidden.at[layer])
-        if layer == 0:
-            loaded(v.matrices.at[0, pl.ds(3 * width, v.matrices.shape[1] - 3 * width)], 14)
         normed, scale = layer_norm(
             dot(hidden, matrix(e_two, layer)) + vector(e_bias_two, layer)
         )
@@ -449,9 +471,7 @@
 
     def node_forward(layer, node, gathered):
         hidden, slope = activate(
-            dot(node, matrix(n_one, layer, 0, 1))
-            + dot(gathered, matrix(n_one, layer, 1, 1))
-            + vector(n_bias_one, layer)
+            v.node_work[...] + dot(gathered, matrix(n_one, layer, 1, 1))
         )
         v.node_slope[layer] = slope
         normed, scale = layer_norm(
@@ -554,30 +574,45 @@
             total = total + v.parts_in[layer, other, start : start + rows].astype(f32)
         return total
 
+    outer_owners = [0, 1, shards - 2, shards - 1]
+    inner_owners = [owner for owner in range(shards) if owner not in outer_owners]
+
+    def state_products(layer, group, place):
+        own = plane * node_dev
+        from_plane(group, layer, node_dev)
+        v.edge_product[layer, place * width : (place + 1) * width] = contract_rows(
+            v.states[layer].reshape(own, width), group.data[layer].reshape(own, quarter)
+        )
+
     def edge_products(layer, relay):
         def act():
             if layer == 0:
                 loaded(v.lefts.at[pl.ds(0, sections)], 15 + layers)
                 ended(v.lefts.at[pl.ds(sections, sections)], v.lefts_recv)
                 from_plane(rights, 0, edge_dev)
-                v.product[0:width] = contract_rows(
+                v.edge_product[0, 0:width] = contract_rows(
                     v.lefts[...].reshape(plane * edge_dev, width),
                     v.rights[0].reshape(plane * edge_dev, quarter),
                 )
+            else:
+                from_parts(layer, width)
+                v.edge_product[layer, 0:width] = add_parts(layer, 0, width)
             ended(v.states.at[layer], v.states_recv.at[layer])
-            from_plane(sum_rights, layer, 2 * node_dev)
-            own = plane * node_dev
-            state = v.states[layer].reshape(own, width)
-            for part in range(2):
-                start = part * node_dev
-                v.product[(1 + part) * width : (2 + part) * width] = contract_rows(
-                    state, v.sum_rights[layer, :, start : start + node_dev].reshape(own, quarter)
-                )
-            if layer > 0:
-                from_parts(layer, width)
-                v.product[0:width] = add_parts(layer, 0, width)
-            store_blocks(edge_pairs.own.at[layer], v.product, 0, three_rows)
-            send_pairs(edge_pairs, layer, relay)
+            state_products(layer, target_rights, 2)
+            if relay:
+                blocks, product = edge_pairs.own.at[layer], v.edge_product.at[layer]
+                store_blocks(blocks, product, 0, three_rows, outer_owners)
+                send_pairs(edge_pairs, layer, True, inner=False)
+
+        on_core(0, act)
+
+    def sender_products(layer, relay):
+        def act():
+            state_products(layer, sum_rights, 1)
+            owners = inner_owners if relay else range(shards)
+            blocks, product = edge_pairs.own.at[layer], v.edge_product.at[layer]
+            store_blocks(blocks, product, 0, three_rows, owners)
+            send_pairs(edge_pairs, layer, relay, outer=False)
 
         on_core(0, act)
 
@@ -615,15 +650,18 @@
         if layer + 1 < layers:
             grad_edge = grad_edge + v.grad_edge[...]
         v.grad_edge[...] = grad_edge.astype(bf16).astype(f32)
-        grad_node = grad_branch + contract_cols(grad_pre, matrix(n_one, layer, 0, 1))
-        v.grad_node[...] = grad_node.astype(bf16).astype(f32)
         target = v.node_rights_own.at[layer]
         quarters(target, 0, grad_pre)
         quarters(target, node_dev, grad_lifted)
         quarters(target, 2 * node_dev, column_sums(grad_pre, grad_lifted, grad_branch, normed, 4))
         to_plane(node_rights, layer, (None, lambda s: v.node_rights_own.at[layer, s]))
-
-    def edge_backward(layer):
+        return grad_branch, grad_pre
+
+    def node_backward_rest(layer, grad_branch, grad_pre):
+        grad_node = grad_branch + contract_cols(grad_pre, matrix(n_one, layer, 0, 1))
+        v.grad_node[...] = grad_node.astype(bf16).astype(f32)
+
+    def edge_backward(layer, rest):
         grad_branch = v.grad_edge[...]
         normed = v.edge_normed[layer]
         grad_lifted = branch_back(
@@ -636,7 +674,12 @@
             block = sums[place * node_dev : (place + 1) * node_dev]
             v.sums[layer, place % 2, place // 2] = block
         mate = (section, row + 1 - 2 * core)
-        send(v.sums.at[layer, 1 - core], v.mate_sums.at[layer], v.mate_sums_recv.at[layer], mate)
+        if layer == 0:
+            send_sums_alone()
+        else:
+            send(
+                v.sums.at[layer, 1 - core], v.mate_sums.at[layer], v.mate_sums_recv.at[layer], mate
+            )
         if layer == 0:
             quarters(v.pre_rights_own, 0, grad_pre)
             to_plane(rights, 0, (lambda s: v.pre_rights_own.at[s], None))
@@ -648,9 +691,13 @@
             grad_pre, grad_lifted, grad_branch, normed, 0
         )
         to_mate(1, v.mate_right.at[layer], v.mate_recv.at[layer], v.lift_own.at[layer])
-        send_sums(layer)
+        node_backward_rest(layer, *rest)
+        if layer > 0:
+            send_sums(layer)
         grad_edge = grad_branch + contract_cols(grad_pre, matrix(e_one, layer, 0, 1))
         by_target = dot(v.to_targets[...], grad_pre).astype(bf16)
+        quarters(v.target_rights_own.at[layer], 0, by_target)
+        to_plane(target_rights, layer, (lambda s: v.target_rights_own.at[layer, s], None))
         v.grad_node[...] = v.grad_node[...] + contract_cols(
             by_target, matrix(e_one, layer, 2, 1)
         )
@@ -659,15 +706,19 @@
         else:
             v.grad_edges_v[0] = grad_edge
             write(v.grad_edges_v, v.grad_edges)
-        return by_target
-
-    def sender_backward(layer, by_target):
-        ended(v.sums_in.at[layer, pl.ds(0, pairs - 1)], v.sums_recv.at[layer])
-        v.sums_in[layer, pair] = v.both_sums[layer, pair]
-        by_sender = jnp.sum(v.sums_in[layer].astype(f32), axis=0).astype(bf16)
+
+    def sender_backward(layer):
+        if layer == 0:
+            ended(v.sums_all.at[pl.ds(0, shards - 1)], v.sums_recv.at[0])
+            v.sums_all[row] = v.sums[0, core, pair]
+            parts = v.sums_all[...]
+        else:
+            ended(v.sums_in.at[layer, pl.ds(0, pairs - 1)], v.sums_recv.at[layer])
+            v.sums_in[layer, pair] = v.both_sums[layer, pair]
+            parts = v.sums_in[layer]
+        by_sender = jnp.sum(parts.astype(f32), axis=0).astype(bf16)
         target = v.sum_rights_own.at[layer]
         quarters(target, 0, by_sender)
-        quarters(target, node_dev, by_target)
         to_plane(sum_rights, layer, (lambda s: v.sum_rights_own.at[layer, s], None))
         grad_node = v.grad_node[...] + contract_cols(
             by_sender, matrix(e_one, layer, 1, 1)
@@ -681,37 +732,35 @@
     loaded(v.cotangent_v, 14 + layers)
     v.grad_node[...] = v.cotangent_v[...].astype(f32)
     relay = pairs == 4
-    for layer in reversed(range(1, layers)):
-        node_backward(layer)
-        by_target = edge_backward(layer)
+    later = list(reversed(range(1, layers)))
+    for layer in later:
+        edge_backward(layer, node_backward(layer))
         edge_parts(layer)
-        sender_backward(layer, by_target)
+        sender_backward(layer)
         hand_states(layer)
         node_products(layer, relay)
-    node_backward(0)
-    by_target = edge_backward(0)
+    edge_backward(0, node_backward(0))
     edge_parts(0)
     hand_states(0)
-    for layer in reversed(range(1, layers)):
+    for layer in later + [0]:
         edge_products(layer, relay)
+    for layer in later:
+        sender_products(layer, relay)
         lift_products(layer, relay)
         relay_products(node_pairs, 1, layer, relay)
         relay_products(lift_pairs, 1, layer, relay)
     node_products(0, relay)
-    sender_backward(0, by_target)
-    edge_products(0, relay)
-    for layer in reversed(range(layers)):
+    sender_backward(0)
+    for layer in later + [0]:
         relay_products(edge_pairs, 0, layer, relay)
-    for layer in reversed(range(1, layers)):
-        add_products(node_pairs, 1, layer, relay)
-        add_products(lift_pairs, 1, layer, relay)
-    for layer in reversed(range(layers)):
-        add_products(edge_pairs, 0, layer, relay)
+    sender_products(0, relay)
     lift_products(0, relay)
     relay_products(node_pairs, 1, 0, relay)
     relay_products(lift_pairs, 1, 0, relay)
-    add_products(node_pairs, 1, 0, relay)
-    add_products(lift_pairs, 1, 0, relay)
+    for layer in later + [0]:
+        add_products(node_pairs, 1, layer, relay)
+        add_products(lift_pairs, 1, layer, relay)
+        add_products(edge_pairs, 0, layer, relay)
 
     for layer in range(layers):
         from_givers(edge_pairs, layer, 0)
@@ -817,6 +866,7 @@
         from_targets=vmem(edge_dev, node_dev),
         to_targets=vmem(node_dev, edge_dev),
         work=vmem(edge_dev, width, kind=f32),
+        node_work=vmem(node_dev, width, kind=f32),
         grad_node=vmem(node_dev, width, kind=f32),
         grad_edge=vmem(edge_dev, width, kind=f32),
         product=vmem(3 * width, quarter, kind=f32),
@@ -835,6 +885,7 @@
         mate_sums_recv=sems(layers),
         both_sums=vmem(layers, pairs, node_dev, width),
         sums_in=vmem(layers, pairs, node_dev, width),
+        sums_all=vmem(shards, node_dev, width),
         sums_recv=sems(layers),
         final_v=vmem(1, node_dev, width),
         grad_nodes_v=vmem(1, node_dev, width, kind=f32),
@@ -864,8 +915,12 @@
         node_rights_own=vmem(layers, sections, 2 * node_dev + vector_rows, quarter),
         node_rights=vmem(layers, plane, 2 * node_dev + vector_rows, quarter),
         node_rights_recv=sems(layers),
-        sum_rights_own=vmem(layers, sections, 2 * node_dev, quarter),
-        sum_rights=vmem(layers, plane, 2 * node_dev, quarter),
+        edge_product=vmem(layers, 3 * width, quarter, kind=f32),
+        target_rights_own=vmem(layers, sections, node_dev, quarter),
+        target_rights=vmem(layers, plane, node_dev, quarter),
+        target_rights_recv=sems(layers),
+        sum_rights_own=vmem(layers, sections, node_dev, quarter),
+        sum_rights=vmem(layers, plane, node_dev, quarter),
         sum_rights_recv=sems(layers),
     )
     pair_groups = []

time: 52.9 us -> 52.2 us (0.987); the launches traced: 52.7 us -> 51.4 us
  Pallas kernels: 52 us -> 50.7 us
    pallas_call x1, Pallas kernels: 50.6 us -> 49.3 us  [fused(): pl.pallas_call(functools.partial(kernel, plan), out_shape=list(outputs.va...]
where the time goes in v6:
time: 52.2 us; the launch traced here: 51.4 us
  Pallas kernels  50.7 us (97%)
  between operations  0.66 us (1%)
    pallas_call x1, Pallas kernels, fused(): pl.pallas_call(functools.partial(kernel, plan), out_shape=list(outputs.va...  49.3 us
    pallas_call x1, Pallas kernels, fused(): pl.pallas_call(functools.partial(write_kernel, shards), out_shape=list(ou...  1.43 us

profile of v6, /device:TPU:0, one launch (start us, length us, event | category | flops | bytes accessed | tf_op | source)
XLA Modules:
  0.0 51.4 jit_solution(16699630010094667844)
XLA Ops:
  0.7 49.3 %shard_map.289 = (bf16[1,16,512]{2,1,0:T(8,128)(2,1)S(1)}, f32[1,16,512]{2,1,0:T(8,128)S(1)}, f32[1,128,512]{2,1,0:T(8,128)S(1)}, bf16[2,4,192,128]{3,2,1,0:T(8,...) custom-call(bf16[4,16,512]{2,1,0:T(8,128)(2,1)} %refs_0_.1, ...), custom_call_target="tpu_custom_call" | custom-call | tf_op jit(solution)/shard_map/pallas_call | solution.py:958
  49.9 1.4 %shard_map.290 = (bf16[1,16,512]{2,1,0:T(8,128)(2,1)}, f32[1,16,512]{2,1,0:T(8,128)}, f32[1,128,512]{2,1,0:T(8,128)}, f32[2,192,512]{2,1,0:T(8,128)}, f32[2,64]{...) custom-call(bf16[1,16,512]{2,1,0:T(8,128)(2,1)S(1)} %get-tuple-eleme, ...), custom_call_target="tpu_custom_call" | custom-call | tf_op jit(solution)/shard_map/pallas_call | solution.py:968

commit v7 on v6

--- a/solution.py
+++ b/solution.py
@@ -389,24 +389,23 @@
     load(v.edge_features.at[section], v.edge_in.at[0], 1)
     load_matrix(e_one, 0, 2)
     for place, source in enumerate((v.owner, v.local, v.receivers)):
-        load(source.at[section], v.index.at[place], 3 + place)
+        load(source.at[section], v.index.at[place], 3)
     for place, kind in enumerate(vector_kinds):
-        load(weights[kind], v.vectors.at[place], 6 + place)
+        load(weights[kind], v.vectors.at[place], 4)
     for kind in (e_two, n_one, n_two):
-        load_matrix(kind, 0, 14)
+        load_matrix(kind, 0, 5)
     for layer in range(1, layers):
         for kind in matrix_kinds:
-            load_matrix(kind, layer, 14 + layer)
-    load(v.cotangent.at[section], v.cotangent_v, 14 + layers)
-
-    on_core(0, lambda: load(v.edge_features, v.lefts.at[pl.ds(0, sections)], 15 + layers))
+            load_matrix(kind, layer, 5 + layer)
+    load(v.cotangent.at[section], v.cotangent_v, 5 + layers)
+
+    on_core(0, lambda: load(v.edge_features, v.lefts.at[pl.ds(0, sections)], 6 + layers))
     to_mate(0, v.lefts.at[pl.ds(sections, sections)], v.lefts_recv, v.edge_features)
 
     loaded(v.nodes.at[0, row], 0)
     loaded(v.edge_in.at[0], 1)
 
-    for place in range(3):
-        loaded(v.index.at[place], 3 + place)
+    loaded(v.index, 3)
     sender_row, target_row = v.index[0] * node_dev + v.index[1], v.index[2]
     eye = lax.broadcasted_iota(jnp.int32, (edge_dev, edge_dev), 0) == lax.broadcasted_iota(
         jnp.int32, (edge_dev, edge_dev), 1
@@ -426,8 +425,7 @@
     v.to_nodes[...] = one_hot(sender_row, nodes_total, 0)
     v.from_targets[...] = one_hot(to_column(target_row), node_dev, 1)
     v.to_targets[...] = one_hot(target_row, node_dev, 0)
-    for place in range(len(vector_kinds)):
-        loaded(v.vectors.at[place], 6 + place)
+    loaded(v.vectors, 4)
 
     def edge_forward(layer):
         node = v.nodes[layer, row]
@@ -435,7 +433,7 @@
         if layer == 0:
             loaded(v.matrices.at[0, pl.ds(0, 3 * width)], 2)
         else:
-            loaded(v.matrices.at[layer], 14 + layer)
+            loaded(v.matrices.at[layer], 5 + layer)
         received = dot(v.from_targets[...], node).astype(bf16)
         v.work[...] = (
             dot(edge, matrix(e_one, layer, 0, 1))
@@ -443,7 +441,7 @@
             + vector(e_bias_one, layer)
         )
         if layer == 0:
-            loaded(v.matrices.at[0, pl.ds(3 * width, v.matrices.shape[1] - 3 * width)], 14)
+            loaded(v.matrices.at[0, pl.ds(3 * width, v.matrices.shape[1] - 3 * width)], 5)
         v.node_work[...] = dot(node, matrix(n_one, layer, 0, 1)) + vector(n_bias_one, layer)
         from_rows(v.nodes, v.nodes_recv, layer)
         sent = dot(v.from_nodes[...], v.nodes[layer].reshape(nodes_total, width)).astype(bf16)
@@ -587,7 +585,7 @@
     def edge_products(layer, relay):
         def act():
             if layer == 0:
-                loaded(v.lefts.at[pl.ds(0, sections)], 15 + layers)
+                loaded(v.lefts.at[pl.ds(0, sections)], 6 + layers)
                 ended(v.lefts.at[pl.ds(sections, sections)], v.lefts_recv)
                 from_plane(rights, 0, edge_dev)
                 v.edge_product[0, 0:width] = contract_rows(
@@ -729,7 +727,7 @@
             v.grad_nodes_v[0] = grad_node
             write(v.grad_nodes_v, v.grad_nodes)
 
-    loaded(v.cotangent_v, 14 + layers)
+    loaded(v.cotangent_v, 5 + layers)
     v.grad_node[...] = v.cotangent_v[...].astype(f32)
     relay = pairs == 4
     later = list(reversed(range(1, layers)))
@@ -745,12 +743,14 @@
     for layer in later + [0]:
         edge_products(layer, relay)
     for layer in later:
-        sender_products(layer, relay)
         lift_products(layer, relay)
         relay_products(node_pairs, 1, layer, relay)
+    node_products(0, relay)
+    for layer in later:
         relay_products(lift_pairs, 1, layer, relay)
-    node_products(0, relay)
     sender_backward(0)
+    for layer in later:
+        sender_products(layer, relay)
     for layer in later + [0]:
         relay_products(edge_pairs, 0, layer, relay)
     sender_products(0, relay)
@@ -856,7 +856,7 @@
     scratch = dict(
         done=pltpu.SemaphoreType.DMA,
         drain=vmem(1024 * (24 + shards // 2), lanes),
-        load_sem=sems(16 + layers),
+        load_sem=sems(7 + layers),
         index=vmem(3, 1, edge_dev, kind=jnp.int32),
         vectors=vmem(len(vector_kinds), layers, width),
         matrices=vmem(layers, int(starts[-1]), width),

time: 52.2 us -> 52.1 us (level)
  no operation moved by 1% of the time
where the time goes in v7:
time: 52.1 us; the launch traced here: 51.3 us
  Pallas kernels  50.6 us (97%)
  between operations  0.66 us (1%)
    pallas_call x1, Pallas kernels, fused(): pl.pallas_call(functools.partial(kernel, plan), out_shape=list(outputs.va...  49.2 us
    pallas_call x1, Pallas kernels, fused(): pl.pallas_call(functools.partial(write_kernel, shards), out_shape=list(ou...  1.43 us

profile of v7, /device:TPU:0, one launch (start us, length us, event | category | flops | bytes accessed | tf_op | source)
XLA Modules:
  0.0 51.3 jit_solution(1631181491753718051)
XLA Ops:
  0.7 49.2 %shard_map.289 = (bf16[1,16,512]{2,1,0:T(8,128)(2,1)S(1)}, f32[1,16,512]{2,1,0:T(8,128)S(1)}, f32[1,128,512]{2,1,0:T(8,128)S(1)}, bf16[2,4,192,128]{3,2,1,0:T(8,...) custom-call(bf16[4,16,512]{2,1,0:T(8,128)(2,1)} %refs_0_.1, ...), custom_call_target="tpu_custom_call" | custom-call | tf_op jit(solution)/shard_map/pallas_call | solution.py:958
  49.8 1.4 %shard_map.290 = (bf16[1,16,512]{2,1,0:T(8,128)(2,1)}, f32[1,16,512]{2,1,0:T(8,128)}, f32[1,128,512]{2,1,0:T(8,128)}, f32[2,192,512]{2,1,0:T(8,128)}, f32[2,64]{...) custom-call(bf16[1,16,512]{2,1,0:T(8,128)(2,1)S(1)} %get-tuple-eleme, ...), custom_call_target="tpu_custom_call" | custom-call | tf_op jit(solution)/shard_map/pallas_call | solution.py:968
